TPU v7x, 128 devices: a whole 4x4x4 slice. The times are simulated.
128 devices in a mesh: dp: 32 (over y, z, core), mp: 4 (over x).
Axes of the slice: x: 4, y: 4, z: 4, core: 2. Of those that a mesh axis runs over, the one named last changes fastest.
Arguments:
- candidates: bfloat16 [1024, 128, 1024], P('dp', None, 'mp'), may hold values from -24 to 24
- live_counts: int32 [1024], P('dp'), may hold values from 1 to 128
- request_user: int32 [1024], P('dp'), may hold values from 0 to 1023, as said below
- score_slot: int32 [1024], replicated, may hold values from 0 to 1023, as said below
- history_cache: bfloat16 [1024, 256, 2048], P('dp', None, 'mp'), may hold values from -6 to 6
- history_length: int32 [1024], P('dp'), may hold values from 1 to 256, as said below
- input_weight: bfloat16 [1024, 4096], P(None, 'mp'), may hold values from -0.1875 to 0.1875
- time_bias: float32 [8, 16], P('mp'), may hold values from -4 to 4
- output_weight: bfloat16 [1024, 1024], P('mp'), may hold values from -0.1875 to 0.1875
Outputs:
- updated: bfloat16 [1024, 128, 1024], P('dp', None, 'mp')
Inputs may be any that keep to these rules, and one draw needn't show every extreme that they name: `request_user`: A permutation: each user has exactly one request. `score_slot`: A permutation. The scoring rank of user u is score_slot[u] // 32, so every rank scores exactly 32 users. At most 1 of the users of one dp index (users d * 32 to d * 32 + 31), and at most 1 of the requests held on one dp index, have the same scoring rank; both bounds are reached in every draw. `history_length`: some user has exactly 256 events.
All inputs are finite; a program needn't handle non-finite values.
Results may differ from a plain program's by a relative error of at most 0.0039.
Values may be sent and summed in bfloat16 or wider, within the bound.
No kernel may reach another device: no remote copies, remote signals or barrier semaphores. Data moves between devices by JAX's collectives and lax.ppermute only.
A program may use at most 128 MiB of HBM per device.

v0:
```python
import math

import jax
import jax.numpy as jnp
from jax import lax
from jax.sharding import PartitionSpec as P

HD = 128


EPSILON = 1e-05


def slot_plan(targets, pair_cap, dp_size):
    item_total = targets.shape[0]
    item_index = jnp.arange(item_total, dtype=jnp.int32)
    same_dest = targets[:, None] == targets[None, :]
    before = item_index[None, :] < item_index[:, None]
    earlier = jnp.sum((same_dest & before).astype(jnp.int32), axis=1)
    placed = targets * pair_cap + earlier
    slot_index = jnp.arange(dp_size * pair_cap, dtype=jnp.int32)
    matches = placed[None, :] == slot_index[:, None]
    source = jnp.sum(jnp.where(matches, item_index[None, :], 0), axis=1)
    filled = jnp.any(matches, axis=1)
    return (placed, source, filled)


def bucket_of(distance, bucket_total):
    bucket = jnp.zeros(distance.shape, jnp.int32)
    for exponent in range(bucket_total - 1):
        bucket = bucket + (distance >= 2**exponent).astype(jnp.int32)
    return bucket


def rounded(values):
    return lax.optimization_barrier(values.astype(jnp.bfloat16)).astype(jnp.float32)


def project(full_rows, input_weight):
    request_total, cand_slots, feat_total = full_rows.shape
    widened = full_rows.astype(jnp.float32)
    row_mean = jnp.mean(widened, axis=-1, keepdims=True)
    row_var = jnp.mean(jnp.square(widened - row_mean), axis=-1, keepdims=True)
    normed = ((widened - row_mean) * lax.rsqrt(row_var + EPSILON)).astype(jnp.bfloat16)
    linear = jnp.dot(
        normed.reshape(request_total * cand_slots, feat_total),
        input_weight,
        preferred_element_type=jnp.float32,
    )
    head_count = input_weight.shape[1] // (4 * HD)
    return (
        jax.nn.silu(linear)
        .astype(jnp.bfloat16)
        .reshape(request_total, cand_slots, head_count, 4, HD)
    )


def attend(queries, caches, lengths, time_bias):
    batch_total, events = (caches.shape[0], caches.shape[1])
    head_count = queries.shape[2]
    caches = caches.reshape(batch_total, events, head_count, 2, HD)
    positions = jnp.arange(events, dtype=jnp.int32)
    distance = lengths[:, None] - positions[None, :]
    bucket_total = time_bias.shape[1]
    one_hot = (
        bucket_of(distance, bucket_total)[:, :, None] == jnp.arange(bucket_total, dtype=jnp.int32)
    ).astype(jnp.float32)
    row_bias = jnp.einsum("ntb,hb->nht", one_hot, time_bias, precision=lax.Precision.HIGHEST)
    scores = jnp.einsum(
        "nchd,nthd->nhct", queries, caches[:, :, :, 0], preferred_element_type=jnp.float32
    )
    scores = scores * (1.0 / math.sqrt(HD)) + row_bias[:, :, None, :]
    is_live = (positions[None, :] < lengths[:, None])[:, None, None, :]
    divisor = (lengths + 1).astype(jnp.float32)[:, None, None, None]
    weights = jnp.where(is_live, jax.nn.silu(scores) / divisor, 0.0).astype(jnp.bfloat16)
    return jnp.einsum(
        "nhct,nthd->nchd", weights, caches[:, :, :, 1], preferred_element_type=jnp.float32
    )


def per_device(
    candidates,
    live_counts,
    request_user,
    score_slot,
    history_cache,
    history_length,
    input_weight,
    time_bias,
    output_weight,
):
    dp_size = lax.axis_size("dp")
    dp_rank = lax.axis_index("dp")
    local_users, cand_slots, feat_part = candidates.shape
    pair_cap = (local_users + dp_size - 1) // dp_size
    slot_total = dp_size * pair_cap
    events = history_cache.shape[1]
    kv_width = history_cache.shape[2]
    slot_range = jnp.arange(slot_total, dtype=jnp.int32)
    score_rank = jnp.take(score_slot, request_user) // local_users
    placed, source, filled = slot_plan(score_rank, pair_cap, dp_size)
    sent_users = jnp.where(filled, jnp.take(request_user, source), -1).reshape(dp_size, pair_cap)
    sent_counts = jnp.take(live_counts, source).reshape(dp_size, pair_cap)
    sent_rows = jnp.take(candidates, source, axis=0).reshape(
        dp_size, pair_cap, cand_slots, feat_part
    )
    got_rows, got_users, got_counts = (
        lax.all_to_all(sent_rows, "dp", split_axis=0, concat_axis=0, tiled=True),
        lax.all_to_all(sent_users, "dp", split_axis=0, concat_axis=0, tiled=True),
        lax.all_to_all(sent_counts, "dp", split_axis=0, concat_axis=0, tiled=True),
    )
    got_users = got_users.reshape(slot_total)
    usable = got_users >= 0
    position = jnp.where(
        usable, jnp.take(score_slot, jnp.maximum(got_users, 0)) - dp_rank * local_users, -1
    )
    out_rank = jnp.arange(local_users, dtype=jnp.int32)
    chosen = jnp.sum(
        jnp.where(position[None, :] == out_rank[:, None], slot_range[None, :], 0), axis=1
    )
    cand_rows = jnp.take(got_rows.reshape(slot_total, cand_slots, feat_part), chosen, axis=0)
    cand_users = jnp.take(got_users, chosen)
    cand_live = jnp.take(got_counts.reshape(slot_total), chosen)
    full_rows = lax.all_gather(cand_rows, "mp", axis=2, tiled=True)
    projected = project(full_rows, input_weight)
    head_count = projected.shape[2]
    query_width = head_count * HD
    gate_part = projected[:, :, :, 0]
    values = projected[:, :, :, 1]
    queries = projected[:, :, :, 2]
    key_part = projected[:, :, :, 3]
    own_targets = (
        lax.dynamic_slice_in_dim(score_slot, dp_rank * local_users, local_users) // local_users
    )
    hist_source, hist_filled = slot_plan(own_targets, pair_cap, dp_size)[1:]
    blocks = jnp.take(history_cache, hist_source, axis=0).reshape(
        dp_size, pair_cap, events, kv_width
    )
    block_users = jnp.where(hist_filled, dp_rank * local_users + hist_source, -1).reshape(
        dp_size, pair_cap
    )
    block_lengths = jnp.take(history_length, hist_source).reshape(dp_size, pair_cap)
    got_blocks, arrived_users, arrived_lengths = (
        lax.all_to_all(blocks, "dp", split_axis=0, concat_axis=0, tiled=True),
        lax.all_to_all(block_users, "dp", split_axis=0, concat_axis=0, tiled=True),
        lax.all_to_all(block_lengths, "dp", split_axis=0, concat_axis=0, tiled=True),
    )
    arrived_users = arrived_users.reshape(slot_total)
    located = jnp.sum(
        jnp.where(arrived_users[None, :] == cand_users[:, None], slot_range[None, :], 0), axis=1
    )
    lengths = jnp.take(arrived_lengths.reshape(slot_total), located)
    history = attend(
        queries,
        jnp.take(got_blocks.reshape(slot_total, events, kv_width), located, axis=0),
        lengths,
        time_bias,
    )
    divisor = (lengths + 1).astype(jnp.float32)[:, None, None]
    self_score = jnp.sum(queries.astype(jnp.float32) * key_part.astype(jnp.float32), axis=-1) * (
        1.0 / math.sqrt(HD)
    )
    self_score = self_score + time_bias[:, 0][None, None, :]
    self_weight = rounded(jax.nn.silu(self_score) / divisor)
    combined = history + self_weight[..., None] * values.astype(jnp.float32)
    head_mean = jnp.mean(combined, axis=-1, keepdims=True)
    head_var = jnp.mean(jnp.square(combined - head_mean), axis=-1, keepdims=True)
    gated_rows = (
        (combined - head_mean) * lax.rsqrt(head_var + EPSILON) * gate_part.astype(jnp.float32)
    ).astype(jnp.bfloat16)
    gated_rows = gated_rows.reshape(local_users * cand_slots, query_width)
    partial_value = jnp.dot(gated_rows, output_weight, preferred_element_type=jnp.float32).reshape(
        local_users, cand_slots, -1
    )
    summed = lax.psum_scatter(partial_value, "mp", scatter_dimension=2, tiled=True)
    result = summed + cand_rows.astype(jnp.float32)
    alive_mask = jnp.arange(cand_slots, dtype=jnp.int32)[None, :] < cand_live[:, None]
    return jnp.where(alive_mask[:, :, None], result, 0.0).astype(jnp.bfloat16)


def solution(mesh):
    in_specs = (
        P("dp", None, "mp"),
        P("dp"),
        P("dp"),
        P(),
        P("dp", None, "mp"),
        P("dp"),
        P(None, "mp"),
        P("mp", None),
        P("mp", None),
    )
    out_specs = P("dp", None, "mp")
    return jax.shard_map(
        per_device, mesh=mesh, in_specs=in_specs, out_specs=out_specs, check_vma=False
    )
```

profile of v0, /device:TPU:1, one launch (start us, length us, event | category | flops | bytes accessed | tf_op | source)
XLA Modules:
  0.0 539.9 jit_solution(12087890661670379902)
XLA Ops:
  6.5 0.8 compare_select_fusion.4
  7.4 1.4 gather_fusion
  9.9 1.4 gather_fusion.2
  11.2 1.4 gather_fusion.1
  12.6 0.7 copy.80
  13.3 9.6 %all-to-all-start.1 = ((s32[32,1,1]{2,1,0:T(1,128)}), s32[32,1,1]{2,1,0:T(1,128)S(1)}, u32[]{:S(2)}, u32[]{:S(2)}) async-start(s32[32,1,1]{2,1,0:T(1,128)} %copy.80), calls=%async_computation.1 | async-start | bytes 32768 | tf_op jit(solution)/shard_map/all_to_all | solution.py:109
  22.9 0.7 copy.81
  23.6 3.6 gather_fusion.10
  27.2 2.7 all-to-all-done.1
  29.8 4.7 all-to-all-start
  34.6 3.2 select_bitcast_fusion.1
  37.7 3.7 all-to-all-done
  41.5 5.0 all-to-all-start.5
  48.7 0.7 gather_fusion.4
  49.4 25.5 %all-to-all-done.5 = bf16[32,1,128,256]{3,2,1,0:T(8,128)(2,1)} async-done(((bf16[32,1,128,256]{3,2,1,0:T(8,128)(2,1)}), bf16[32,1,128,256]{3,2,1,0:T(8,128)(2,1)}, u32[]{:S(2)}, u32[]{:S(2)}) %all-to-all-start.5) | async-done | bytes 2097184 | tf_op jit(solution)/shard_map/all_to_all | solution.py:108
  74.9 3.6 gather_fusion.11
  78.5 3.2 broadcast_select_fusion.1
  82.3 0.7 gather_fusion.8
  83.1 0.7 copy.82
  83.8 4.3 all-to-all-start.3
  88.1 0.7 copy.85
  88.8 9.5 %gather_fusion.5 = bf16[32,256,512]{2,1,0:T(8,128)(2,1)} fusion(bf16[32,256,512]{2,1,0:T(8,128)(2,1)} %param.21, s32[1024]{0:T(1024)S(1)} %pad_clamp_fusion.1), kind=kCustom, calls=%fused_computation.2.clone | custom fusion | bytes 16777344 | tf_op jit(solution)/shard_map/jit(_take)/gather | solution.py:136
  98.3 7.5 %all-to-all-start.4 = ((s32[32,1,1]{2,1,0:T(1,128)}), s32[32,1,1]{2,1,0:T(1,128)S(1)}, u32[]{:S(2)}, u32[]{:S(2)}) async-start(s32[32,1,1]{2,1,0:T(1,128)} %copy.85), calls=%async_computation.4 | async-start | bytes 32768 | tf_op jit(solution)/shard_map/all_to_all | solution.py:146
  105.8 7.5 %select_bitcast_fusion = bf16[32,1,256,512]{3,2,1,0:T(8,128)(2,1)} fusion(bf16[32,256,512]{2,1,0:T(8,128)(2,1)} %gather_fusion.5, pred[32]{0:T(512)(128)(4,1)S(1)} %get-tuple-element.17), kind=kLoop, calls=%fused_computation.19 | loop fusion | flops 4194304 | bytes 16777248 | tf_op jit(solution)/shard_map/reshape | solution.py:136
  113.3 7.6 %all-to-all-start.2 = ((bf16[32,1,256,512]{3,2,1,0:T(8,128)(2,1)}), bf16[32,1,256,512]{3,2,1,0:T(8,128)(2,1)}, u32[]{:S(2)}, u32[]{:S(2)}) async-start(bf16[32,1,256,512]{3,2,1,0:T(8,128)(2,1)} %select_bitcast_fusion), calls=%async_computation.2 | async-start | bytes 16777216 | tf_op jit(solution)/shard_map/all_to_all | solution.py:144
  121.1 0.7 gather_fusion.6
  123.3 0.7 gather_fusion.9
  124.5 104.9 %all-to-all-done.2 = bf16[32,1,256,512]{3,2,1,0:T(8,128)(2,1)} async-done(((bf16[32,1,256,512]{3,2,1,0:T(8,128)(2,1)}), bf16[32,1,256,512]{3,2,1,0:T(8,128)(2,1)}, u32[]{:S(2)}, u32[]{:S(2)}) %all-to-all-start.2) | async-done | bytes 8388640 | tf_op jit(solution)/shard_map/all_to_all | solution.py:144
  229.4 8.6 %gather_fusion.7 = bf16[32,256,512]{2,1,0:T(8,128)(2,1)} fusion(bf16[32,256,512]{2,1,0:T(8,128)(2,1)} %bitcast.4, s32[1024]{0:T(1024)S(1)} %pad_clamp_fusion), kind=kCustom, calls=%fused_computation.10.clone | custom fusion | bytes 16777344 | tf_op jit(solution)/shard_map/jit(_take)/gather | solution.py:155
  238.0 7.5 %broadcast_select_fusion = bf16[32,256,512]{2,1,0:T(8,128)(2,1)} fusion(bf16[32,256,512]{2,1,0:T(8,128)(2,1)} %gather_fusion.7, pred[32]{0:T(512)(128)(4,1)S(1)} %get-tuple-element.15), kind=kLoop, calls=%fused_computation.21 | loop fusion | flops 4194304 | bytes 16777248 | tf_op jit(solution)/shard_map/jit(_take)/select_n | solution.py:155
  245.5 11.9 %copy.83 = bf16[32,256,512]{1,2,0:T(8,128)(2,1)} copy(bf16[32,256,512]{2,1,0:T(8,128)(2,1)} %broadcast_select_fusion) | data formatting | bytes 16777216 | tf_op jit(solution)/shard_map/jit(_take)/select_n | solution.py:155
  257.3 4.7 convert_reduce_fusion
  262.1 1.1 copy-done.4
  263.1 2.8 fusion.2
  265.9 2.2 fusion.3
  268.2 12.7 %multiply_convert_fusion = bf16[4096,1024]{1,0:T(8,128)(2,1)} fusion(bf16[4096,1024]{1,0:T(8,128)(2,1)S(1)} %bitcast.72, bf16[1024,1024]{1,0:T(8,128)(2,1)S(1)} %copy-done), kind=kOutput, calls=%fused_computation.18 | convolution fusion | flops 8610906112 | bytes 18874368 | tf_op jit(solution)/shard_map/dot_general | solution.py:45
  280.8 14.3 %reshape.247 = bf16[32,128,2,4,128]{4,3,2,1,0:T(4,128)(2,1)} reshape(bf16[4096,1024]{1,0:T(8,128)(2,1)} %multiply_convert_fusion) | data formatting | bytes 16777216 | tf_op jit(solution)/shard_map/reshape | solution.py:54
  295.1 26.3 %fusion.43 = (bf16[32,128,2,1,128]{4,3,2,1,0:T(2,128)(2,1)}, bf16[32,128,2,1,128]{4,3,2,1,0:T(2,128)(2,1)S(1)}, bf16[32,128,2,1,128]{4,3,2,1,0:T(2,128)(2,1)S(1)}, bf16[32,128,2,1,128]{4,3,2,1,0:T(2,128)(2,1)}) fusion(bf16[32,128,2,4,128]{4,3,2,1,0:T(4,128)(2,1)} %reshape.247), kind=kLoop, calls=%fused_computation.130 | loop fusion | bytes 16777216 | tf_op jit(solution)/shard_map/slice | solution.py:128
  321.4 1.3 fusion.8
  322.7 0.7 copy-done.5
  323.5 8.6 %copy.99 = bf16[32,128,2,1,128]{1,4,2,0,3:T(8,128)(2,1)S(1)} copy(bf16[32,128,2,1,128]{4,3,2,1,0:T(2,128)(2,1)} %get-tuple-element.21) | data formatting | bytes 4194304
  332.1 8.7 %fusion.44 = (f32[32,128,2]{1,2,0:T(2,128)S(1)}, f32[32,128,2,128]{1,3,2,0:T(8,128)}) fusion(bf16[32,128,2,1,128]{1,4,2,0,3:T(8,128)(2,1)S(1)} %copy.99, f32[32,128,2]{1,2,0:T(2,128)S(1)} %copy.90, f32[32]{0:T(128)S(1)} %get-tuple-element.13, f32[32,2,256]{2,1,0:T(2,128)S(1)} %convolution_bitcast_fusion, pred[32,256]{1,0:T(8,128)(4,1)S(1)} %iota_compare_fusion.2, ...), kind=kOutput, calls=%fused_computation.131 | convolution fusion | flops 1096802304 | bytes 16916608 | tf_op jit(solution)/shard_map/nhct,nthd->nchd/dot_general | solution.py:76
  340.8 3.0 multiply_reduce_fusion
  343.9 9.7 %copy.100 = bf16[32,128,2,1,128]{1,4,2,0,3:T(8,128)(2,1)} copy(bf16[32,128,2,1,128]{4,3,2,1,0:T(2,128)(2,1)} %get-tuple-element.18) | data formatting | bytes 4194304
  353.6 4.0 fusion.6
  357.6 8.1 %fusion.14 = f32[32,128,1024]{2,1,0:T(8,128)} fusion(bf16[32,128,256]{1,2,0:T(8,128)(2,1)S(1)} %bitcast.70, bf16[256,1024]{1,0:T(8,128)(2,1)S(1)} %copy-done.6), kind=kOutput, calls=%fused_computation.44 | convolution fusion | flops 2147483648 | bytes 19398656 | tf_op jit(solution)/shard_map/dot_general | solution.py:172
  365.8 163.0 %reduce-scatter.2.cloned.1.call-done = f32[32,128,256]{2,1,0:T(8,128)} async-done(((f32[32,128,1024]{2,1,0:T(8,128)}), f32[32,128,256]{2,1,0:T(8,128)}) %reduce-scatter.2.cloned.1.call-update) | async-done | bytes 4194320 | tf_op jit(solution)/shard_map/reduce_scatter | solution.py:175
  528.8 4.2 select_convert_fusion.1
  (67 shorter events, 6.4 us)
Async XLA Ops:
  6.5 261.6 %copy-start = (bf16[1024,1024]{1,0:T(8,128)(2,1)S(1)}, bf16[1024,1024]{1,0:T(8,128)(2,1)}, u32[]{:S(2)}) copy-start(bf16[1024,1024]{1,0:T(8,128)(2,1)} %param.23) | copy-start | bytes 6291460
  13.3 16.6 %all-to-all-start.1 = ((s32[32,1,1]{2,1,0:T(1,128)}), s32[32,1,1]{2,1,0:T(1,128)S(1)}, u32[]{:S(2)}, u32[]{:S(2)}) async-start(s32[32,1,1]{2,1,0:T(1,128)} %copy.80), calls=%async_computation.1 | async-start | bytes 32768 | tf_op jit(solution)/shard_map/all_to_all | solution.py:109
  29.8 11.7 %all-to-all-start = ((s32[32,1,1]{2,1,0:T(1,128)}), s32[32,1,1]{2,1,0:T(1,128)S(1)}, u32[]{:S(2)}, u32[]{:S(2)}) async-start(s32[32,1,1]{2,1,0:T(1,128)} %copy.81), calls=%async_computation | async-start | bytes 32768 | tf_op jit(solution)/shard_map/all_to_all | solution.py:110
  34.6 12.7 %copy-start.3 = (s32[1024]{0:T(1024)S(1)}, s32[1024]{0:T(1024)}, u32[]{:S(2)}) copy-start(s32[1024]{0:T(1024)} %param.20) | copy-start | bytes 12292
  41.5 33.4 %all-to-all-start.5 = ((bf16[32,1,128,256]{3,2,1,0:T(8,128)(2,1)}), bf16[32,1,128,256]{3,2,1,0:T(8,128)(2,1)}, u32[]{:S(2)}, u32[]{:S(2)}) async-start(bf16[32,1,128,256]{3,2,1,0:T(8,128)(2,1)} %select_bitcast_fusion.1), calls=%async_computation.5 | async-start | bytes 4194304 | tf_op jit(solution)/shard_map/all_to_all | solution.py:108
  46.5 210.8 %all-gather.2.cloned.1.call-start = ((), (), s32[]{:S(2)}) async-start(), calls=%async_computation.7 | async-start | bytes 10485760 | tf_op jit(solution)/shard_map/all_gather | solution.py:124
  78.5 3.8 copy-start.2
  83.8 14.5 %all-to-all-start.3 = ((s32[32,1,1]{2,1,0:T(1,128)}), s32[32,1,1]{2,1,0:T(1,128)S(1)}, u32[]{:S(2)}, u32[]{:S(2)}) async-start(s32[32,1,1]{2,1,0:T(1,128)} %copy.82), calls=%async_computation.3 | async-start | bytes 32768 | tf_op jit(solution)/shard_map/all_to_all | solution.py:145
  98.3 15.0 %all-to-all-start.4 = ((s32[32,1,1]{2,1,0:T(1,128)}), s32[32,1,1]{2,1,0:T(1,128)S(1)}, u32[]{:S(2)}, u32[]{:S(2)}) async-start(s32[32,1,1]{2,1,0:T(1,128)} %copy.85), calls=%async_computation.4 | async-start | bytes 32768 | tf_op jit(solution)/shard_map/all_to_all | solution.py:146
  113.3 7.6 %copy-start.7 = (f32[2,16]{1,0:T(2,128)S(1)}, f32[2,16]{1,0:T(2,128)}, u32[]{:S(2)}) copy-start(f32[2,16]{1,0:T(2,128)} %param.24) | copy-start | bytes 388
  113.3 116.1 %all-to-all-start.2 = ((bf16[32,1,256,512]{3,2,1,0:T(8,128)(2,1)}), bf16[32,1,256,512]{3,2,1,0:T(8,128)(2,1)}, u32[]{:S(2)}, u32[]{:S(2)}) async-start(bf16[32,1,256,512]{3,2,1,0:T(8,128)(2,1)} %select_bitcast_fusion), calls=%async_computation.2 | async-start | bytes 16777216 | tf_op jit(solution)/shard_map/all_to_all | solution.py:144
  120.9 407.9 %reduce-scatter.2.cloned.1.call-start = ((), (), s32[]{:S(2)}) async-start(), calls=%async_computation.8 | async-start | bytes 20971520 | tf_op jit(solution)/shard_map/reduce_scatter | solution.py:175
  257.3 5.8 %copy-start.4 = (bf16[32,128,1024]{2,1,0:T(8,128)(2,1)S(1)}, bf16[32,128,1024]{2,1,0:T(8,128)(2,1)}, u32[]{:S(2)}) copy-start(bf16[32,128,1024]{2,1,0:T(8,128)(2,1)} %all-gather.2.cloned.1.call-done) | copy-start | bytes 25165828
  321.4 2.0 copy-start.5
  353.6 4.0 copy-start.6
  365.7 167.3 %copy-start.1 = (bf16[1024,1024]{1,0:T(8,128)(2,1)S(1)}, bf16[1024,1024]{1,0:T(8,128)(2,1)}, u32[]{:S(2)}) copy-start(bf16[1024,1024]{1,0:T(8,128)(2,1)} %param.23) | copy-start | bytes 6291460
Sparse Core Ops, SparseCore 0:
  81.9 83.9 all-gather.1
  365.8 162.9 reduce-scatter.1
where the time goes:
time: 542 us; the launch traced here: 540 us
  waiting for transfers between devices  300 us (55%)
  local copies, waits for them, and re-layouts  108 us (20%)
  other arithmetic  49.5 us (9%)
  starting transfers between devices  38.8 us (7%)
  matrix products  29.7 us (5%)
  between operations  13.8 us (3%)
    reduce_scatter x1, waiting for transfers between devices, per_device(): lax.psum_scatter(partial_value, 'mp', scatter_dimension=2, tiled=True)  163 us
    all_to_all x1, waiting for transfers between devices, per_device(): lax.all_to_all(blocks, 'dp', split_axis=0, concat_axis=0, tiled=True)  105 us
    slice x1, local copies, waits for them, and re-layouts, per_device(): gate_part = projected[:, :, :, 0]  26.3 us
    all_to_all x1, waiting for transfers between devices, per_device(): lax.all_to_all(sent_rows, 'dp', split_axis=0, concat_axis=0, tiled=True)  25.5 us
    unnamed x18, local copies, waits for them, and re-layouts  20.1 us
    reshape x1, local copies, waits for them, and re-layouts, project(): return jax.nn.silu(linear).astype(jnp.bfloat16).reshape(request_total, ca...  14.3 us
    dot_general x1, matrix products, project(): jnp.dot(normed.reshape(request_total * cand_slots, feat_total), input_wei...  12.7 us
    select_n x1, local copies, waits for them, and re-layouts, per_device(): jnp.take(got_blocks.reshape(slot_total, events, kv_width), located, axis=0)  11.9 us
  transfers between devices with their start and end apart: 8, of which 5 were waited for; matrix products, arithmetic and copies ran while one was open for 11% of the time, Pallas kernels for 0%

commit v1 on v0

v1 whole, which is shorter than its diff:
```python
import math

import jax
import jax.numpy as jnp
from jax import lax
from jax.experimental import pallas as pl
from jax.experimental.pallas import tpu as pltpu
from jax.sharding import PartitionSpec as P

HD = 128
EPSILON = 1e-05
VMEM = 48 * 1024 * 1024

PIECES = ((0, 128),)
BATCH = 4


def permute_out(index, parts, out_rows, pieces):
    users = parts[0].shape[0]
    width = parts[0].shape[2]

    def body(index_ref, *refs):
        ins, out, sem = refs[: len(parts)], refs[len(parts)], refs[len(parts) + 1]

        def copy(i, c):
            start, size = pieces[c]
            return pltpu.make_async_copy(
                ins[c].at[i], out.at[index_ref[i], pl.ds(start, size)], sem.at[c, i]
            )

        for c in range(len(parts)):
            for i in range(users):
                copy(i, c).start()
        for c in range(len(parts)):
            for i in range(users):
                copy(i, c).wait()

    return pl.pallas_call(
        body,
        out_shape=jax.ShapeDtypeStruct((users, out_rows, width), parts[0].dtype),
        in_specs=[pl.BlockSpec(memory_space=pltpu.SMEM)]
        + [pl.BlockSpec(memory_space=pl.ANY)] * len(parts),
        out_specs=pl.BlockSpec(memory_space=pl.ANY),
        scratch_shapes=[pltpu.SemaphoreType.DMA((len(parts), users))],
    )(index, *parts)


def permute_in(index, whole, piece):
    users, _, width = whole.shape
    start, size = piece

    def body(index_ref, src, out, sem):
        def copy(i):
            return pltpu.make_async_copy(
                src.at[index_ref[i], pl.ds(start, size)], out.at[i], sem.at[i]
            )

        for i in range(users):
            copy(i).start()
        for i in range(users):
            copy(i).wait()

    return pl.pallas_call(
        body,
        out_shape=jax.ShapeDtypeStruct((users, size, width), whole.dtype),
        in_specs=[pl.BlockSpec(memory_space=pltpu.SMEM), pl.BlockSpec(memory_space=pl.ANY)],
        out_specs=pl.BlockSpec(memory_space=pl.ANY),
        scratch_shapes=[pltpu.SemaphoreType.DMA((users,))],
    )(index, whole)


def attend(full, weight, history, order, rows_info, heads):
    mp, users, rows, part = full.shape
    events, kv_width = history.shape[1:]
    quarter = rows // mp
    total = BATCH * rows
    inv_scale = 1.0 / math.sqrt(HD)

    def body(order_ref, full_ref, weight_ref, info_ref, *refs):
        hist_refs, out_ref = refs[:BATCH], refs[BATCH]
        parts = [full_ref[k].reshape(total, part).astype(jnp.float32) for k in range(mp)]
        width = mp * part
        mean = sum(jnp.sum(p, axis=-1, keepdims=True) for p in parts) * (1.0 / width)
        parts = [p - mean for p in parts]
        var = sum(jnp.sum(p * p, axis=-1, keepdims=True) for p in parts) * (1.0 / width)
        factor = lax.rsqrt(var + EPSILON)
        normed = jnp.concatenate([(p * factor).astype(jnp.bfloat16) for p in parts], axis=1)
        for h in range(heads):
            half = 0.5 * jnp.dot(
                normed,
                weight_ref[:, h * 4 * HD : (h + 1) * 4 * HD],
                preferred_element_type=jnp.float32,
            )
            projected = (half + half * jnp.tanh(half)).astype(jnp.bfloat16)
            for b in range(BATCH):
                mine = projected[b * rows : (b + 1) * rows]
                gate = mine[:, :HD].astype(jnp.float32)
                value = mine[:, HD : 2 * HD].astype(jnp.float32)
                query = mine[:, 2 * HD : 3 * HD]
                key = mine[:, 3 * HD :].astype(jnp.float32)
                cache_key = hist_refs[b][0, :, 2 * h * HD : (2 * h + 1) * HD]
                cache_value = hist_refs[b][0, :, (2 * h + 1) * HD : (2 * h + 2) * HD]
                score = lax.dot_general(
                    query, cache_key, (((1,), (1,)), ((), ())), preferred_element_type=jnp.float32
                )
                score = score * (0.5 * inv_scale) + info_ref[b, h : h + 1, :]
                weights = (score + score * jnp.tanh(score)) * info_ref[b, 2 * heads : 2 * heads + 1, :]
                summed = jnp.dot(
                    weights.astype(jnp.bfloat16), cache_value, preferred_element_type=jnp.float32
                )
                own = jnp.sum(query.astype(jnp.float32) * key, axis=-1, keepdims=True)
                own = own * (0.5 * inv_scale) + info_ref[b, heads + h : heads + h + 1, :HD]
                own = (own + own * jnp.tanh(own)) * info_ref[b, 2 * heads + 1 : 2 * heads + 2, :HD]
                own = own.astype(jnp.bfloat16).astype(jnp.float32)
                combined = summed + own * value
                head_mean = jnp.mean(combined, axis=-1, keepdims=True)
                centred = combined - head_mean
                head_var = jnp.mean(centred * centred, axis=-1, keepdims=True)
                gated = (centred * lax.rsqrt(head_var + EPSILON) * gate).astype(jnp.bfloat16)
                for q in range(mp):
                    out_ref[q, b, :, h * HD : (h + 1) * HD] = gated[q * quarter : (q + 1) * quarter]

    def hist_spec(b):
        return pl.BlockSpec((1, events, kv_width), lambda i, order: (order[i * BATCH + b], 0, 0))

    return pl.pallas_call(
        body,
        out_shape=jax.ShapeDtypeStruct((mp, users, quarter, heads * HD), jnp.bfloat16),
        grid_spec=pltpu.PrefetchScalarGridSpec(
            num_scalar_prefetch=1,
            grid=(users // BATCH,),
            in_specs=[
                pl.BlockSpec((mp, BATCH, rows, part), lambda i, order: (0, i, 0, 0)),
                pl.BlockSpec(weight.shape, lambda i, order: (0, 0)),
                pl.BlockSpec((BATCH,) + rows_info.shape[1:], lambda i, order: (i, 0, 0)),
            ]
            + [hist_spec(b) for b in range(BATCH)],
            out_specs=pl.BlockSpec(
                (mp, BATCH, quarter, heads * HD), lambda i, order: (0, i, 0, 0)
            ),
        ),
        compiler_params=pltpu.CompilerParams(vmem_limit_bytes=VMEM),
    )(order, full, weight, rows_info, *([history] * BATCH))


def project_out(gated, full, weight, scalars, start):
    mp, users, quarter, part = gated.shape
    out_part = weight.shape[2] // mp
    batch = 8

    def body(scalar_ref, gated_ref, full_ref, weight_ref, out_ref):
        first = pl.program_id(0) * batch
        acc = jnp.dot(
            gated_ref[0].reshape(batch * quarter, part),
            weight_ref[0],
            preferred_element_type=jnp.float32,
        )
        for k in range(1, mp):
            acc = acc + jnp.dot(
                gated_ref[k].reshape(batch * quarter, part),
                weight_ref[k],
                preferred_element_type=jnp.float32,
            )
        row = lax.broadcasted_iota(jnp.int32, (quarter, out_part), 0)
        row = row + (start + scalar_ref[0] * quarter)
        for b in range(batch):
            alive = row < scalar_ref[1 + first + b]
            for k in range(mp):
                mine = acc[b * quarter : (b + 1) * quarter, k * out_part : (k + 1) * out_part]
                mine = mine + full_ref[k, b].astype(jnp.float32)
                out_ref[b, k] = jnp.where(alive, mine, 0.0).astype(jnp.bfloat16)

    return pl.pallas_call(
        body,
        out_shape=jax.ShapeDtypeStruct((users, mp, quarter, out_part), jnp.bfloat16),
        grid_spec=pltpu.PrefetchScalarGridSpec(
            num_scalar_prefetch=1,
            grid=(users // batch,),
            in_specs=[
                pl.BlockSpec((mp, batch, quarter, part), lambda i, s: (0, i, 0, 0)),
                pl.BlockSpec((mp, batch, quarter, part), lambda i, s: (0, i, s[0], 0)),
                pl.BlockSpec(weight.shape, lambda i, s: (0, 0, 0)),
            ],
            out_specs=pl.BlockSpec((batch, mp, quarter, out_part), lambda i, s: (i, 0, 0, 0)),
        ),
        compiler_params=pltpu.CompilerParams(vmem_limit_bytes=VMEM),
    )(scalars, gated, full, weight)


def bucket_bias(distance, time_bias):
    bias = jnp.broadcast_to(time_bias[:, 0][:, None, None], time_bias.shape[:1] + distance.shape)
    for k in range(time_bias.shape[1] - 1):
        bias = jnp.where((distance >= 2**k)[None], time_bias[:, k + 1][:, None, None], bias)
    return bias


def per_device(
    candidates,
    live_counts,
    request_user,
    score_slot,
    history_cache,
    history_length,
    input_weight,
    time_bias,
    output_weight,
):
    dp_size = lax.axis_size("dp")
    dp_rank = lax.axis_index("dp")
    mp_rank = lax.axis_index("mp")
    users, slots, part = candidates.shape
    events = history_cache.shape[1]
    heads = time_bias.shape[0]
    ranks = jnp.arange(dp_size, dtype=jnp.int32)
    local = jnp.arange(users, dtype=jnp.int32)
    scorer = score_slot // users

    table = lax.all_gather(jnp.stack([request_user, live_counts]), "dp", axis=0, tiled=False)
    all_users = table[:, 0].reshape(-1)
    all_live = table[:, 1].reshape(-1)
    weight_out = lax.all_gather(output_weight, "mp", axis=0, tiled=False)

    target = jnp.take(scorer, request_user)
    send_first = jnp.sum(jnp.where(target[None, :] == ranks[:, None], local[None, :], 0), axis=1)
    scored_here = scorer.reshape(dp_size, users) == dp_rank
    ids = jnp.arange(dp_size * users, dtype=jnp.int32)
    mine = jnp.sum(jnp.where(scored_here, ids.reshape(dp_size, users), 0), axis=1)
    place = jnp.sum(
        jnp.where(scored_here, score_slot.reshape(dp_size, users), 0), axis=1
    ) - dp_rank * users
    send_second = (
        jnp.sum(jnp.where(all_users[None, :] == mine[:, None], ids[None, :], 0), axis=1) // users
    )
    own_scorer = lax.dynamic_slice_in_dim(scorer, dp_rank * users, users)
    order = jnp.sum(jnp.where(own_scorer[None, :] == ranks[:, None], local[None, :], 0), axis=1)
    owned = dp_rank * users + order
    live = jnp.sum(jnp.where(all_users[None, :] == owned[:, None], all_live[None, :], 0), axis=1)
    scalars = jnp.concatenate([mp_rank[None], live]).astype(jnp.int32)

    lengths = jnp.take(history_length, order)
    position = jnp.arange(events, dtype=jnp.int32)
    distance = lengths[:, None] - position[None, :]
    inverse = 1.0 / (lengths + 1).astype(jnp.float32)
    spread = jnp.broadcast_to(inverse[:, None], (users, events))
    bias = 0.5 * bucket_bias(distance, time_bias)
    own_bias = jnp.broadcast_to(0.5 * time_bias[:, 0][:, None, None], bias.shape)
    info = [bias[h] for h in range(heads)] + [own_bias[h] for h in range(heads)]
    info = info + [jnp.where(distance > 0, spread, 0.0), spread]
    info = info + [jnp.zeros_like(spread)] * (-len(info) % 8)
    rows_info = jnp.stack(info, axis=1)

    results = []
    for piece in PIECES:
        rows = permute_in(send_first, candidates, piece)
        rows = lax.all_to_all(rows, "dp", split_axis=0, concat_axis=0, tiled=True)
        rows = permute_in(send_second, rows, (0, piece[1]))
        rows = lax.all_to_all(rows, "dp", split_axis=0, concat_axis=0, tiled=True)
        full = lax.all_gather(rows, "mp", axis=0, tiled=False)
        gated = attend(full, input_weight, history_cache, order, rows_info, heads)
        gated = lax.all_to_all(gated, "mp", split_axis=0, concat_axis=0, tiled=True)
        done = project_out(gated, full, weight_out, scalars, piece[0])
        done = done.reshape((-1,) + done.shape[2:])
        done = lax.all_to_all(done, ("dp", "mp"), split_axis=0, concat_axis=0, tiled=True)
        results.append(done.reshape(users, piece[1], part))
    return permute_out(place, results, slots, PIECES)


def solution(mesh):
    in_specs = (
        P("dp", None, "mp"),
        P("dp"),
        P("dp"),
        P(),
        P("dp", None, "mp"),
        P("dp"),
        P(None, "mp"),
        P("mp", None),
        P("mp", None),
    )
    out_specs = P("dp", None, "mp")
    return jax.shard_map(
        per_device, mesh=mesh, in_specs=in_specs, out_specs=out_specs, check_vma=False
    )
```

time: 542 us -> 487 us (0.90)
  Pallas kernels: 0 us -> 227 us
  waiting for transfers between devices: 300 us -> 134 us
  local copies, waits for them, and re-layouts: 108 us -> 8.18 us
  blocking collectives: 0 us -> 76.2 us
  other arithmetic: 49.5 us -> 5.6 us
  matrix products: 29.7 us -> 0 us
  starting transfers between devices: 38.8 us -> 21.8 us
    pallas_call x0 -> x5, Pallas kernels: none -> 227 us  [the longest x2 131 us: permute_in(): pl.pallas_call(body, out_shape=jax.ShapeDtypeStruct((users, size, width),...]
    reduce_scatter x1 -> x0, waiting for transfers between devices: 163 us -> none  [per_device(): lax.psum_scatter(partial_value, 'mp', scatter_dimension=2, tiled=True)]
    all_to_all x6 -> x3, waiting for transfers between devices: 137 us -> 52.2 us  [the longest x1 30.5 us: per_device(): lax.all_to_all(done, ('dp', 'mp'), split_axis=0, concat_axis=0, tiled=True)]
    all_gather x1 -> x2, waiting for transfers between devices: 0.01 us -> 81.1 us  [the longest x1 75.6 us: per_device(): full = lax.all_gather(rows, 'mp', axis=0, tiled=False)]
    all_gather x0 -> x1, blocking collectives: none -> 43.4 us  [per_device(): lax.all_gather(jnp.stack([request_user, live_counts]), 'dp', axis=0, tile...]
    all_to_all x0 -> x1, blocking collectives: none -> 32.8 us  [per_device(): rows = lax.all_to_all(rows, 'dp', split_axis=0, concat_axis=0, tiled=True)]
    gather x12 -> x2, local copies, waits for them, and re-layouts: 32.8 us -> 1.37 us  [the longest x1 0.7 us: per_device(): lengths = jnp.take(history_length, order)]
    dot_general x4 -> x0, matrix products: 29.7 us -> none  [the longest x1 12.7 us: project(): jnp.dot(normed.reshape(request_total * cand_slots, feat_total), input_wei...]
  transfers between devices with their start and end apart: 8 -> 5, of which waited for: 5 -> 4; matrix products, arithmetic and copies ran while one was open for 11% -> 1% of each run, Pallas kernels for 0% -> 5%
where the time goes in v1:
time: 487 us; the launch traced here: 486 us
  Pallas kernels  227 us (47%)
  waiting for transfers between devices  134 us (28%)
  blocking collectives  76.2 us (16%)
  starting transfers between devices  21.8 us (4%)
  between operations  13.6 us (3%)
  local copies, waits for them, and re-layouts  8.18 us (2%)
  other arithmetic  5.6 us (1%)
    pallas_call x2, Pallas kernels, permute_in(): pl.pallas_call(body, out_shape=jax.ShapeDtypeStruct((users, size, width),...  131 us
    all_gather x1, waiting for transfers between devices, per_device(): full = lax.all_gather(rows, 'mp', axis=0, tiled=False)  75.6 us
    pallas_call x1, Pallas kernels, permute_out(): pl.pallas_call(body, out_shape=jax.ShapeDtypeStruct((users, out_rows, wid...  65.6 us
    all_gather x1, blocking collectives, per_device(): lax.all_gather(jnp.stack([request_user, live_counts]), 'dp', axis=0, tile...  43.4 us
    all_to_all x1, blocking collectives, per_device(): rows = lax.all_to_all(rows, 'dp', split_axis=0, concat_axis=0, tiled=True)  32.8 us
    all_to_all x1, waiting for transfers between devices, per_device(): lax.all_to_all(done, ('dp', 'mp'), split_axis=0, concat_axis=0, tiled=True)  30.5 us
    pallas_call x1, Pallas kernels, attend(): pl.pallas_call(body, out_shape=jax.ShapeDtypeStruct((mp, users, quarter,...  24.6 us
    all_to_all x1, waiting for transfers between devices, per_device(): gated = lax.all_to_all(gated, 'mp', split_axis=0, concat_axis=0, tiled=True)  21.7 us
  transfers between devices with their start and end apart: 5, of which 4 were waited for; matrix products, arithmetic and copies ran while one was open for 1% of the time, Pallas kernels for 5%

profile of v1, /device:TPU:1, one launch (start us, length us, event | category | flops | bytes accessed | tf_op | source)
XLA Modules:
  0.0 486.5 jit_solution(13965470674185476310)
XLA Ops:
  6.5 0.7 compare_select_fusion.3
  7.2 0.7 broadcast_compare_fusion
  7.9 0.7 gather_fusion
  8.6 0.7 and_select_fusion.1
  9.3 0.7 select_reduce_fusion.2.index_ref
  10.0 65.6 %shard_map.91 = bf16[32,128,256]{2,1,0:T(8,128)(2,1)} custom-call(s32[32]{0:T(128)} %select_reduce_fusion.2.index_ref, bf16[32,128,256]{2,1,0:T(8,128)(2,1)} %src.1), custom_call_target="tpu_custom_call" | custom-call | tf_op jit(solution)/shard_map/pallas_call | solution.py:63
  75.6 9.7 %all-to-all-start = ((bf16[32,128,256]{2,1,0:T(8,128)(2,1)}), bf16[32,128,256]{2,1,0:T(8,128)(2,1)S(1)}, u32[]{:S(2)}, u32[]{:S(2)}) async-start(bf16[32,128,256]{2,1,0:T(8,128)(2,1)} %shard_map.91), calls=%async_computation | async-start | bytes 4194304 | tf_op jit(solution)/shard_map/all_to_all | solution.py:255
  85.3 0.0 all-gather.7.cloned.1.call-start
  85.4 0.1 reshape.431
  85.5 0.1 eq.63
  85.6 43.4 %all-gather.3 = s32[32,2,32]{2,1,0:T(2,128)S(1)} all-gather(s32[1,2,32]{2,1,0:T(2,128)S(1)} %add_bitcast_fusion), channel_id=2, replica_groups=mesh['dp'=32,'mp'=4] {'dp'}, dimensions={0}, use_global_device_ids=true | all-gather | bytes 8448 | tf_op jit(solution)/shard_map/all_gather | solution.py:218
  128.9 0.1 slice_reduce_fusion.1
  129.0 0.1 eq.64
  129.1 0.1 broadcast_in_dim.299
  129.2 0.1 dynamic_slice.3
  129.2 0.1 select_reduce_fusion.4.order_ref
  129.4 0.1 select_reduce_fusion.3
  129.5 0.2 select_reduce_fusion
  129.7 0.5 and_select_fusion.2.index_ref
  130.2 1.3 copy-done.3
  131.6 65.6 %shard_map.92 = bf16[32,128,256]{2,1,0:T(8,128)(2,1)} custom-call(s32[32]{0:T(128)} %and_select_fusion.2.index_ref, bf16[32,128,256]{2,1,0:T(8,128)(2,1)} %copy-done.3), custom_call_target="tpu_custom_call" | custom-call | tf_op jit(solution)/shard_map/pallas_call | solution.py:63
  197.1 32.8 %all_to_all.20 = bf16[32,128,256]{2,1,0:T(8,128)(2,1)} all-to-all(bf16[32,128,256]{2,1,0:T(8,128)(2,1)} %shard_map.92), channel_id=1, replica_groups=mesh['dp'=32,'mp'=4] {'dp'}, dimensions={0} | all-to-all | bytes 4194304 | tf_op jit(solution)/shard_map/all_to_all | solution.py:257
  230.0 0.0 all-gather.9.cloned.1.call-start
  230.0 0.7 all-gather.9.cloned.1.call-update
  230.8 0.7 gather_fusion.1
  231.5 0.4 slice_reduce_fusion.2
  231.9 0.5 fusion.18
  232.4 0.1 compare_select_fusion
  232.6 0.1 fusion.14
  232.7 0.5 select_multiply_fusion
  233.3 0.1 slice_bitcast_fusion
  233.3 0.6 broadcast_in_dim.354
  234.0 0.7 broadcast_in_dim.356
  234.6 0.1 broadcast_in_dim.357
  234.8 0.3 stack.20.info_ref
  235.1 75.6 %all-gather.7.cloned.1.call-done = bf16[128,128,256]{2,1,0:T(8,128)(2,1)} async-done(((bf16[32,128,256]{2,1,0:T(8,128)(2,1)}), bf16[128,128,256]{2,1,0:T(8,128)(2,1)}) %all-gather.7.cloned.1.call-update) | async-done | bytes 8388624 | tf_op jit(solution)/shard_map/all_gather | solution.py:258
  310.8 24.6 %shard_map.93 = bf16[4,32,32,256]{3,2,1,0:T(8,128)(2,1)} custom-call(s32[32]{0:T(128)S(1)} %select_reduce_fusion.4.order_ref, bf16[4,32,128,256]{3,2,1,0:T(8,128)(2,1)} %bitcast.20, bf16[1024,1024]{1,0:T(8,128)(2,1)S(1)} %copy-done.2, f32[32,8,256]{2,1,0:T(8,128)S(1)} %stack.20.info_ref, bf16[32,256,512]{2,1,0:T(8,128)(2,1)} %refs_3_.1, ...), custom_call_target="tpu_custom_call" | custom-call | tf_op jit(solution)/shard_map/pallas_call | solution.py:126
  335.4 3.7 all-to-all-start.2
  339.1 0.1 pad_add_fusion.scalar_ref
  339.1 5.5 %all-gather.9.cloned.1.call-done = bf16[1024,1024]{1,0:T(8,128)(2,1)} async-done(((bf16[256,1024]{1,0:T(8,128)(2,1)}), bf16[1024,1024]{1,0:T(8,128)(2,1)}) %all-gather.9.cloned.1.call-update) | async-done | bytes 2097168 | tf_op jit(solution)/shard_map/all_gather | solution.py:221
  344.6 21.7 %all-to-all-done.2.gated_ref = bf16[4,32,32,256]{3,2,1,0:T(8,128)(2,1)S(1)} async-done(((bf16[4,32,32,256]{3,2,1,0:T(8,128)(2,1)}), bf16[4,32,32,256]{3,2,1,0:T(8,128)(2,1)S(1)}, u32[]{:S(2)}, u32[]{:S(2)}) %all-to-all-start.2) | async-done | bytes 2097184 | tf_op jit(solution)/shard_map/all_to_all | solution.py:260
  366.3 5.7 %shard_map.94 = bf16[32,4,32,256]{3,2,1,0:T(8,128)(2,1)S(1)} custom-call(s32[33]{0:T(128)S(1)} %pad_add_fusion.scalar_ref, bf16[4,32,32,256]{3,2,1,0:T(8,128)(2,1)S(1)} %all-to-all-done.2.gated_ref, bf16[4,32,128,256]{3,2,1,0:T(8,128)(2,1)} %bitcast.21, bf16[4,256,1024]{2,1,0:T(8,128)(2,1)} %bitcast.23), custom_call_target="tpu_custom_call" | custom-call | tf_op jit(solution)/shard_map/pallas_call | solution.py:173
  372.1 1.3 copy-done.1
  373.4 8.3 %all-to-all-start.3 = ((bf16[128,32,256]{2,1,0:T(8,128)(2,1)}), bf16[128,32,256]{2,1,0:T(8,128)(2,1)S(1)}, u32[]{:S(2)}, u32[]{:S(2)}) async-start(bf16[128,32,256]{2,1,0:T(8,128)(2,1)} %bitcast.19), calls=%async_computation.3 | async-start | bytes 4194304 | tf_op jit(solution)/shard_map/all_to_all | solution.py:263
  381.7 0.5 broadcast_subtract_fusion.index_ref
  382.2 30.5 %all-to-all-done.3 = bf16[128,32,256]{2,1,0:T(8,128)(2,1)S(1)} async-done(((bf16[128,32,256]{2,1,0:T(8,128)(2,1)}), bf16[128,32,256]{2,1,0:T(8,128)(2,1)S(1)}, u32[]{:S(2)}, u32[]{:S(2)}) %all-to-all-start.3) | async-done | bytes 2097184 | tf_op jit(solution)/shard_map/all_to_all | solution.py:263
  412.7 1.3 copy-done.4
  414.0 65.6 %shard_map.95 = bf16[32,128,256]{2,1,0:T(8,128)(2,1)} custom-call(s32[32]{0:T(128)} %broadcast_subtract_fusion.index_ref, bf16[32,128,256]{2,1,0:T(8,128)(2,1)} %bitcast.22), custom_call_target="tpu_custom_call" | custom-call | tf_op jit(solution)/shard_map/pallas_call | solution.py:38
  (24 shorter events, 0.1 us)
Async XLA Ops:
  6.5 224.2 %copy-start = (s32[32]{0:T(128)S(1)}, s32[32]{0:T(128)}, u32[]{:S(2)}) copy-start(s32[32]{0:T(128)} %param.14) | copy-start | bytes 388
  75.5 9.8 %copy-start.6 = (s32[1024]{0:T(1024)S(1)}, s32[1024]{0:T(1024)}, u32[]{:S(2)}) copy-start(s32[1024]{0:T(1024)} %param.12) | copy-start | bytes 12292
  75.6 10.0 %copy-start.7 = (s32[32]{0:T(128)S(1)}, s32[32]{0:T(128)}, u32[]{:S(2)}) copy-start(s32[32]{0:T(128)} %param.10) | copy-start | bytes 388
  75.6 10.0 %copy-start.8 = (s32[32]{0:T(128)S(1)}, s32[32]{0:T(128)}, u32[]{:S(2)}) copy-start(s32[32]{0:T(128)} %param.11) | copy-start | bytes 388
  75.6 54.6 %all-to-all-start = ((bf16[32,128,256]{2,1,0:T(8,128)(2,1)}), bf16[32,128,256]{2,1,0:T(8,128)(2,1)S(1)}, u32[]{:S(2)}, u32[]{:S(2)}) async-start(bf16[32,128,256]{2,1,0:T(8,128)(2,1)} %shard_map.91), calls=%async_computation | async-start | bytes 4194304 | tf_op jit(solution)/shard_map/all_to_all | solution.py:255
  85.3 225.4 %all-gather.7.cloned.1.call-start = ((), (), s32[]{:S(2)}) async-start(), calls=%async_computation.4 | async-start | bytes 10485760 | tf_op jit(solution)/shard_map/all_gather | solution.py:258
  130.2 1.3 copy-start.3
  229.9 1.5 copy-start.5
  229.9 80.8 %copy-start.2 = (bf16[1024,1024]{1,0:T(8,128)(2,1)S(1)}, bf16[1024,1024]{1,0:T(8,128)(2,1)}, u32[]{:S(2)}) copy-start(bf16[1024,1024]{1,0:T(8,128)(2,1)} %weight_ref.1) | copy-start | bytes 6291460
  230.0 114.6 %all-gather.9.cloned.1.call-start = ((), (), s32[]{:S(2)}) async-start(), calls=%async_computation.5 | async-start | bytes 2621440 | tf_op jit(solution)/shard_map/all_gather | solution.py:221
  335.4 31.0 %all-to-all-start.2 = ((bf16[4,32,32,256]{3,2,1,0:T(8,128)(2,1)}), bf16[4,32,32,256]{3,2,1,0:T(8,128)(2,1)S(1)}, u32[]{:S(2)}, u32[]{:S(2)}) async-start(bf16[4,32,32,256]{3,2,1,0:T(8,128)(2,1)} %shard_map.93), calls=%async_computation.2 | async-start | bytes 4194304 | tf_op jit(solution)/shard_map/all_to_all | solution.py:260
  372.1 1.3 copy-start.1
  373.4 39.3 %all-to-all-start.3 = ((bf16[128,32,256]{2,1,0:T(8,128)(2,1)}), bf16[128,32,256]{2,1,0:T(8,128)(2,1)S(1)}, u32[]{:S(2)}, u32[]{:S(2)}) async-start(bf16[128,32,256]{2,1,0:T(8,128)(2,1)} %bitcast.19), calls=%async_computation.3 | async-start | bytes 4194304 | tf_op jit(solution)/shard_map/all_to_all | solution.py:263
  412.7 1.4 copy-start.4
Sparse Core Ops, SparseCore 0:
  230.1 80.6 all-gather.6
  312.4 32.1 all-gather.8

commit v2 on v1

--- a/solution.py
+++ b/solution.py
@@ -11,37 +11,45 @@
 EPSILON = 1e-05
 VMEM = 48 * 1024 * 1024
 
-PIECES = ((0, 128),)
-BATCH = 4
+PIECES = ((0, 64), (64, 64))
+BATCH = 8
 
 
 def permute_out(index, parts, out_rows, pieces):
-    users = parts[0].shape[0]
-    width = parts[0].shape[2]
+    users, _, width = parts[0].shape
+    count = len(parts)
 
     def body(index_ref, *refs):
-        ins, out, sem = refs[: len(parts)], refs[len(parts)], refs[len(parts) + 1]
-
-        def copy(i, c):
+        ins, out = refs[:count], refs[count]
+        buffers, sem_in, sem_out = refs[count + 1 : 2 * count + 1], refs[-2], refs[-1]
+
+        def load(c, i):
+            return pltpu.make_async_copy(ins[c].at[i], buffers[c].at[i], sem_in.at[c, i])
+
+        def store(c, i):
             start, size = pieces[c]
             return pltpu.make_async_copy(
-                ins[c].at[i], out.at[index_ref[i], pl.ds(start, size)], sem.at[c, i]
+                buffers[c].at[i], out.at[index_ref[i], pl.ds(start, size)], sem_out.at[c, i]
             )
 
-        for c in range(len(parts)):
-            for i in range(users):
-                copy(i, c).start()
-        for c in range(len(parts)):
-            for i in range(users):
-                copy(i, c).wait()
+        every = [(c, i) for c in range(count) for i in range(users)]
+        for c, i in every:
+            load(c, i).start()
+        for c, i in every:
+            load(c, i).wait()
+            store(c, i).start()
+        for c, i in every:
+            store(c, i).wait()
 
     return pl.pallas_call(
         body,
         out_shape=jax.ShapeDtypeStruct((users, out_rows, width), parts[0].dtype),
         in_specs=[pl.BlockSpec(memory_space=pltpu.SMEM)]
-        + [pl.BlockSpec(memory_space=pl.ANY)] * len(parts),
+        + [pl.BlockSpec(memory_space=pl.ANY)] * count,
         out_specs=pl.BlockSpec(memory_space=pl.ANY),
-        scratch_shapes=[pltpu.SemaphoreType.DMA((len(parts), users))],
+        scratch_shapes=[pltpu.VMEM(p.shape, p.dtype) for p in parts]
+        + [pltpu.SemaphoreType.DMA((count, users))] * 2,
+        compiler_params=pltpu.CompilerParams(vmem_limit_bytes=VMEM),
     )(index, *parts)
 
 
@@ -49,23 +57,31 @@
     users, _, width = whole.shape
     start, size = piece
 
-    def body(index_ref, src, out, sem):
-        def copy(i):
+    def body(index_ref, src, out, buffer, sem_in, sem_out):
+        def load(i):
             return pltpu.make_async_copy(
-                src.at[index_ref[i], pl.ds(start, size)], out.at[i], sem.at[i]
+                src.at[index_ref[i], pl.ds(start, size)], buffer.at[i], sem_in.at[i]
             )
 
+        def store(i):
+            return pltpu.make_async_copy(buffer.at[i], out.at[i], sem_out.at[i])
+
         for i in range(users):
-            copy(i).start()
+            load(i).start()
         for i in range(users):
-            copy(i).wait()
+            load(i).wait()
+            store(i).start()
+        for i in range(users):
+            store(i).wait()
 
     return pl.pallas_call(
         body,
         out_shape=jax.ShapeDtypeStruct((users, size, width), whole.dtype),
         in_specs=[pl.BlockSpec(memory_space=pltpu.SMEM), pl.BlockSpec(memory_space=pl.ANY)],
         out_specs=pl.BlockSpec(memory_space=pl.ANY),
-        scratch_shapes=[pltpu.SemaphoreType.DMA((users,))],
+        scratch_shapes=[pltpu.VMEM((users, size, width), whole.dtype)]
+        + [pltpu.SemaphoreType.DMA((users,))] * 2,
+        compiler_params=pltpu.CompilerParams(vmem_limit_bytes=VMEM),
     )(index, whole)
 
 
@@ -215,7 +231,14 @@
     local = jnp.arange(users, dtype=jnp.int32)
     scorer = score_slot // users
 
-    table = lax.all_gather(jnp.stack([request_user, live_counts]), "dp", axis=0, tiled=False)
+    own_table = jnp.stack([request_user, live_counts])
+    table = lax.all_to_all(
+        jnp.broadcast_to(own_table[None], (dp_size,) + own_table.shape),
+        "dp",
+        split_axis=0,
+        concat_axis=0,
+        tiled=True,
+    )
     all_users = table[:, 0].reshape(-1)
     all_live = table[:, 1].reshape(-1)
     weight_out = lax.all_gather(output_weight, "mp", axis=0, tiled=False)
@@ -249,12 +272,20 @@
     info = info + [jnp.zeros_like(spread)] * (-len(info) % 8)
     rows_info = jnp.stack(info, axis=1)
 
-    results = []
+    arrived = []
+    before = None
     for piece in PIECES:
         rows = permute_in(send_first, candidates, piece)
+        if before is not None:
+            rows, before = lax.optimization_barrier((rows, before))
         rows = lax.all_to_all(rows, "dp", split_axis=0, concat_axis=0, tiled=True)
         rows = permute_in(send_second, rows, (0, piece[1]))
-        rows = lax.all_to_all(rows, "dp", split_axis=0, concat_axis=0, tiled=True)
+        before = lax.all_to_all(rows, "dp", split_axis=0, concat_axis=0, tiled=True)
+        arrived.append(before)
+
+    results = []
+    for piece, rows in zip(PIECES, arrived):
+        rows, weight_out = lax.optimization_barrier((rows, weight_out))
         full = lax.all_gather(rows, "mp", axis=0, tiled=False)
         gated = attend(full, input_weight, history_cache, order, rows_info, heads)
         gated = lax.all_to_all(gated, "mp", split_axis=0, concat_axis=0, tiled=True)

time: 487 us -> 288 us (0.59)
  Pallas kernels: 227 us -> 71.4 us
  waiting for transfers between devices: 134 us -> 88.9 us
  starting transfers between devices: 21.8 us -> 37.8 us
  blocking collectives: 76.2 us -> 62.5 us
    pallas_call x2 -> x4, Pallas kernels: 131 us -> 15.6 us  [permute_in(): pl.pallas_call(body, out_shape=jax.ShapeDtypeStruct((users, size, width),...]
    pallas_call x1, Pallas kernels: 65.6 us -> 5.69 us  [permute_out(): pl.pallas_call(body, out_shape=jax.ShapeDtypeStruct((users, out_rows, wid...]
    all_gather x1 -> x2, waiting for transfers between devices: 75.6 us -> 28.2 us  [per_device(): full = lax.all_gather(rows, 'mp', axis=0, tiled=False)]
    all_gather x1 -> x0, blocking collectives: 43.4 us -> none  [per_device(): lax.all_gather(jnp.stack([request_user, live_counts]), 'dp', axis=0, tile...]
    all_to_all x0 -> x2, blocking collectives: none -> 41.8 us  [per_device(): before = lax.all_to_all(rows, 'dp', split_axis=0, concat_axis=0, tiled=True)]
    pallas_call x1 -> x2, Pallas kernels: 24.6 us -> 42 us  [attend(): pl.pallas_call(body, out_shape=jax.ShapeDtypeStruct((mp, users, quarter,...]
    all_to_all x1, waiting for transfers between devices: 0.01 us -> 15.9 us  [per_device(): rows = lax.all_to_all(rows, 'dp', split_axis=0, concat_axis=0, tiled=True)]
    all_to_all x1 -> x2, waiting for transfers between devices: 21.7 us -> 9.53 us  [per_device(): gated = lax.all_to_all(gated, 'mp', split_axis=0, concat_axis=0, tiled=True)]
  transfers between devices with their start and end apart: 5 -> 9, of which waited for: 4 -> 5; matrix products, arithmetic and copies ran while one was open for 1% -> 3% of each run, Pallas kernels for 5% -> 23%
where the time goes in v2:
time: 288 us; the launch traced here: 287 us
  waiting for transfers between devices  88.9 us (31%)
  Pallas kernels  71.4 us (25%)
  blocking collectives  62.5 us (22%)
  starting transfers between devices  37.8 us (13%)
  between operations  13.4 us (5%)
  local copies, waits for them, and re-layouts  8.49 us (3%)
  other arithmetic  4.63 us (2%)
    pallas_call x2, Pallas kernels, attend(): pl.pallas_call(body, out_shape=jax.ShapeDtypeStruct((mp, users, quarter,...  42 us
    all_to_all x2, blocking collectives, per_device(): before = lax.all_to_all(rows, 'dp', split_axis=0, concat_axis=0, tiled=True)  41.8 us
    all_to_all x2, waiting for transfers between devices, per_device(): lax.all_to_all(done, ('dp', 'mp'), split_axis=0, concat_axis=0, tiled=True)  34.5 us
    all_gather x2, waiting for transfers between devices, per_device(): full = lax.all_gather(rows, 'mp', axis=0, tiled=False)  28.2 us
    all_to_all x1, blocking collectives, per_device(): rows = lax.all_to_all(rows, 'dp', split_axis=0, concat_axis=0, tiled=True)  20.7 us
    all_to_all x1, waiting for transfers between devices, per_device(): rows = lax.all_to_all(rows, 'dp', split_axis=0, concat_axis=0, tiled=True)  15.9 us
    pallas_call x4, Pallas kernels, permute_in(): pl.pallas_call(body, out_shape=jax.ShapeDtypeStruct((users, size, width),...  15.6 us
    all_to_all x2, starting transfers between devices, per_device(): lax.all_to_all(done, ('dp', 'mp'), split_axis=0, concat_axis=0, tiled=True)  12.3 us
  transfers between devices with their start and end apart: 9, of which 5 were waited for; matrix products, arithmetic and copies ran while one was open for 3% of the time, Pallas kernels for 23%

profile of v2, /device:TPU:1, one launch (start us, length us, event | category | flops | bytes accessed | tf_op | source)
XLA Modules:
  0.0 287.2 jit_solution(8361783383685430880)
XLA Ops:
  6.5 0.7 all-gather.7.cloned.1.call-update
  7.3 0.7 pad_add_fusion
  7.9 0.6 broadcast_in_dim.304
  8.6 9.6 %all-to-all-start = ((s32[32,2,32]{2,1,0:T(2,128)}), s32[32,2,32]{2,1,0:T(2,128)S(1)}, u32[]{:S(2)}, u32[]{:S(2)}) async-start(s32[32,2,32]{2,1,0:T(2,128)} %broadcast_in_dim.304), calls=%async_computation | async-start | bytes 65536 | tf_op jit(solution)/shard_map/all_to_all | solution.py:235
  18.2 0.7 compare_select_fusion.3
  18.8 0.7 broadcast_compare_fusion
  19.5 0.7 gather_fusion
  20.2 0.7 and_select_fusion.1
  20.9 0.1 select_reduce_fusion.2.index_ref
  21.0 1.7 copy-done.2
  22.7 3.5 %shard_map.91 = bf16[32,64,256]{2,1,0:T(8,128)(2,1)} custom-call(s32[32]{0:T(128)S(1)} %select_reduce_fusion.2.index_ref, bf16[32,128,256]{2,1,0:T(8,128)(2,1)S(1)} %copy-done.2), custom_call_target="tpu_custom_call" | custom-call | tf_op jit(solution)/shard_map/pallas_call | solution.py:77
  26.3 7.4 %all-to-all-start.1 = ((bf16[32,64,256]{2,1,0:T(8,128)(2,1)}), bf16[32,64,256]{2,1,0:T(8,128)(2,1)S(1)}, u32[]{:S(2)}, u32[]{:S(2)}) async-start(bf16[32,64,256]{2,1,0:T(8,128)(2,1)} %shard_map.91), calls=%async_computation.1 | async-start | bytes 2097152 | tf_op jit(solution)/shard_map/all_to_all | solution.py:281
  33.9 0.1 select_reduce_fusion.4.order_ref
  34.1 0.1 select_reduce_fusion.3
  34.2 0.1 slice_reduce_fusion.1
  34.4 0.2 select_reduce_fusion
  34.7 15.9 %all-to-all-done.1.src = bf16[32,64,256]{2,1,0:T(8,128)(2,1)S(1)} async-done(((bf16[32,64,256]{2,1,0:T(8,128)(2,1)}), bf16[32,64,256]{2,1,0:T(8,128)(2,1)S(1)}, u32[]{:S(2)}, u32[]{:S(2)}) %all-to-all-start.1) | async-done | bytes 1048608 | tf_op jit(solution)/shard_map/all_to_all | solution.py:281
  50.6 4.0 %shard_map.92 = bf16[32,64,256]{2,1,0:T(8,128)(2,1)S(1)} custom-call(s32[32]{0:T(128)S(1)} %and_select_fusion.2.index_ref, bf16[32,64,256]{2,1,0:T(8,128)(2,1)S(1)} %all-to-all-done.1.src), custom_call_target="tpu_custom_call" | custom-call | tf_op jit(solution)/shard_map/pallas_call | solution.py:77
  54.6 20.9 %all_to_all.45 = bf16[32,64,256]{2,1,0:T(8,128)(2,1)} all-to-all(bf16[32,64,256]{2,1,0:T(8,128)(2,1)S(1)} %shard_map.92), channel_id=1, replica_groups=mesh['dp'=32,'mp'=4] {'dp'}, dimensions={0} | all-to-all | bytes 2097152 | tf_op jit(solution)/shard_map/all_to_all | solution.py:283
  75.6 4.0 %shard_map.95 = bf16[32,64,256]{2,1,0:T(8,128)(2,1)S(1)} custom-call(s32[32]{0:T(128)S(1)} %select_reduce_fusion.2.index_ref, bf16[32,128,256]{2,1,0:T(8,128)(2,1)S(1)} %copy-done.3), custom_call_target="tpu_custom_call" | custom-call | tf_op jit(solution)/shard_map/pallas_call | solution.py:77
  79.7 20.7 %all_to_all.46.src = bf16[32,64,256]{2,1,0:T(8,128)(2,1)S(1)} all-to-all(bf16[32,64,256]{2,1,0:T(8,128)(2,1)S(1)} %shard_map.95), channel_id=1, replica_groups=mesh['dp'=32,'mp'=4] {'dp'}, dimensions={0} | all-to-all | bytes 2097152 | tf_op jit(solution)/shard_map/all_to_all | solution.py:281
  100.3 4.0 %shard_map.96 = bf16[32,64,256]{2,1,0:T(8,128)(2,1)S(1)} custom-call(s32[32]{0:T(128)S(1)} %and_select_fusion.2.index_ref, bf16[32,64,256]{2,1,0:T(8,128)(2,1)S(1)} %all_to_all.46.src), custom_call_target="tpu_custom_call" | custom-call | tf_op jit(solution)/shard_map/pallas_call | solution.py:77
  104.4 20.9 %all_to_all.47 = bf16[32,64,256]{2,1,0:T(8,128)(2,1)} all-to-all(bf16[32,64,256]{2,1,0:T(8,128)(2,1)S(1)} %shard_map.96), channel_id=1, replica_groups=mesh['dp'=32,'mp'=4] {'dp'}, dimensions={0} | all-to-all | bytes 2097152 | tf_op jit(solution)/shard_map/all_to_all | solution.py:283
  125.3 0.7 gather_fusion.1
  126.0 0.4 slice_reduce_fusion.2
  126.5 0.5 fusion.18
  127.0 0.1 compare_select_fusion
  127.2 0.1 fusion.14
  127.3 0.5 select_multiply_fusion
  127.9 0.6 broadcast_in_dim.361
  128.6 0.7 broadcast_in_dim.363
  129.2 0.1 broadcast_in_dim.364
  129.4 0.3 stack.20.info_ref
  129.7 21.0 %shard_map.93 = bf16[4,32,16,256]{3,2,1,0:T(8,128)(2,1)} custom-call(s32[32]{0:T(128)S(1)} %select_reduce_fusion.4.order_ref, bf16[4,32,64,256]{3,2,1,0:T(8,128)(2,1)} %bitcast.26, bf16[1024,1024]{1,0:T(8,128)(2,1)S(1)} %copy-done.1, f32[32,8,256]{2,1,0:T(8,128)S(1)} %stack.20.info_ref, bf16[32,256,512]{2,1,0:T(8,128)(2,1)} %refs_7_.3, ...), custom_call_target="tpu_custom_call" | custom-call | tf_op jit(solution)/shard_map/pallas_call | solution.py:142
  150.8 4.0 %all-to-all-start.3 = ((bf16[4,32,16,256]{3,2,1,0:T(8,128)(2,1)}), bf16[4,32,16,256]{3,2,1,0:T(8,128)(2,1)S(1)}, u32[]{:S(2)}, u32[]{:S(2)}) async-start(bf16[4,32,16,256]{3,2,1,0:T(8,128)(2,1)} %shard_map.93), calls=%async_computation.3 | async-start | bytes 2097152 | tf_op jit(solution)/shard_map/all_to_all | solution.py:291
  154.8 28.2 %all-gather.11.cloned.1.call-done = bf16[128,64,256]{2,1,0:T(8,128)(2,1)} async-done(((bf16[32,64,256]{2,1,0:T(8,128)(2,1)}), bf16[128,64,256]{2,1,0:T(8,128)(2,1)}) %all-gather.11.cloned.1.call-update) | async-done | bytes 4194320 | tf_op jit(solution)/shard_map/all_gather | solution.py:289
  183.0 21.0 %shard_map.97 = bf16[4,32,16,256]{3,2,1,0:T(8,128)(2,1)} custom-call(s32[32]{0:T(128)S(1)} %select_reduce_fusion.4.order_ref, bf16[4,32,64,256]{3,2,1,0:T(8,128)(2,1)} %bitcast.28, bf16[1024,1024]{1,0:T(8,128)(2,1)S(1)} %copy-done.1, f32[32,8,256]{2,1,0:T(8,128)S(1)} %stack.20.info_ref, bf16[32,256,512]{2,1,0:T(8,128)(2,1)} %refs_7_.3, ...), custom_call_target="tpu_custom_call" | custom-call | tf_op jit(solution)/shard_map/pallas_call | solution.py:142
  204.0 4.4 %all-to-all-start.7 = ((bf16[4,32,16,256]{3,2,1,0:T(8,128)(2,1)}), bf16[4,32,16,256]{3,2,1,0:T(8,128)(2,1)}, u32[]{:S(2)}, u32[]{:S(2)}) async-start(bf16[4,32,16,256]{3,2,1,0:T(8,128)(2,1)} %shard_map.97), calls=%async_computation.7 | async-start | bytes 2097152 | tf_op jit(solution)/shard_map/all_to_all | solution.py:291
  208.5 4.0 %shard_map.94 = bf16[32,4,16,256]{3,2,1,0:T(8,128)(2,1)S(1)} custom-call(s32[33]{0:T(128)S(1)} %pad_add_fusion.1.scalar_ref, bf16[4,32,16,256]{3,2,1,0:T(8,128)(2,1)S(1)} %all-to-all-done.3.gated_ref, bf16[4,32,64,256]{3,2,1,0:T(8,128)(2,1)} %bitcast.27, bf16[4,256,1024]{2,1,0:T(8,128)(2,1)S(1)} %bitcast.20), custom_call_target="tpu_custom_call" | custom-call | tf_op jit(solution)/shard_map/pallas_call | solution.py:189
  212.5 1.0 copy-done.6
  213.5 9.5 %all-to-all-done.7.gated_ref = bf16[4,32,16,256]{3,2,1,0:T(8,128)(2,1)} async-done(((bf16[4,32,16,256]{3,2,1,0:T(8,128)(2,1)}), bf16[4,32,16,256]{3,2,1,0:T(8,128)(2,1)}, u32[]{:S(2)}, u32[]{:S(2)}) %all-to-all-start.7) | async-done | bytes 1048608 | tf_op jit(solution)/shard_map/all_to_all | solution.py:291
  223.0 8.6 %all-to-all-start.4 = ((bf16[128,16,256]{2,1,0:T(8,128)(2,1)}), bf16[128,16,256]{2,1,0:T(8,128)(2,1)S(1)}, u32[]{:S(2)}, u32[]{:S(2)}) async-start(bf16[128,16,256]{2,1,0:T(8,128)(2,1)} %bitcast.24), calls=%async_computation.4 | async-start | bytes 2097152 | tf_op jit(solution)/shard_map/all_to_all | solution.py:294
  231.6 4.1 %shard_map.98 = bf16[32,4,16,256]{3,2,1,0:T(8,128)(2,1)S(1)} custom-call(s32[33]{0:T(128)S(1)} %pad_add_fusion.1.scalar_ref, bf16[4,32,16,256]{3,2,1,0:T(8,128)(2,1)} %all-to-all-done.7.gated_ref, bf16[4,32,64,256]{3,2,1,0:T(8,128)(2,1)} %bitcast.29, bf16[4,256,1024]{2,1,0:T(8,128)(2,1)S(1)} %bitcast.21), custom_call_target="tpu_custom_call" | custom-call | tf_op jit(solution)/shard_map/pallas_call | solution.py:189
  235.7 1.0 copy-done.5
  236.7 14.7 %all-to-all-done.4 = bf16[128,16,256]{2,1,0:T(8,128)(2,1)S(1)} async-done(((bf16[128,16,256]{2,1,0:T(8,128)(2,1)}), bf16[128,16,256]{2,1,0:T(8,128)(2,1)S(1)}, u32[]{:S(2)}, u32[]{:S(2)}) %all-to-all-start.4) | async-done | bytes 1048608 | tf_op jit(solution)/shard_map/all_to_all | solution.py:294
  251.4 3.7 %all-to-all-start.8 = ((bf16[128,16,256]{2,1,0:T(8,128)(2,1)}), bf16[128,16,256]{2,1,0:T(8,128)(2,1)S(1)}, u32[]{:S(2)}, u32[]{:S(2)}) async-start(bf16[128,16,256]{2,1,0:T(8,128)(2,1)} %bitcast.23), calls=%async_computation.8 | async-start | bytes 2097152 | tf_op jit(solution)/shard_map/all_to_all | solution.py:294
  255.1 19.9 %all-to-all-done.8 = bf16[128,16,256]{2,1,0:T(8,128)(2,1)S(1)} async-done(((bf16[128,16,256]{2,1,0:T(8,128)(2,1)}), bf16[128,16,256]{2,1,0:T(8,128)(2,1)S(1)}, u32[]{:S(2)}, u32[]{:S(2)}) %all-to-all-start.8) | async-done | bytes 1048608 | tf_op jit(solution)/shard_map/all_to_all | solution.py:294
  274.9 5.7 %shard_map.99 = bf16[32,128,256]{2,1,0:T(8,128)(2,1)} custom-call(s32[32]{0:T(128)S(1)} %broadcast_subtract_fusion.index_ref, bf16[32,64,256]{2,1,0:T(8,128)(2,1)S(1)} %bitcast.22, bf16[32,64,256]{2,1,0:T(8,128)(2,1)S(1)} %bitcast.25), custom_call_target="tpu_custom_call" | custom-call | tf_op jit(solution)/shard_map/pallas_call | solution.py:44
  (39 shorter events, 0.7 us)
Async XLA Ops:
  6.5 118.8 %copy-start = (s32[32]{0:T(128)S(1)}, s32[32]{0:T(128)}, u32[]{:S(2)}) copy-start(s32[32]{0:T(128)} %param.14) | copy-start | bytes 388
  6.5 69.0 %all-gather.7.cloned.1.call-start = ((), (), s32[]{:S(2)}) async-start(), calls=%async_computation.9 | async-start | bytes 2621440 | tf_op jit(solution)/shard_map/all_gather | solution.py:244
  8.6 17.7 %all-to-all-start = ((s32[32,2,32]{2,1,0:T(2,128)}), s32[32,2,32]{2,1,0:T(2,128)S(1)}, u32[]{:S(2)}, u32[]{:S(2)}) async-start(s32[32,2,32]{2,1,0:T(2,128)} %broadcast_in_dim.304), calls=%async_computation | async-start | bytes 65536 | tf_op jit(solution)/shard_map/all_to_all | solution.py:235
  21.0 1.7 copy-start.2
  22.7 11.0 %copy-start.8 = (s32[1024]{0:T(1024)S(1)}, s32[1024]{0:T(1024)}, u32[]{:S(2)}) copy-start(s32[1024]{0:T(1024)} %param.12) | copy-start | bytes 12292
  26.3 24.3 %all-to-all-start.1 = ((bf16[32,64,256]{2,1,0:T(8,128)(2,1)}), bf16[32,64,256]{2,1,0:T(8,128)(2,1)S(1)}, u32[]{:S(2)}, u32[]{:S(2)}) async-start(bf16[32,64,256]{2,1,0:T(8,128)(2,1)} %shard_map.91), calls=%async_computation.1 | async-start | bytes 2097152 | tf_op jit(solution)/shard_map/all_to_all | solution.py:281
  33.7 96.1 %all-gather.9.cloned.1.call-start = ((), (), s32[]{:S(2)}) async-start(), calls=%async_computation.10 | async-start | bytes 5242880 | tf_op jit(solution)/shard_map/all_gather | solution.py:289
  54.6 21.0 %copy-start.3 = (bf16[32,128,256]{2,1,0:T(8,128)(2,1)S(1)}, bf16[32,128,256]{2,1,0:T(8,128)(2,1)}, u32[]{:S(2)}) copy-start(bf16[32,128,256]{2,1,0:T(8,128)(2,1)} %src.3) | copy-start | bytes 6291460
  75.5 107.4 %all-gather.11.cloned.1.call-start = ((), (), s32[]{:S(2)}) async-start(), calls=%async_computation.11 | async-start | bytes 5242880 | tf_op jit(solution)/shard_map/all_gather | solution.py:289
  104.4 21.7 %copy-start.7 = (f32[2,16]{1,0:T(2,128)S(1)}, f32[2,16]{1,0:T(2,128)}, u32[]{:S(2)}) copy-start(f32[2,16]{1,0:T(2,128)} %param.16) | copy-start | bytes 388
  104.4 25.4 %copy-start.1 = (bf16[1024,1024]{1,0:T(8,128)(2,1)S(1)}, bf16[1024,1024]{1,0:T(8,128)(2,1)}, u32[]{:S(2)}) copy-start(bf16[1024,1024]{1,0:T(8,128)(2,1)} %weight_ref.3) | copy-start | bytes 6291460
  150.8 53.2 %all-to-all-start.3 = ((bf16[4,32,16,256]{3,2,1,0:T(8,128)(2,1)}), bf16[4,32,16,256]{3,2,1,0:T(8,128)(2,1)S(1)}, u32[]{:S(2)}, u32[]{:S(2)}) async-start(bf16[4,32,16,256]{3,2,1,0:T(8,128)(2,1)} %shard_map.93), calls=%async_computation.3 | async-start | bytes 2097152 | tf_op jit(solution)/shard_map/all_to_all | solution.py:291
  204.0 4.5 %copy-start.4 = (bf16[1024,1024]{1,0:T(8,128)(2,1)S(1)}, bf16[1024,1024]{1,0:T(8,128)(2,1)}, u32[]{:S(2)}) copy-start(bf16[1024,1024]{1,0:T(8,128)(2,1)} %all-gather.7.cloned.1.call-done) | copy-start | bytes 6291460
  204.0 19.0 %all-to-all-start.7 = ((bf16[4,32,16,256]{3,2,1,0:T(8,128)(2,1)}), bf16[4,32,16,256]{3,2,1,0:T(8,128)(2,1)}, u32[]{:S(2)}, u32[]{:S(2)}) async-start(bf16[4,32,16,256]{3,2,1,0:T(8,128)(2,1)} %shard_map.97), calls=%async_computation.7 | async-start | bytes 2097152 | tf_op jit(solution)/shard_map/all_to_all | solution.py:291
  212.5 1.0 copy-start.6
  223.0 28.4 %all-to-all-start.4 = ((bf16[128,16,256]{2,1,0:T(8,128)(2,1)}), bf16[128,16,256]{2,1,0:T(8,128)(2,1)S(1)}, u32[]{:S(2)}, u32[]{:S(2)}) async-start(bf16[128,16,256]{2,1,0:T(8,128)(2,1)} %bitcast.24), calls=%async_computation.4 | async-start | bytes 2097152 | tf_op jit(solution)/shard_map/all_to_all | solution.py:294
  235.7 1.0 copy-start.5
  251.4 23.6 %all-to-all-start.8 = ((bf16[128,16,256]{2,1,0:T(8,128)(2,1)}), bf16[128,16,256]{2,1,0:T(8,128)(2,1)S(1)}, u32[]{:S(2)}, u32[]{:S(2)}) async-start(bf16[128,16,256]{2,1,0:T(8,128)(2,1)} %bitcast.23), calls=%async_computation.8 | async-start | bytes 2097152 | tf_op jit(solution)/shard_map/all_to_all | solution.py:294
Sparse Core Ops, SparseCore 0:
  9.0 34.0 all-gather.6
  75.7 45.7 all-gather.8
  125.4 57.5 all-gather.10

commit v3 on v1

v3 whole, which is shorter than its diff:
```python
import math

import jax
import jax.numpy as jnp
from jax import lax
from jax.experimental import pallas as pl
from jax.experimental.pallas import tpu as pltpu
from jax.sharding import PartitionSpec as P

HD = 128
EPSILON = 1e-05
VMEM = 48 * 1024 * 1024

PIECES = ((0, 64), (64, 64))
BATCH = 8
SIZE = 1088
GROUP = 16


def permute_out(index, part, piece, out_rows, whole=None):
    users, _, width = part.shape
    start, size = piece

    def body(index_ref, src, *refs):
        out, sem = refs[-2:]

        def store(i):
            return pltpu.make_async_copy(
                src.at[i], out.at[index_ref[i], pl.ds(start, size)], sem.at[i]
            )

        for i in range(users):
            store(i).start()
        for i in range(users):
            store(i).wait()

    extra = () if whole is None else (whole,)
    return pl.pallas_call(
        body,
        out_shape=jax.ShapeDtypeStruct((users, out_rows, width), part.dtype),
        in_specs=[
            pl.BlockSpec(memory_space=pltpu.SMEM),
            pl.BlockSpec(memory_space=pltpu.VMEM),
        ]
        + [pl.BlockSpec(memory_space=pl.ANY)] * len(extra),
        out_specs=pl.BlockSpec(memory_space=pl.ANY),
        scratch_shapes=[pltpu.SemaphoreType.DMA((users,))],
        input_output_aliases={2: 0} if extra else {},
        compiler_params=pltpu.CompilerParams(vmem_limit_bytes=VMEM),
    )(index, part, *extra)


def permute_in(index, whole, piece, tags=()):
    users, _, width = whole.shape
    start, size = piece
    rows = size + GROUP if tags else size

    def body(index_ref, *refs):
        src, out = refs[-2:]
        upper = lax.broadcasted_iota(jnp.int32, (GROUP, width), 0) < GROUP // 2
        for i in range(users):
            at = index_ref[i]
            out[i, :size, :] = src[at, start : start + size, :]
            if tags:
                tag = jnp.where(upper, refs[0][at], refs[1][at])
                out[i, size:, :] = tag.astype(jnp.float32).astype(whole.dtype)

    return pl.pallas_call(
        body,
        out_shape=jax.ShapeDtypeStruct((users, rows, width), whole.dtype),
        in_specs=[pl.BlockSpec(memory_space=pltpu.SMEM)] * (1 + len(tags))
        + [pl.BlockSpec(memory_space=pltpu.VMEM)],
        out_specs=pl.BlockSpec(memory_space=pltpu.VMEM),
        compiler_params=pltpu.CompilerParams(vmem_limit_bytes=VMEM),
    )(index, *tags, whole)


def attend_batch(projected, caches, infos, h, heads):
    inv_scale = 1.0 / math.sqrt(HD)
    batch = len(projected)
    rows = projected[0].shape[0]
    scores = [
        lax.dot_general(
            p[:, 2 * HD : 3 * HD],
            cache[0],
            (((1,), (1,)), ((), ())),
            preferred_element_type=jnp.float32,
        )
        for p, cache in zip(projected, caches)
    ]
    scores = [s * (0.5 * inv_scale) + info[h : h + 1, :] for s, info in zip(scores, infos)]
    weights = [
        ((s + s * jnp.tanh(s)) * info[2 * heads : 2 * heads + 1, :]).astype(jnp.bfloat16)
        for s, info in zip(scores, infos)
    ]
    summed = [
        jnp.dot(w, cache[1], preferred_element_type=jnp.float32)
        for w, cache in zip(weights, caches)
    ]
    whole = jnp.concatenate(projected, axis=0)
    gate, value, query, key = [
        whole[:, k * HD : (k + 1) * HD].astype(jnp.float32) for k in range(4)
    ]
    inverse = jnp.concatenate(
        [
            jnp.broadcast_to(info[2 * heads + 1 : 2 * heads + 2, :HD], (rows, HD))
            for info in infos
        ],
        axis=0,
    )
    own = jnp.sum(query * key, axis=-1, keepdims=True)
    own = own * (0.5 * inv_scale) + infos[0][heads + h : heads + h + 1, :HD]
    own = (own + own * jnp.tanh(own)) * inverse
    own = own.astype(jnp.bfloat16).astype(jnp.float32)
    combined = jnp.concatenate(summed, axis=0) + own * value
    head_mean = jnp.mean(combined, axis=-1, keepdims=True)
    centred = combined - head_mean
    head_var = jnp.mean(centred * centred, axis=-1, keepdims=True)
    return (centred * lax.rsqrt(head_var + EPSILON) * gate).astype(jnp.bfloat16)


def spread_quarters(whole_ref, out_refs, rows, rank):
    mp = len(out_refs)
    quarter = rows // mp
    for k in range(mp):
        at = ((rank + k) % mp) * quarter
        for b in range(BATCH):
            out_refs[k][b] = whole_ref[pl.ds(pl.multiple_of(b * rows + at, GROUP), quarter), :]


def normalise(parts):
    parts = [p.astype(jnp.float32) for p in parts]
    width = len(parts) * parts[0].shape[1]
    mean = sum(jnp.sum(p, axis=-1, keepdims=True) for p in parts) * (1.0 / width)
    parts = [p - mean for p in parts]
    var = sum(jnp.sum(p * p, axis=-1, keepdims=True) for p in parts) * (1.0 / width)
    factor = lax.rsqrt(var + EPSILON)
    return jnp.concatenate([(p * factor).astype(jnp.bfloat16) for p in parts], axis=1)


def silu_dot(normed, weight):
    half = 0.5 * jnp.dot(normed, weight, preferred_element_type=jnp.float32)
    return (half + half * jnp.tanh(half)).astype(jnp.bfloat16)


def head_cache(hist_ref, h):
    return (
        hist_ref[0, :, 2 * h * HD : (2 * h + 1) * HD],
        hist_ref[0, :, (2 * h + 1) * HD : (2 * h + 2) * HD],
    )


def attend(full, weight, history, order, rank, rows_info, heads):
    mp, users, rows, part = full.shape
    events, kv_width = history.shape[1:]
    quarter = rows // mp
    total = BATCH * rows

    def body(order_ref, rank_ref, full_ref, weight_ref, info_ref, *refs):
        hist_refs, out_refs, store = refs[:BATCH], refs[BATCH : BATCH + mp], refs[-1]
        normed = normalise([full_ref[k].reshape(total, part) for k in range(mp)])
        infos = [info_ref.at[b] for b in range(BATCH)]
        for h in range(heads):
            projected = silu_dot(normed, weight_ref[:, h * 4 * HD : (h + 1) * 4 * HD])
            store[:, h * HD : (h + 1) * HD] = attend_batch(
                [projected[b * rows : (b + 1) * rows] for b in range(BATCH)],
                [head_cache(hist_refs[b], h) for b in range(BATCH)],
                infos,
                h,
                heads,
            )
        spread_quarters(store, out_refs, rows, rank_ref[0])

    def hist_spec(b):
        return pl.BlockSpec((1, events, kv_width), lambda i, order, _: (order[i * BATCH + b], 0, 0))

    width = heads * HD
    return pl.pallas_call(
        body,
        out_shape=[jax.ShapeDtypeStruct((users, quarter, width), jnp.bfloat16)] * mp,
        grid_spec=pltpu.PrefetchScalarGridSpec(
            num_scalar_prefetch=2,
            grid=(users // BATCH,),
            in_specs=[
                pl.BlockSpec((mp, BATCH, rows, part), lambda i, *_: (0, i, 0, 0)),
                pl.BlockSpec(weight.shape, lambda i, *_: (0, 0)),
                pl.BlockSpec((BATCH,) + rows_info.shape[1:], lambda i, *_: (i, 0, 0)),
            ]
            + [hist_spec(b) for b in range(BATCH)],
            out_specs=[pl.BlockSpec((BATCH, quarter, width), lambda i, *_: (i, 0, 0))] * mp,
            scratch_shapes=[pltpu.VMEM((total, width), jnp.bfloat16)],
        ),
        compiler_params=pltpu.CompilerParams(vmem_limit_bytes=VMEM),
    )(order, rank, full, weight, rows_info, *([history] * BATCH))


def pack(slots, offsets, rows, size):
    users, count, width = rows.shape

    def body(slots_ref, offsets_ref, rows_ref, out, buffer, sem):
        for j in range(users):
            at = pl.multiple_of(offsets_ref[j], GROUP)
            buffer[pl.ds(at, count), :] = rows_ref[slots_ref[j]]
        copy = pltpu.make_async_copy(buffer.at[pl.ds(0, size)], out, sem)
        copy.start()
        copy.wait()

    return pl.pallas_call(
        body,
        out_shape=jax.ShapeDtypeStruct((size, width), rows.dtype),
        in_specs=[
            pl.BlockSpec(memory_space=pltpu.SMEM),
            pl.BlockSpec(memory_space=pltpu.SMEM),
            pl.BlockSpec(memory_space=pltpu.VMEM),
        ],
        out_specs=pl.BlockSpec(memory_space=pl.ANY),
        scratch_shapes=[
            pltpu.VMEM((size + count, width), rows.dtype),
            pltpu.SemaphoreType.DMA,
        ],
        compiler_params=pltpu.CompilerParams(vmem_limit_bytes=VMEM),
    )(slots, offsets, rows)


def attend_packed(
    full, weight, history, order, offsets, seats, last, rank, rows_info, rows, heads
):
    mp, size, part = full.shape
    users = order.shape[0]
    events, kv_width = history.shape[1:]
    quarter = rows // mp
    blocks = max(4, size // 256)
    block = size // blocks

    def body(
        order_ref, offsets_ref, seats_ref, last_ref, rank_ref, full_ref, weight_ref, info_ref, *refs
    ):
        hist_refs, out_refs = refs[:BATCH], refs[BATCH : BATCH + mp]
        store, merged = refs[-2:]
        step = pl.program_id(0)

        @pl.when(step < blocks)
        def _():
            normed = normalise([full_ref[k] for k in range(mp)])
            at = pl.multiple_of(step * block, GROUP)
            store[pl.ds(at, block), :] = silu_dot(normed, weight_ref[...])

        @pl.when((step >= blocks) & (step - blocks <= last_ref[0]))
        def _():
            seats = [(step - blocks) * BATCH + b for b in range(BATCH)]
            starts = [pl.multiple_of(offsets_ref[j], GROUP) for j in seats]
            infos = [info_ref.at[seats_ref[j]] for j in seats]
            for h in range(heads):
                merged[:, h * HD : (h + 1) * HD] = attend_batch(
                    [store[pl.ds(at, rows), h * 4 * HD : (h + 1) * 4 * HD] for at in starts],
                    [head_cache(hist_refs[b], h) for b in range(BATCH)],
                    infos,
                    h,
                    heads,
                )
            spread_quarters(merged, out_refs, rows, rank_ref[0])

    def batch_of(i):
        return jnp.maximum(i - blocks, 0)

    def hist_spec(b):
        return pl.BlockSpec(
            (1, events, kv_width),
            lambda i, order, offsets, seats, last, rank: (
                order[jnp.minimum(batch_of(i), last[0]) * BATCH + b],
                0,
                0,
            ),
        )

    width = heads * HD
    return pl.pallas_call(
        body,
        out_shape=[jax.ShapeDtypeStruct((users, quarter, width), jnp.bfloat16)] * mp,
        grid_spec=pltpu.PrefetchScalarGridSpec(
            num_scalar_prefetch=5,
            grid=(blocks + users // BATCH,),
            in_specs=[
                pl.BlockSpec(
                    (mp, block, part), lambda i, *_: (0, jnp.minimum(i, blocks - 1), 0)
                ),
                pl.BlockSpec(weight.shape, lambda i, *_: (0, 0)),
                pl.BlockSpec(rows_info.shape, lambda i, *_: (0, 0, 0)),
            ]
            + [hist_spec(b) for b in range(BATCH)],
            out_specs=[pl.BlockSpec((BATCH, quarter, width), lambda i, *_: (batch_of(i), 0, 0))]
            * mp,
            scratch_shapes=[
                pltpu.VMEM((size + rows, weight.shape[1]), jnp.bfloat16),
                pltpu.VMEM((BATCH * rows, width), jnp.bfloat16),
            ],
        ),
        compiler_params=pltpu.CompilerParams(vmem_limit_bytes=VMEM),
    )(order, offsets, seats, last, rank, full, weight, rows_info, *([history] * BATCH))


def rank_dot(gated, weights):
    terms = [
        jnp.dot(g, w, preferred_element_type=jnp.float32) for g, w in zip(gated, weights)
    ]
    return sum(terms[1:], terms[0])


def project_out(gated, full, weights, scalars, start):
    mp = len(gated)
    users, quarter, part = gated[0].shape
    out_part = weights[0].shape[1] // mp
    batch = 8

    def body(scalar_ref, full_ref, *refs):
        gated_refs, weight_refs, out_ref = refs[:mp], refs[mp : 2 * mp], refs[-1]
        first = pl.program_id(0) * batch
        acc = rank_dot(
            [g[...].reshape(batch * quarter, part) for g in gated_refs],
            [w[...] for w in weight_refs],
        )
        row = lax.broadcasted_iota(jnp.int32, (quarter, out_part), 0)
        row = row + (start + scalar_ref[0] * quarter)
        for b in range(batch):
            alive = row < scalar_ref[1 + first + b]
            for k in range(mp):
                mine = acc[b * quarter : (b + 1) * quarter, k * out_part : (k + 1) * out_part]
                mine = mine + full_ref[k, b].astype(jnp.float32)
                out_ref[b, k] = jnp.where(alive, mine, 0.0).astype(jnp.bfloat16)

    return pl.pallas_call(
        body,
        out_shape=jax.ShapeDtypeStruct((users, mp, quarter, out_part), jnp.bfloat16),
        grid_spec=pltpu.PrefetchScalarGridSpec(
            num_scalar_prefetch=1,
            grid=(users // batch,),
            in_specs=[pl.BlockSpec((mp, batch, quarter, part), lambda i, s: (0, i, s[0], 0))]
            + [pl.BlockSpec((batch, quarter, part), lambda i, s: (i, 0, 0)) for _ in gated]
            + [pl.BlockSpec(w.shape, lambda i, s: (0, 0)) for w in weights],
            out_specs=pl.BlockSpec((batch, mp, quarter, out_part), lambda i, s: (i, 0, 0, 0)),
        ),
        compiler_params=pltpu.CompilerParams(vmem_limit_bytes=VMEM),
    )(scalars, full, *gated, *weights)


def project_out_packed(gated, full, weights, scalars, slots, offsets, start):
    mp = len(gated)
    users, quarter, part = gated[0].shape
    size = full.shape[1]
    out_part = weights[0].shape[1] // mp

    def body(scalar_ref, slots_ref, offsets_ref, full_ref, *refs):
        gated_refs, weight_refs, out_ref = refs[:mp], refs[mp : 2 * mp], refs[-1]
        rank = scalar_ref[0]
        acc = rank_dot(
            [g[...].reshape(users * quarter, part) for g in gated_refs],
            [w[...] for w in weight_refs],
        )
        row = lax.broadcasted_iota(jnp.int32, (quarter, out_part), 0) + (start + rank * quarter)
        for j in range(users):
            at = jnp.minimum(offsets_ref[j] + rank * quarter, size - quarter)
            residual = full_ref[0, pl.ds(pl.multiple_of(at, GROUP), quarter), :]
            mine = acc[j * quarter : (j + 1) * quarter] + residual.astype(jnp.float32)
            alive = row < scalar_ref[1 + j]
            out_ref[slots_ref[j], 0] = jnp.where(alive, mine, 0.0).astype(jnp.bfloat16)

    return pl.pallas_call(
        body,
        out_shape=jax.ShapeDtypeStruct((users, mp, quarter, out_part), jnp.bfloat16),
        grid_spec=pltpu.PrefetchScalarGridSpec(
            num_scalar_prefetch=3,
            grid=(mp,),
            in_specs=[pl.BlockSpec((1, size, part), lambda i, *_: (i, 0, 0))]
            + [pl.BlockSpec((users, quarter, part), lambda i, *_: (0, 0, 0)) for _ in gated]
            + [pl.BlockSpec((part, out_part), lambda i, *_: (0, i)) for _ in weights],
            out_specs=pl.BlockSpec((users, 1, quarter, out_part), lambda i, *_: (0, i, 0, 0)),
        ),
        compiler_params=pltpu.CompilerParams(vmem_limit_bytes=VMEM),
    )(scalars, slots, offsets, full, *gated, *weights)


def bucket_bias(distance, time_bias):
    bias = jnp.broadcast_to(time_bias[:, 0][:, None, None], time_bias.shape[:1] + distance.shape)
    for k in range(time_bias.shape[1] - 1):
        bias = jnp.where((distance >= 2**k)[None], time_bias[:, k + 1][:, None, None], bias)
    return bias


def per_device(
    candidates,
    live_counts,
    request_user,
    score_slot,
    history_cache,
    history_length,
    input_weight,
    time_bias,
    output_weight,
):
    dp_size = lax.axis_size("dp")
    dp_rank = lax.axis_index("dp")
    mp_rank = lax.axis_index("mp")
    users, slots, part = candidates.shape
    events = history_cache.shape[1]
    heads = time_bias.shape[0]
    ranks = jnp.arange(dp_size, dtype=jnp.int32)
    local = jnp.arange(users, dtype=jnp.int32)
    scorer = score_slot // users

    target = jnp.take(scorer, request_user)
    send_first = jnp.sum(jnp.where(target[None, :] == ranks[:, None], local[None, :], 0), axis=1)
    def exchange(rows):
        return lax.all_to_all(rows, "dp", split_axis=0, concat_axis=0, tiled=True)

    mp_size = lax.axis_size("mp")

    def shifted(array, k):
        return lax.ppermute(array, "mp", [(i, (i + k) % mp_size) for i in range(mp_size)])

    first_rows, second_rows = PIECES[0][1], PIECES[1][1]
    weights_out = [output_weight] + [shifted(output_weight, k) for k in range(1, mp_size)]
    rows_0 = permute_in(send_first, candidates, PIECES[0], (request_user // users, live_counts))
    scored_0 = exchange(rows_0)
    owner_rank = scored_0[:, first_rows, 0].astype(jnp.int32)
    send_second = jnp.sum(
        jnp.where(owner_rank[None, :] == ranks[:, None], ranks[None, :], 0), axis=1
    )
    tagged_0 = exchange(permute_in(send_second, scored_0, (0, first_rows + GROUP)))
    owned_0 = tagged_0[:, :first_rows]
    live = tagged_0[:, first_rows + GROUP // 2, 0].astype(jnp.int32)

    scored_here = scorer.reshape(dp_size, users) == dp_rank
    place = jnp.sum(
        jnp.where(scored_here, score_slot.reshape(dp_size, users), 0), axis=1
    ) - dp_rank * users
    own_scorer = lax.dynamic_slice_in_dim(scorer, dp_rank * users, users)
    order = jnp.sum(jnp.where(own_scorer[None, :] == ranks[:, None], local[None, :], 0), axis=1)
    scalars = jnp.concatenate([mp_rank[None], live]).astype(jnp.int32)

    lengths = jnp.take(history_length, order)
    position = jnp.arange(events, dtype=jnp.int32)
    distance = lengths[:, None] - position[None, :]
    inverse = 1.0 / (lengths + 1).astype(jnp.float32)
    spread = jnp.broadcast_to(inverse[:, None], (users, events))
    bias = 0.5 * bucket_bias(distance, time_bias)
    own_bias = jnp.broadcast_to(0.5 * time_bias[:, 0][:, None, None], bias.shape)
    info = [bias[h] for h in range(heads)] + [own_bias[h] for h in range(heads)]
    info = info + [jnp.where(distance > 0, spread, 0.0), spread]
    info = info + [jnp.zeros_like(spread)] * (-len(info) % 8)
    rows_info = jnp.stack(info, axis=1)

    def padded(count):
        return (jnp.maximum(count - first_rows, 0) + (GROUP - 1)) // GROUP * GROUP

    groups = padded(live)
    has = groups > 0
    earlier = local[None, :] < local[:, None]
    count = jnp.sum(has.astype(jnp.int32))
    seat = jnp.where(
        has,
        jnp.sum((earlier & has[None, :]).astype(jnp.int32), axis=1),
        count + jnp.sum((earlier & ~has[None, :]).astype(jnp.int32), axis=1),
    )
    seated = seat[None, :] == local[:, None]

    def by_seat(values):
        return jnp.sum(jnp.where(seated, values[None, :], 0), axis=1).astype(jnp.int32)

    seat_slots = by_seat(local)
    seat_order = by_seat(order)
    seat_scalars = jnp.concatenate([mp_rank[None], by_seat(live)]).astype(jnp.int32)
    seat_offsets = jnp.sum(
        jnp.where(seat[None, :] < local[:, None], groups[None, :], 0), axis=1
    ).astype(jnp.int32)
    seat_offsets = jnp.minimum(seat_offsets, SIZE)
    rank = mp_rank[None].astype(jnp.int32)
    seat_last = (jnp.maximum(count - 1, 0) // BATCH)[None].astype(jnp.int32)

    def gather(rows):
        return lax.all_gather(rows, "mp", axis=0, tiled=False)

    def by_quarter(gated):
        return [gated[0]] + [shifted(gated[k], k) for k in range(1, mp_size)]

    def finish(done, size):
        done = done.reshape((-1,) + done.shape[2:])
        done = lax.all_to_all(done, ("dp", "mp"), split_axis=0, concat_axis=0, tiled=True)
        return done.reshape(users, size, part)

    def whole_piece(full, info, start):
        gated = attend(full, input_weight, history_cache, order, rank, info, heads)
        done = project_out(by_quarter(gated), full, weights_out, scalars, start)
        return finish(done, full.shape[2])

    rows_1 = permute_in(send_first, candidates, PIECES[1])
    rows_1, owned_0, rows_info, *weights_out = lax.optimization_barrier(
        (rows_1, owned_0, rows_info, *weights_out)
    )
    full_0 = gather(owned_0)
    owned_1 = exchange(permute_in(send_second, exchange(rows_1), (0, second_rows)))
    owned_1, full_0, groups = lax.optimization_barrier((owned_1, full_0, groups))
    packed = pack(seat_slots, seat_offsets, owned_1, SIZE)
    full_1 = gather(packed)
    own_most = jnp.broadcast_to(jnp.sum(groups).astype(jnp.int32)[None, None], (dp_size, 1))
    most = jnp.max(exchange(own_most))
    result_0 = whole_piece(full_0, rows_info, PIECES[0][0])
    gated_1 = attend_packed(
        full_1,
        input_weight,
        history_cache,
        seat_order,
        seat_offsets,
        seat_slots,
        seat_last,
        rank,
        rows_info,
        second_rows,
        heads,
    )
    done_1 = project_out_packed(
        by_quarter(gated_1),
        full_1,
        weights_out,
        seat_scalars,
        seat_slots,
        seat_offsets,
        PIECES[1][0],
    )
    result_1 = finish(done_1, second_rows)
    result_1 = lax.cond(
        most > SIZE,
        lambda ready, rows: whole_piece(gather(rows), rows_info, PIECES[1][0]),
        lambda ready, rows: ready,
        result_1,
        owned_1,
    )
    out = permute_out(place, result_0, PIECES[0], slots)
    return permute_out(place, result_1, PIECES[1], slots, out)


def solution(mesh):
    in_specs = (
        P("dp", None, "mp"),
        P("dp"),
        P("dp"),
        P(),
        P("dp", None, "mp"),
        P("dp"),
        P(None, "mp"),
        P("mp", None),
        P("mp", None),
    )
    out_specs = P("dp", None, "mp")
    return jax.shard_map(
        per_device, mesh=mesh, in_specs=in_specs, out_specs=out_specs, check_vma=False
    )
```

time: 487 us -> 251 us (0.52)
  Pallas kernels: 227 us -> 48 us
  blocking collectives: 76.2 us -> 0 us
  starting transfers between devices: 21.8 us -> 64.3 us
  waiting for transfers between devices: 134 us -> 99.4 us
  local copies, waits for them, and re-layouts: 8.18 us -> 14.6 us
    pallas_call x3 -> x8, Pallas kernels: 156 us -> 38.2 us  [the longest x1 14.7 us: attend(): pl.pallas_call(body, out_shape=[jax.ShapeDtypeStruct((users, quarter, wid...]
    all_gather x2, waiting for transfers between devices: 81.1 us -> 2.45 us  [gather(): return lax.all_gather(rows, 'mp', axis=0, tiled=False)]
    pallas_call x1 -> x2, Pallas kernels: 65.6 us -> 4.23 us  [permute_out(): pl.pallas_call(body, out_shape=jax.ShapeDtypeStruct((users, out_rows, wid...]
    all_gather x1 -> x0, blocking collectives: 43.4 us -> none  [per_device(): lax.all_gather(jnp.stack([request_user, live_counts]), 'dp', axis=0, tile...]
    all_to_all x1 -> x0, blocking collectives: 32.8 us -> none  [per_device(): rows = lax.all_to_all(rows, 'dp', split_axis=0, concat_axis=0, tiled=True)]
    all_to_all x3 -> x7, starting transfers between devices: 21.7 us -> 50.9 us  [the longest x5 30.7 us: exchange(): return lax.all_to_all(rows, 'dp', split_axis=0, concat_axis=0, tiled=True)]
    all_to_all x3 -> x7, waiting for transfers between devices: 52.2 us -> 75.5 us  [the longest x5 59.3 us: exchange(): return lax.all_to_all(rows, 'dp', split_axis=0, concat_axis=0, tiled=True)]
    ppermute x0 -> x9, waiting for transfers between devices: none -> 21.4 us  [shifted(): lax.ppermute(array, 'mp', [(i, (i + k) % mp_size) for i in range(mp_size)])]
  transfers between devices with their start and end apart: 5 -> 18, of which waited for: 4 -> 10; matrix products, arithmetic and copies ran while one was open for 1% -> 5% of each run, Pallas kernels for 5% -> 17%
where the time goes in v3:
time: 251 us; the launch traced here: 250 us
  waiting for transfers between devices  99.4 us (40%)
  starting transfers between devices  64.3 us (26%)
  Pallas kernels  48 us (19%)
  between operations  15 us (6%)
  local copies, waits for them, and re-layouts  14.6 us (6%)
  other arithmetic  8.92 us (4%)
    all_to_all x5, waiting for transfers between devices, exchange(): return lax.all_to_all(rows, 'dp', split_axis=0, concat_axis=0, tiled=True)  59.3 us
    all_to_all x5, starting transfers between devices, exchange(): return lax.all_to_all(rows, 'dp', split_axis=0, concat_axis=0, tiled=True)  30.7 us
    ppermute x9, waiting for transfers between devices, shifted(): lax.ppermute(array, 'mp', [(i, (i + k) % mp_size) for i in range(mp_size)])  21.4 us
    all_to_all x2, starting transfers between devices, finish(): lax.all_to_all(done, ('dp', 'mp'), split_axis=0, concat_axis=0, tiled=True)  20.2 us
    all_to_all x2, waiting for transfers between devices, finish(): lax.all_to_all(done, ('dp', 'mp'), split_axis=0, concat_axis=0, tiled=True)  16.1 us
    pallas_call x1, Pallas kernels, attend(): pl.pallas_call(body, out_shape=[jax.ShapeDtypeStruct((users, quarter, wid...  14.7 us
    ppermute x9, starting transfers between devices, shifted(): lax.ppermute(array, 'mp', [(i, (i + k) % mp_size) for i in range(mp_size)])  13.2 us
    pallas_call x1, Pallas kernels, attend_packed(): pl.pallas_call(body, out_shape=[jax.ShapeDtypeStruct((users, quarter, wid...  11.5 us
  transfers between devices with their start and end apart: 18, of which 10 were waited for; matrix products, arithmetic and copies ran while one was open for 5% of the time, Pallas kernels for 17%

profile of v3, /device:TPU:1, one launch (start us, length us, event | category | flops | bytes accessed | tf_op | source)
XLA Modules:
  0.0 250.1 jit_solution(14029872817384482019)
XLA Ops:
  6.5 0.7 compare_select_fusion.7
  7.2 0.7 add_select_fusion
  7.9 0.7 gather_fusion
  8.6 0.7 and_select_fusion.2
  9.4 1.6 copy-done.5
  11.6 1.7 shard_map.91
  13.3 9.6 %all-to-all-start.1 = ((bf16[32,80,256]{2,1,0:T(8,128)(2,1)}), bf16[32,80,256]{2,1,0:T(8,128)(2,1)S(1)}, u32[]{:S(2)}, u32[]{:S(2)}) async-start(bf16[32,80,256]{2,1,0:T(8,128)(2,1)} %shard_map.91), calls=%async_computation.1 | async-start | bytes 2621440 | tf_op jit(solution)/shard_map/all_to_all | solution.py:413
  22.9 1.3 collective-permute-start.3
  24.2 2.5 collective-permute-start.4
  26.6 1.2 collective-permute-start.5
  28.0 0.7 gather_fusion.1
  28.7 14.0 %all-to-all-done.1.refs_0_ = bf16[32,80,256]{2,1,0:T(8,128)(2,1)S(1)} async-done(((bf16[32,80,256]{2,1,0:T(8,128)(2,1)}), bf16[32,80,256]{2,1,0:T(8,128)(2,1)S(1)}, u32[]{:S(2)}, u32[]{:S(2)}) %all-to-all-start.1) | async-done | bytes 1310752 | tf_op jit(solution)/shard_map/all_to_all | solution.py:413
  44.2 1.0 copy-done.7
  45.2 4.7 %all-to-all-start.2 = ((bf16[32,80,256]{2,1,0:T(8,128)(2,1)}), bf16[32,80,256]{2,1,0:T(8,128)(2,1)}, u32[]{:S(2)}, u32[]{:S(2)}) async-start(bf16[32,80,256]{2,1,0:T(8,128)(2,1)} %copy-done.7), calls=%async_computation.2 | async-start | bytes 2621440 | tf_op jit(solution)/shard_map/all_to_all | solution.py:413
  50.0 1.6 shard_map.92
  55.2 14.6 %all-to-all-done.2 = bf16[32,80,256]{2,1,0:T(8,128)(2,1)} async-done(((bf16[32,80,256]{2,1,0:T(8,128)(2,1)}), bf16[32,80,256]{2,1,0:T(8,128)(2,1)}, u32[]{:S(2)}, u32[]{:S(2)}) %all-to-all-start.2) | async-done | bytes 1310752 | tf_op jit(solution)/shard_map/all_to_all | solution.py:413
  69.8 2.3 slice.104
  72.2 4.0 %all-to-all-start.3 = ((bf16[32,64,256]{2,1,0:T(8,128)(2,1)}), bf16[32,64,256]{2,1,0:T(8,128)(2,1)S(1)}, u32[]{:S(2)}, u32[]{:S(2)}) async-start(bf16[32,64,256]{2,1,0:T(8,128)(2,1)} %shard_map.92), calls=%async_computation.3 | async-start | bytes 2097152 | tf_op jit(solution)/shard_map/all_to_all | solution.py:413
  76.2 1.5 fusion.15
  77.7 15.5 %all-to-all-done.3.refs_0_ = bf16[32,64,256]{2,1,0:T(8,128)(2,1)S(1)} async-done(((bf16[32,64,256]{2,1,0:T(8,128)(2,1)}), bf16[32,64,256]{2,1,0:T(8,128)(2,1)S(1)}, u32[]{:S(2)}, u32[]{:S(2)}) %all-to-all-start.3) | async-done | bytes 1048608 | tf_op jit(solution)/shard_map/all_to_all | solution.py:413
  93.2 1.6 shard_map.94
  94.8 3.9 %all-to-all-start.4 = ((bf16[32,64,256]{2,1,0:T(8,128)(2,1)}), bf16[32,64,256]{2,1,0:T(8,128)(2,1)S(1)}, u32[]{:S(2)}, u32[]{:S(2)}) async-start(bf16[32,64,256]{2,1,0:T(8,128)(2,1)} %shard_map.94), calls=%async_computation.4 | async-start | bytes 2097152 | tf_op jit(solution)/shard_map/all_to_all | solution.py:413
  100.3 15.3 %all-to-all-done.4.rows_ref = bf16[32,64,256]{2,1,0:T(8,128)(2,1)S(1)} async-done(((bf16[32,64,256]{2,1,0:T(8,128)(2,1)}), bf16[32,64,256]{2,1,0:T(8,128)(2,1)S(1)}, u32[]{:S(2)}, u32[]{:S(2)}) %all-to-all-start.4) | async-done | bytes 1048608 | tf_op jit(solution)/shard_map/all_to_all | solution.py:413
  115.6 2.4 all-gather.9.cloned.1.call-done
  118.1 1.4 shard_map.95
  119.5 2.2 copy-done.1
  121.7 14.7 %shard_map.98 = (bf16[32,16,256]{2,1,0:T(8,128)(2,1)S(1)}, bf16[32,16,256]{2,1,0:T(8,128)(2,1)S(1)}, bf16[32,16,256]{2,1,0:T(8,128)(2,1)S(1)}, bf16[32,16,256]{2,1,0:T(8,128)(2,1)S(1)}) custom-call(s32[32]{0:T(128)S(1)} %select_reduce_fusion.4.order_ref, s32[1]{0:T(128)} %bitcast.9.rank_ref, bf16[4,32,64,256]{3,2,1,0:T(8,128)(2,1)S(1)} %bitcast.21, ...), custom_call_target="tpu_custom_call" | custom-call | tf_op jit(solution)/shard_map/pallas_call | solution.py:178
  136.4 1.9 collective-permute-start.10
  138.3 1.2 collective-permute-start.11
  140.4 1.2 broadcast_in_dim.391
  141.7 8.5 %all-to-all-start.5 = ((s32[32,1,1]{2,1,0:T(1,128)}), s32[32,1,1]{2,1,0:T(1,128)S(1)}, u32[]{:S(2)}, u32[]{:S(2)}) async-start(s32[32,1,1]{2,1,0:T(1,128)} %broadcast_in_dim.391), calls=%async_computation.5 | async-start | bytes 32768 | tf_op jit(solution)/shard_map/all_to_all | solution.py:413
  150.2 1.3 collective-permute-done.10.refs_2_
  151.5 9.5 %collective-permute-done.11.refs_3_ = bf16[32,16,256]{2,1,0:T(8,128)(2,1)S(1)} collective-permute-done((bf16[32,16,256]{2,1,0:T(8,128)(2,1)S(1)}, bf16[32,16,256]{2,1,0:T(8,128)(2,1)S(1)}, u32[]{:S(2)}, u32[]{:S(2)}) %collective-permute-start.11) | collective-permute-done | bytes 262176 | tf_op jit(solution)/shard_map/ppermute | solution.py:418
  161.0 5.5 %shard_map.99 = bf16[32,4,16,256]{3,2,1,0:T(8,128)(2,1)} custom-call(s32[33]{0:T(128)S(1)} %pad_add_fusion.1.scalar_ref, bf16[4,32,64,256]{3,2,1,0:T(8,128)(2,1)} %bitcast.20, bf16[32,16,256]{2,1,0:T(8,128)(2,1)S(1)} %get-tuple-element.84.refs_0_, bf16[32,16,256]{2,1,0:T(8,128)(2,1)S(1)} %collective-permute-done.9.refs_1_, ...), custom_call_target="tpu_custom_call" | custom-call | tf_op jit(solution)/shard_map/pallas_call | solution.py:331
  166.5 10.2 %all-to-all-start.7 = ((bf16[128,16,256]{2,1,0:T(8,128)(2,1)}), bf16[128,16,256]{2,1,0:T(8,128)(2,1)S(1)}, u32[]{:S(2)}, u32[]{:S(2)}) async-start(bf16[128,16,256]{2,1,0:T(8,128)(2,1)} %bitcast.14), calls=%async_computation.7 | async-start | bytes 2097152 | tf_op jit(solution)/shard_map/all_to_all | solution.py:487
  177.3 1.6 copy-done.3
  179.0 11.5 %shard_map.96 = (bf16[32,16,256]{2,1,0:T(8,128)(2,1)S(1)}, bf16[32,16,256]{2,1,0:T(8,128)(2,1)S(1)}, bf16[32,16,256]{2,1,0:T(8,128)(2,1)S(1)}, bf16[32,16,256]{2,1,0:T(8,128)(2,1)S(1)}) custom-call(s32[32]{0:T(128)S(1)} %get-tuple-element.106.order_ref, s32[32]{0:T(128)S(1)} %broadcast_minimum_fusion.offsets_ref, ...), custom_call_target="tpu_custom_call" | custom-call | tf_op jit(solution)/shard_map/pallas_call | solution.py:277
  190.5 1.5 collective-permute-start.6
  191.9 2.4 collective-permute-start.7
  194.3 1.2 collective-permute-start.8
  195.6 4.2 %collective-permute-done.6.refs_1_ = bf16[32,16,256]{2,1,0:T(8,128)(2,1)S(1)} collective-permute-done((bf16[32,16,256]{2,1,0:T(8,128)(2,1)S(1)}, bf16[32,16,256]{2,1,0:T(8,128)(2,1)S(1)}, u32[]{:S(2)}, u32[]{:S(2)}) %collective-permute-start.6) | collective-permute-done | bytes 262176 | tf_op jit(solution)/shard_map/ppermute | solution.py:418
  199.8 6.4 %collective-permute-done.7.refs_2_ = bf16[32,16,256]{2,1,0:T(8,128)(2,1)S(1)} collective-permute-done((bf16[32,16,256]{2,1,0:T(8,128)(2,1)S(1)}, bf16[32,16,256]{2,1,0:T(8,128)(2,1)S(1)}, u32[]{:S(2)}, u32[]{:S(2)}) %collective-permute-start.7) | collective-permute-done | bytes 262176 | tf_op jit(solution)/shard_map/ppermute | solution.py:418
  206.2 5.1 %shard_map.97 = bf16[32,4,16,256]{3,2,1,0:T(8,128)(2,1)} custom-call(s32[33]{0:T(128)S(1)} %pad_add_fusion.scalar_ref, s32[32]{0:T(128)S(1)} %get-tuple-element.108.slots_ref.seats_ref, s32[32]{0:T(128)S(1)} %broadcast_minimum_fusion.offsets_ref, bf16[4,1088,256]{2,1,0:T(8,128)(2,1)S(1)} %bitcast.25, bf16[32,16,256]{2,1,0:T(8,128)(2,1)S(1)} %get-tuple-element.75.refs_0_, ...), custom_call_target="tpu_custom_call" | custom-call | tf_op jit(solution)/shard_map/pallas_call | solution.py:367
  211.3 10.0 %all-to-all-start.6 = ((bf16[128,16,256]{2,1,0:T(8,128)(2,1)}), bf16[128,16,256]{2,1,0:T(8,128)(2,1)}, u32[]{:S(2)}, u32[]{:S(2)}) async-start(bf16[128,16,256]{2,1,0:T(8,128)(2,1)} %bitcast.12), calls=%async_computation.6 | async-start | bytes 2097152 | tf_op jit(solution)/shard_map/all_to_all | solution.py:487
  221.5 0.7 reduce_max.9
  222.9 1.8 shard_map.100.refs_0_
  224.6 16.1 %all-to-all-done.6 = bf16[128,16,256]{2,1,0:T(8,128)(2,1)} async-done(((bf16[128,16,256]{2,1,0:T(8,128)(2,1)}), bf16[128,16,256]{2,1,0:T(8,128)(2,1)}, u32[]{:S(2)}, u32[]{:S(2)}) %all-to-all-start.6) | async-done | bytes 1048608 | tf_op jit(solution)/shard_map/all_to_all | solution.py:487
  240.7 2.5 shard_map.101
  (65 shorter events, 9.0 us)
Async XLA Ops:
  6.5 21.5 %copy-start = (s32[32]{0:T(128)S(1)}, s32[32]{0:T(128)}, u32[]{:S(2)}) copy-start(s32[32]{0:T(128)} %param.16) | copy-start | bytes 388
  9.4 1.6 copy-start.5
  11.0 0.7 copy-start.8
  13.3 29.4 %all-to-all-start.1 = ((bf16[32,80,256]{2,1,0:T(8,128)(2,1)}), bf16[32,80,256]{2,1,0:T(8,128)(2,1)S(1)}, u32[]{:S(2)}, u32[]{:S(2)}) async-start(bf16[32,80,256]{2,1,0:T(8,128)(2,1)} %shard_map.91), calls=%async_computation.1 | async-start | bytes 2621440 | tf_op jit(solution)/shard_map/all_to_all | solution.py:413
  22.9 49.2 %collective-permute-start.3 = (bf16[256,1024]{1,0:T(8,128)(2,1)}, bf16[256,1024]{1,0:T(8,128)(2,1)}, u32[]{:S(2)}, u32[]{:S(2)}) collective-permute-start(bf16[256,1024]{1,0:T(8,128)(2,1)} %refs_4_.5), channel_id=1, source_target_pairs={{0,1},{1,2},{2,3},{3,0},{4,5},{5,6},{6,7},{7,4},{8,9},{9,10},{10,1... | collective-permute-start | bytes 1572872 | tf_op jit(solution)/shard_map/ppermute | solution.py:418
  24.2 48.0 %collective-permute-start.4 = (bf16[256,1024]{1,0:T(8,128)(2,1)}, bf16[256,1024]{1,0:T(8,128)(2,1)}, u32[]{:S(2)}, u32[]{:S(2)}) collective-permute-start(bf16[256,1024]{1,0:T(8,128)(2,1)} %refs_4_.5), channel_id=1, source_target_pairs={{0,2},{1,3},{2,0},{3,1},{4,6},{5,7},{6,4},{7,5},{8,10},{9,11},{10,... | collective-permute-start | bytes 1572872 | tf_op jit(solution)/shard_map/ppermute | solution.py:418
  26.6 45.5 %collective-permute-start.5 = (bf16[256,1024]{1,0:T(8,128)(2,1)}, bf16[256,1024]{1,0:T(8,128)(2,1)}, u32[]{:S(2)}, u32[]{:S(2)}) collective-permute-start(bf16[256,1024]{1,0:T(8,128)(2,1)} %refs_4_.5), channel_id=1, source_target_pairs={{0,3},{1,0},{2,1},{3,2},{4,7},{5,4},{6,5},{7,6},{8,11},{9,8},{10,9... | collective-permute-start | bytes 1572872 | tf_op jit(solution)/shard_map/ppermute | solution.py:418
  43.5 6.5 %copy-start.6 = (bf16[32,128,256]{2,1,0:T(8,128)(2,1)S(1)}, bf16[32,128,256]{2,1,0:T(8,128)(2,1)}, u32[]{:S(2)}) copy-start(bf16[32,128,256]{2,1,0:T(8,128)(2,1)} %refs_0_.3) | copy-start | bytes 6291460
  44.1 1.1 copy-start.7
  45.2 24.6 %all-to-all-start.2 = ((bf16[32,80,256]{2,1,0:T(8,128)(2,1)}), bf16[32,80,256]{2,1,0:T(8,128)(2,1)}, u32[]{:S(2)}, u32[]{:S(2)}) async-start(bf16[32,80,256]{2,1,0:T(8,128)(2,1)} %copy-done.7), calls=%async_computation.2 | async-start | bytes 2621440 | tf_op jit(solution)/shard_map/all_to_all | solution.py:413
  49.9 1.7 copy-start.11
  49.9 68.2 %all-gather.9.cloned.1.call-start = ((), (), s32[]{:S(2)}) async-start(), calls=%async_computation.9 | async-start | bytes 5242880 | tf_op jit(solution)/shard_map/all_gather | solution.py:480
  72.2 21.0 %all-to-all-start.3 = ((bf16[32,64,256]{2,1,0:T(8,128)(2,1)}), bf16[32,64,256]{2,1,0:T(8,128)(2,1)S(1)}, u32[]{:S(2)}, u32[]{:S(2)}) async-start(bf16[32,64,256]{2,1,0:T(8,128)(2,1)} %shard_map.92), calls=%async_computation.3 | async-start | bytes 2097152 | tf_op jit(solution)/shard_map/all_to_all | solution.py:413
  94.8 20.9 %all-to-all-start.4 = ((bf16[32,64,256]{2,1,0:T(8,128)(2,1)}), bf16[32,64,256]{2,1,0:T(8,128)(2,1)S(1)}, u32[]{:S(2)}, u32[]{:S(2)}) async-start(bf16[32,64,256]{2,1,0:T(8,128)(2,1)} %shard_map.94), calls=%async_computation.4 | async-start | bytes 2097152 | tf_op jit(solution)/shard_map/all_to_all | solution.py:413
  98.7 78.6 %all-gather.11.cloned.1.call-start = ((), (), s32[]{:S(2)}) async-start(), calls=%async_computation.10 | async-start | bytes 2785280 | tf_op jit(solution)/shard_map/all_gather | solution.py:480
  115.6 3.9 %copy-start.10 = (bf16[32,64,256]{2,1,0:T(8,128)(2,1)}, bf16[32,64,256]{2,1,0:T(8,128)(2,1)S(1)}, u32[]{:S(2)}) copy-start(bf16[32,64,256]{2,1,0:T(8,128)(2,1)S(1)} %all-to-all-done.4.rows_ref) | copy-start | bytes 3145732
  119.5 2.2 copy-start.1
  136.4 15.1 %collective-permute-start.10 = (bf16[32,16,256]{2,1,0:T(8,128)(2,1)S(1)}, bf16[32,16,256]{2,1,0:T(8,128)(2,1)S(1)}, u32[]{:S(2)}, u32[]{:S(2)}) collective-permute-start(bf16[32,16,256]{2,1,0:T(8,128)(2,1)S(1)} %get-tuple-element.86), channel_id=1, source_target_pairs={{0,2},{1,3},{2,0},{3,1},{4,6},{5,7},{6,4},{7,5},{8,10},{9,11},{10,... | collective-permute-start | bytes 786440 | tf_op jit(solution)/shard_map/ppermute | solution.py:418
  138.3 22.8 %collective-permute-start.11 = (bf16[32,16,256]{2,1,0:T(8,128)(2,1)S(1)}, bf16[32,16,256]{2,1,0:T(8,128)(2,1)S(1)}, u32[]{:S(2)}, u32[]{:S(2)}) collective-permute-start(bf16[32,16,256]{2,1,0:T(8,128)(2,1)S(1)} %get-tuple-element.87), channel_id=1, source_target_pairs={{0,3},{1,0},{2,1},{3,2},{4,7},{5,4},{6,5},{7,6},{8,11},{9,8},{10,9... | collective-permute-start | bytes 786440 | tf_op jit(solution)/shard_map/ppermute | solution.py:418
  139.4 21.6 %collective-permute-start.9 = (bf16[32,16,256]{2,1,0:T(8,128)(2,1)S(1)}, bf16[32,16,256]{2,1,0:T(8,128)(2,1)S(1)}, u32[]{:S(2)}, u32[]{:S(2)}) collective-permute-start(bf16[32,16,256]{2,1,0:T(8,128)(2,1)S(1)} %get-tuple-element.85), channel_id=1, source_target_pairs={{0,1},{1,2},{2,3},{3,0},{4,5},{5,6},{6,7},{7,4},{8,9},{9,10},{10,1... | collective-permute-start | bytes 786440 | tf_op jit(solution)/shard_map/ppermute | solution.py:418
  141.7 24.9 %all-to-all-start.5 = ((s32[32,1,1]{2,1,0:T(1,128)}), s32[32,1,1]{2,1,0:T(1,128)S(1)}, u32[]{:S(2)}, u32[]{:S(2)}) async-start(s32[32,1,1]{2,1,0:T(1,128)} %broadcast_in_dim.391), calls=%async_computation.5 | async-start | bytes 32768 | tf_op jit(solution)/shard_map/all_to_all | solution.py:413
  166.5 10.8 %copy-start.9 = (bf16[1024,1024]{1,0:T(8,128)(2,1)S(1)}, bf16[1024,1024]{1,0:T(8,128)(2,1)}, u32[]{:S(2)}) copy-start(bf16[1024,1024]{1,0:T(8,128)(2,1)} %weight_ref.3) | copy-start | bytes 6291460
  166.5 44.8 %all-to-all-start.7 = ((bf16[128,16,256]{2,1,0:T(8,128)(2,1)}), bf16[128,16,256]{2,1,0:T(8,128)(2,1)S(1)}, u32[]{:S(2)}, u32[]{:S(2)}) async-start(bf16[128,16,256]{2,1,0:T(8,128)(2,1)} %bitcast.14), calls=%async_computation.7 | async-start | bytes 2097152 | tf_op jit(solution)/shard_map/all_to_all | solution.py:487
  177.3 1.6 copy-start.3
  179.0 27.3 %copy-start.4 = (bf16[4352,256]{1,0:T(8,128)(2,1)S(1)}, bf16[4352,256]{1,0:T(8,128)(2,1)}, u32[]{:S(2)}) copy-start(bf16[4352,256]{1,0:T(8,128)(2,1)} %all-gather.11.cloned.1.call-done) | copy-start | bytes 6684676
  190.5 9.3 %collective-permute-start.6 = (bf16[32,16,256]{2,1,0:T(8,128)(2,1)S(1)}, bf16[32,16,256]{2,1,0:T(8,128)(2,1)S(1)}, u32[]{:S(2)}, u32[]{:S(2)}) collective-permute-start(bf16[32,16,256]{2,1,0:T(8,128)(2,1)S(1)} %get-tuple-element.76), channel_id=1, source_target_pairs={{0,1},{1,2},{2,3},{3,0},{4,5},{5,6},{6,7},{7,4},{8,9},{9,10},{10,1... | collective-permute-start | bytes 786440 | tf_op jit(solution)/shard_map/ppermute | solution.py:418
  191.9 14.3 %collective-permute-start.7 = (bf16[32,16,256]{2,1,0:T(8,128)(2,1)S(1)}, bf16[32,16,256]{2,1,0:T(8,128)(2,1)S(1)}, u32[]{:S(2)}, u32[]{:S(2)}) collective-permute-start(bf16[32,16,256]{2,1,0:T(8,128)(2,1)S(1)} %get-tuple-element.77), channel_id=1, source_target_pairs={{0,2},{1,3},{2,0},{3,1},{4,6},{5,7},{6,4},{7,5},{8,10},{9,11},{10,... | collective-permute-start | bytes 786440 | tf_op jit(solution)/shard_map/ppermute | solution.py:418
  194.3 11.9 %collective-permute-start.8 = (bf16[32,16,256]{2,1,0:T(8,128)(2,1)S(1)}, bf16[32,16,256]{2,1,0:T(8,128)(2,1)S(1)}, u32[]{:S(2)}, u32[]{:S(2)}) collective-permute-start(bf16[32,16,256]{2,1,0:T(8,128)(2,1)S(1)} %get-tuple-element.78), channel_id=1, source_target_pairs={{0,3},{1,0},{2,1},{3,2},{4,7},{5,4},{6,5},{7,6},{8,11},{9,8},{10,9... | collective-permute-start | bytes 786440 | tf_op jit(solution)/shard_map/ppermute | solution.py:418
  211.3 29.4 %all-to-all-start.6 = ((bf16[128,16,256]{2,1,0:T(8,128)(2,1)}), bf16[128,16,256]{2,1,0:T(8,128)(2,1)}, u32[]{:S(2)}, u32[]{:S(2)}) async-start(bf16[128,16,256]{2,1,0:T(8,128)(2,1)} %bitcast.12), calls=%async_computation.6 | async-start | bytes 2097152 | tf_op jit(solution)/shard_map/all_to_all | solution.py:487
Sparse Core Ops, SparseCore 0:
  72.3 45.6 all-gather.8
  119.7 43.4 all-gather.10

commit v4 on v3

--- a/solution.py
+++ b/solution.py
@@ -17,37 +17,37 @@
 GROUP = 16
 
 
-def permute_out(index, part, piece, out_rows, whole=None):
-    users, _, width = part.shape
-    start, size = piece
-
-    def body(index_ref, src, *refs):
-        out, sem = refs[-2:]
-
+def permute_out(index, results):
+    users, mp, pieces, quarter, width = results.shape
+    rows = pieces * mp * quarter
+
+    def body(index_ref, src, out, buffer, sem):
         def store(i):
-            return pltpu.make_async_copy(
-                src.at[i], out.at[index_ref[i], pl.ds(start, size)], sem.at[i]
-            )
+            return pltpu.make_async_copy(buffer.at[i], out.at[index_ref[i]], sem.at[i])
 
         for i in range(users):
+            for n in range(pieces):
+                for q in range(mp):
+                    at = (n * mp + q) * quarter
+                    buffer[i, at : at + quarter, :] = src[i, q, n]
             store(i).start()
         for i in range(users):
             store(i).wait()
 
-    extra = () if whole is None else (whole,)
-    return pl.pallas_call(
-        body,
-        out_shape=jax.ShapeDtypeStruct((users, out_rows, width), part.dtype),
+    return pl.pallas_call(
+        body,
+        out_shape=jax.ShapeDtypeStruct((users, rows, width), results.dtype),
         in_specs=[
             pl.BlockSpec(memory_space=pltpu.SMEM),
             pl.BlockSpec(memory_space=pltpu.VMEM),
-        ]
-        + [pl.BlockSpec(memory_space=pl.ANY)] * len(extra),
+        ],
         out_specs=pl.BlockSpec(memory_space=pl.ANY),
-        scratch_shapes=[pltpu.SemaphoreType.DMA((users,))],
-        input_output_aliases={2: 0} if extra else {},
-        compiler_params=pltpu.CompilerParams(vmem_limit_bytes=VMEM),
-    )(index, part, *extra)
+        scratch_shapes=[
+            pltpu.VMEM((users, rows, width), results.dtype),
+            pltpu.SemaphoreType.DMA((users,)),
+        ],
+        compiler_params=pltpu.CompilerParams(vmem_limit_bytes=VMEM),
+    )(index, results)
 
 
 def permute_in(index, whole, piece, tags=()):
@@ -73,6 +73,22 @@
         out_specs=pl.BlockSpec(memory_space=pltpu.VMEM),
         compiler_params=pltpu.CompilerParams(vmem_limit_bytes=VMEM),
     )(index, *tags, whole)
+
+
+def trim(rows, size):
+    users, _, width = rows.shape
+
+    def body(src, out):
+        for i in range(users):
+            out[i] = src[i, :size, :]
+
+    return pl.pallas_call(
+        body,
+        out_shape=jax.ShapeDtypeStruct((users, size, width), rows.dtype),
+        in_specs=[pl.BlockSpec(memory_space=pltpu.VMEM)],
+        out_specs=pl.BlockSpec(memory_space=pltpu.VMEM),
+        compiler_params=pltpu.CompilerParams(vmem_limit_bytes=VMEM),
+    )(rows)
 
 
 def attend_batch(projected, caches, infos, h, heads):
@@ -150,14 +166,16 @@
     )
 
 
-def attend(full, weight, history, order, rank, rows_info, heads):
+def attend(full, weight, history, order, rank, rows_info, heads, first, some, before=None):
     mp, users, rows, part = full.shape
     events, kv_width = history.shape[1:]
     quarter = rows // mp
     total = BATCH * rows
+    width = heads * HD
+    skip = first // BATCH
 
     def body(order_ref, rank_ref, full_ref, weight_ref, info_ref, *refs):
-        hist_refs, out_refs, store = refs[:BATCH], refs[BATCH : BATCH + mp], refs[-1]
+        hist_refs, out_refs, store = refs[:BATCH], refs[-1 - mp : -1], refs[-1]
         normed = normalise([full_ref[k].reshape(total, part) for k in range(mp)])
         infos = [info_ref.at[b] for b in range(BATCH)]
         for h in range(heads):
@@ -172,52 +190,55 @@
         spread_quarters(store, out_refs, rows, rank_ref[0])
 
     def hist_spec(b):
-        return pl.BlockSpec((1, events, kv_width), lambda i, order, _: (order[i * BATCH + b], 0, 0))
-
-    width = heads * HD
+        return pl.BlockSpec(
+            (1, events, kv_width), lambda i, order, _: (order[(skip + i) * BATCH + b], 0, 0)
+        )
+
+    extra = () if before is None else tuple(before)
+    inputs = (order, rank, full, weight, rows_info, *([history] * BATCH), *extra)
+    at = len(inputs) - len(extra)
     return pl.pallas_call(
         body,
         out_shape=[jax.ShapeDtypeStruct((users, quarter, width), jnp.bfloat16)] * mp,
         grid_spec=pltpu.PrefetchScalarGridSpec(
             num_scalar_prefetch=2,
-            grid=(users // BATCH,),
+            grid=(some // BATCH,),
             in_specs=[
-                pl.BlockSpec((mp, BATCH, rows, part), lambda i, *_: (0, i, 0, 0)),
+                pl.BlockSpec((mp, BATCH, rows, part), lambda i, *_: (0, skip + i, 0, 0)),
                 pl.BlockSpec(weight.shape, lambda i, *_: (0, 0)),
-                pl.BlockSpec((BATCH,) + rows_info.shape[1:], lambda i, *_: (i, 0, 0)),
+                pl.BlockSpec((BATCH,) + rows_info.shape[1:], lambda i, *_: (skip + i, 0, 0)),
             ]
-            + [hist_spec(b) for b in range(BATCH)],
-            out_specs=[pl.BlockSpec((BATCH, quarter, width), lambda i, *_: (i, 0, 0))] * mp,
+            + [hist_spec(b) for b in range(BATCH)]
+            + [pl.BlockSpec(memory_space=pl.ANY) for _ in extra],
+            out_specs=[pl.BlockSpec((BATCH, quarter, width), lambda i, *_: (skip + i, 0, 0))] * mp,
             scratch_shapes=[pltpu.VMEM((total, width), jnp.bfloat16)],
         ),
-        compiler_params=pltpu.CompilerParams(vmem_limit_bytes=VMEM),
-    )(order, rank, full, weight, rows_info, *([history] * BATCH))
+        input_output_aliases={at + k: k for k in range(len(extra))},
+        compiler_params=pltpu.CompilerParams(vmem_limit_bytes=VMEM),
+    )(*inputs)
 
 
 def pack(slots, offsets, rows, size):
     users, count, width = rows.shape
-
-    def body(slots_ref, offsets_ref, rows_ref, out, buffer, sem):
+    half = size // 2
+
+    def body(slots_ref, offsets_ref, rows_ref, low, high, buffer):
         for j in range(users):
             at = pl.multiple_of(offsets_ref[j], GROUP)
             buffer[pl.ds(at, count), :] = rows_ref[slots_ref[j]]
-        copy = pltpu.make_async_copy(buffer.at[pl.ds(0, size)], out, sem)
-        copy.start()
-        copy.wait()
-
-    return pl.pallas_call(
-        body,
-        out_shape=jax.ShapeDtypeStruct((size, width), rows.dtype),
+        low[...] = buffer[:half, :]
+        high[...] = buffer[half:size, :]
+
+    return pl.pallas_call(
+        body,
+        out_shape=[jax.ShapeDtypeStruct((half, width), rows.dtype)] * 2,
         in_specs=[
             pl.BlockSpec(memory_space=pltpu.SMEM),
             pl.BlockSpec(memory_space=pltpu.SMEM),
             pl.BlockSpec(memory_space=pltpu.VMEM),
         ],
-        out_specs=pl.BlockSpec(memory_space=pl.ANY),
-        scratch_shapes=[
-            pltpu.VMEM((size + count, width), rows.dtype),
-            pltpu.SemaphoreType.DMA,
-        ],
+        out_specs=[pl.BlockSpec(memory_space=pltpu.VMEM)] * 2,
+        scratch_shapes=[pltpu.VMEM((size + count, width), rows.dtype)],
         compiler_params=pltpu.CompilerParams(vmem_limit_bytes=VMEM),
     )(slots, offsets, rows)
 
@@ -225,23 +246,36 @@
 def attend_packed(
     full, weight, history, order, offsets, seats, last, rank, rows_info, rows, heads
 ):
-    mp, size, part = full.shape
+    mp = len(full)
+    part = full[0][0].shape[1]
+    size = sum(array.shape[0] for array in full[0])
     users = order.shape[0]
     events, kv_width = history.shape[1:]
     quarter = rows // mp
-    blocks = max(4, size // 256)
+    blocks = 4
     block = size // blocks
+    count = sum(len(arrays) for arrays in full)
 
     def body(
-        order_ref, offsets_ref, seats_ref, last_ref, rank_ref, full_ref, weight_ref, info_ref, *refs
+        order_ref, offsets_ref, seats_ref, last_ref, rank_ref, *refs
     ):
-        hist_refs, out_refs = refs[:BATCH], refs[BATCH : BATCH + mp]
+        weight_ref, info_ref = refs[count], refs[count + 1]
+        hist_refs = refs[count + 2 : count + 2 + BATCH]
+        out_refs = refs[count + 2 + BATCH : count + 2 + BATCH + mp]
         store, merged = refs[-2:]
         step = pl.program_id(0)
 
         @pl.when(step < blocks)
         def _():
-            normed = normalise([full_ref[k] for k in range(mp)])
+            parts, at = [], 0
+            for arrays in full:
+                block_rows = refs[at][...]
+                if len(arrays) > 1:
+                    low = step < arrays[0].shape[0] // block
+                    block_rows = jnp.where(low, block_rows, refs[at + 1][...])
+                parts.append(block_rows)
+                at = at + len(arrays)
+            normed = normalise(parts)
             at = pl.multiple_of(step * block, GROUP)
             store[pl.ds(at, block), :] = silu_dot(normed, weight_ref[...])
 
@@ -260,6 +294,10 @@
                 )
             spread_quarters(merged, out_refs, rows, rank_ref[0])
 
+    def full_spec(array, n):
+        steps = array.shape[0] // block
+        return pl.BlockSpec((block, part), lambda i, *_: (jnp.clip(i - n * steps, 0, steps - 1), 0))
+
     def batch_of(i):
         return jnp.maximum(i - blocks, 0)
 
@@ -280,10 +318,8 @@
         grid_spec=pltpu.PrefetchScalarGridSpec(
             num_scalar_prefetch=5,
             grid=(blocks + users // BATCH,),
-            in_specs=[
-                pl.BlockSpec(
-                    (mp, block, part), lambda i, *_: (0, jnp.minimum(i, blocks - 1), 0)
-                ),
+            in_specs=[full_spec(array, n) for arrays in full for n, array in enumerate(arrays)]
+            + [
                 pl.BlockSpec(weight.shape, lambda i, *_: (0, 0)),
                 pl.BlockSpec(rows_info.shape, lambda i, *_: (0, 0, 0)),
             ]
@@ -296,7 +332,7 @@
             ],
         ),
         compiler_params=pltpu.CompilerParams(vmem_limit_bytes=VMEM),
-    )(order, offsets, seats, last, rank, full, weight, rows_info, *([history] * BATCH))
+    )(order, offsets, seats, last, rank, *sum(full, []), weight, rows_info, *([history] * BATCH))
 
 
 def rank_dot(gated, weights):
@@ -306,11 +342,13 @@
     return sum(terms[1:], terms[0])
 
 
-def project_out(gated, full, weights, scalars, start):
+def project_out(gated, full, weights, scalars, piece, before=None):
     mp = len(gated)
     users, quarter, part = gated[0].shape
     out_part = weights[0].shape[1] // mp
     batch = 8
+    start = PIECES[piece][0]
+    extra = () if before is None else (before,)
 
     def body(scalar_ref, full_ref, *refs):
         gated_refs, weight_refs, out_ref = refs[:mp], refs[mp : 2 * mp], refs[-1]
@@ -326,32 +364,53 @@
             for k in range(mp):
                 mine = acc[b * quarter : (b + 1) * quarter, k * out_part : (k + 1) * out_part]
                 mine = mine + full_ref[k, b].astype(jnp.float32)
-                out_ref[b, k] = jnp.where(alive, mine, 0.0).astype(jnp.bfloat16)
-
-    return pl.pallas_call(
-        body,
-        out_shape=jax.ShapeDtypeStruct((users, mp, quarter, out_part), jnp.bfloat16),
+                out_ref[b, k, 0] = jnp.where(alive, mine, 0.0).astype(jnp.bfloat16)
+
+    return pl.pallas_call(
+        body,
+        out_shape=jax.ShapeDtypeStruct((users, mp, len(PIECES), quarter, out_part), jnp.bfloat16),
         grid_spec=pltpu.PrefetchScalarGridSpec(
             num_scalar_prefetch=1,
             grid=(users // batch,),
             in_specs=[pl.BlockSpec((mp, batch, quarter, part), lambda i, s: (0, i, s[0], 0))]
             + [pl.BlockSpec((batch, quarter, part), lambda i, s: (i, 0, 0)) for _ in gated]
-            + [pl.BlockSpec(w.shape, lambda i, s: (0, 0)) for w in weights],
-            out_specs=pl.BlockSpec((batch, mp, quarter, out_part), lambda i, s: (i, 0, 0, 0)),
+            + [pl.BlockSpec(w.shape, lambda i, s: (0, 0)) for w in weights]
+            + [pl.BlockSpec(memory_space=pl.ANY) for _ in extra],
+            out_specs=pl.BlockSpec(
+                (batch, mp, 1, quarter, out_part), lambda i, s: (i, 0, piece, 0, 0)
+            ),
         ),
-        compiler_params=pltpu.CompilerParams(vmem_limit_bytes=VMEM),
-    )(scalars, full, *gated, *weights)
-
-
-def project_out_packed(gated, full, weights, scalars, slots, offsets, start):
+        input_output_aliases={2 + 2 * mp: 0} if extra else {},
+        compiler_params=pltpu.CompilerParams(vmem_limit_bytes=VMEM),
+    )(scalars, full, *gated, *weights, *extra)
+
+
+def project_out_packed(gated, full, weights, scalars, slots, offsets, piece, before):
     mp = len(gated)
     users, quarter, part = gated[0].shape
-    size = full.shape[1]
+    size = sum(array.shape[0] for array in full[0])
     out_part = weights[0].shape[1] // mp
-
-    def body(scalar_ref, slots_ref, offsets_ref, full_ref, *refs):
-        gated_refs, weight_refs, out_ref = refs[:mp], refs[mp : 2 * mp], refs[-1]
+    start = PIECES[piece][0]
+    count = sum(len(arrays) for arrays in full)
+
+    def column_of(k, rank):
+        return (rank + (mp - k)) % mp
+
+    def body(scalar_ref, slots_ref, offsets_ref, *refs):
+        gated_refs, weight_refs = refs[count : count + mp], refs[count + mp : count + 2 * mp]
+        out_ref, whole = refs[-2], refs[-1]
         rank = scalar_ref[0]
+        first = 0
+        for k, arrays in enumerate(full):
+
+            @pl.when(pl.program_id(0) == k)
+            def _():
+                at = 0
+                for n, array in enumerate(arrays):
+                    whole[at : at + array.shape[0], :] = refs[first + n][...]
+                    at = at + array.shape[0]
+
+            first = first + len(arrays)
         acc = rank_dot(
             [g[...].reshape(users * quarter, part) for g in gated_refs],
             [w[...] for w in weight_refs],
@@ -359,24 +418,35 @@
         row = lax.broadcasted_iota(jnp.int32, (quarter, out_part), 0) + (start + rank * quarter)
         for j in range(users):
             at = jnp.minimum(offsets_ref[j] + rank * quarter, size - quarter)
-            residual = full_ref[0, pl.ds(pl.multiple_of(at, GROUP), quarter), :]
+            residual = whole[pl.ds(pl.multiple_of(at, GROUP), quarter), :]
             mine = acc[j * quarter : (j + 1) * quarter] + residual.astype(jnp.float32)
             alive = row < scalar_ref[1 + j]
-            out_ref[slots_ref[j], 0] = jnp.where(alive, mine, 0.0).astype(jnp.bfloat16)
-
-    return pl.pallas_call(
-        body,
-        out_shape=jax.ShapeDtypeStruct((users, mp, quarter, out_part), jnp.bfloat16),
+            out_ref[slots_ref[j], 0, 0] = jnp.where(alive, mine, 0.0).astype(jnp.bfloat16)
+
+    return pl.pallas_call(
+        body,
+        out_shape=jax.ShapeDtypeStruct((users, mp, len(PIECES), quarter, out_part), jnp.bfloat16),
         grid_spec=pltpu.PrefetchScalarGridSpec(
             num_scalar_prefetch=3,
             grid=(mp,),
-            in_specs=[pl.BlockSpec((1, size, part), lambda i, *_: (i, 0, 0))]
+            in_specs=[
+                pl.BlockSpec(array.shape, lambda i, *_: (0, 0)) for arrays in full for array in arrays
+            ]
             + [pl.BlockSpec((users, quarter, part), lambda i, *_: (0, 0, 0)) for _ in gated]
-            + [pl.BlockSpec((part, out_part), lambda i, *_: (0, i)) for _ in weights],
-            out_specs=pl.BlockSpec((users, 1, quarter, out_part), lambda i, *_: (0, i, 0, 0)),
+            + [
+                pl.BlockSpec((part, out_part), lambda i, s, *_: (0, column_of(i, s[0])))
+                for _ in weights
+            ]
+            + [pl.BlockSpec(memory_space=pl.ANY)],
+            out_specs=pl.BlockSpec(
+                (users, 1, 1, quarter, out_part),
+                lambda i, s, *_: (0, column_of(i, s[0]), piece, 0, 0),
+            ),
+            scratch_shapes=[pltpu.VMEM((size, part), jnp.bfloat16)],
         ),
-        compiler_params=pltpu.CompilerParams(vmem_limit_bytes=VMEM),
-    )(scalars, slots, offsets, full, *gated, *weights)
+        input_output_aliases={3 + count + 2 * mp: 0},
+        compiler_params=pltpu.CompilerParams(vmem_limit_bytes=VMEM),
+    )(scalars, slots, offsets, *sum(full, []), *gated, *weights, before)
 
 
 def bucket_bias(distance, time_bias):
@@ -426,7 +496,7 @@
         jnp.where(owner_rank[None, :] == ranks[:, None], ranks[None, :], 0), axis=1
     )
     tagged_0 = exchange(permute_in(send_second, scored_0, (0, first_rows + GROUP)))
-    owned_0 = tagged_0[:, :first_rows]
+    owned_0 = trim(tagged_0, first_rows)
     live = tagged_0[:, first_rows + GROUP // 2, 0].astype(jnp.int32)
 
     scored_here = scorer.reshape(dp_size, users) == dp_rank
@@ -479,34 +549,40 @@
     def gather(rows):
         return lax.all_gather(rows, "mp", axis=0, tiled=False)
 
+    turned = (mp_rank + (mp_size - jnp.arange(mp_size, dtype=jnp.int32))) % mp_size
+    weight_in = jnp.take(input_weight.reshape(mp_size, part, -1), turned, axis=0)
+    weight_in = weight_in.reshape(input_weight.shape)
+
     def by_quarter(gated):
         return [gated[0]] + [shifted(gated[k], k) for k in range(1, mp_size)]
 
-    def finish(done, size):
-        done = done.reshape((-1,) + done.shape[2:])
-        done = lax.all_to_all(done, ("dp", "mp"), split_axis=0, concat_axis=0, tiled=True)
-        return done.reshape(users, size, part)
-
-    def whole_piece(full, info, start):
-        gated = attend(full, input_weight, history_cache, order, rank, info, heads)
-        done = project_out(by_quarter(gated), full, weights_out, scalars, start)
-        return finish(done, full.shape[2])
-
     rows_1 = permute_in(send_first, candidates, PIECES[1])
-    rows_1, owned_0, rows_info, *weights_out = lax.optimization_barrier(
-        (rows_1, owned_0, rows_info, *weights_out)
+    rows_1, owned_0, rows_info, weight_in, *weights_out = lax.optimization_barrier(
+        (rows_1, owned_0, rows_info, weight_in, *weights_out)
     )
     full_0 = gather(owned_0)
     owned_1 = exchange(permute_in(send_second, exchange(rows_1), (0, second_rows)))
-    owned_1, full_0, groups = lax.optimization_barrier((owned_1, full_0, groups))
+    owned_1, groups = lax.optimization_barrier((owned_1, groups))
     packed = pack(seat_slots, seat_offsets, owned_1, SIZE)
-    full_1 = gather(packed)
-    own_most = jnp.broadcast_to(jnp.sum(groups).astype(jnp.int32)[None, None], (dp_size, 1))
-    most = jnp.max(exchange(own_most))
-    result_0 = whole_piece(full_0, rows_info, PIECES[0][0])
+    (low, high), full_0 = lax.optimization_barrier((packed, full_0))
+
+    low_1, high_3 = shifted(low, 1), shifted(high, 3)
+    high_1, low_3 = shifted(high, 1), shifted(low, 3)
+    half = users // 2
+
+    def attend_some(full, first, some, before=None):
+        return attend(
+            full, input_weight, history_cache, order, rank, rows_info, heads, first, some, before
+        )
+
+    gated_0 = attend_some(full_0, 0, half)
+    low_1, high_3, gated_0 = lax.optimization_barrier((low_1, high_3, gated_0))
+    low_2, high_2 = shifted(low_1, 1), shifted(high_3, 3)
+    gated_0 = attend_some(full_0, half, users - half, gated_0)
+    full_1 = [[low, high], [low_1, high_1], [low_2, high_2], [low_3, high_3]]
     gated_1 = attend_packed(
         full_1,
-        input_weight,
+        weight_in,
         history_cache,
         seat_order,
         seat_offsets,
@@ -517,25 +593,31 @@
         second_rows,
         heads,
     )
-    done_1 = project_out_packed(
+    done_0 = project_out(by_quarter(gated_0), full_0, weights_out, scalars, 0)
+    done = project_out_packed(
         by_quarter(gated_1),
         full_1,
         weights_out,
         seat_scalars,
         seat_slots,
         seat_offsets,
-        PIECES[1][0],
-    )
-    result_1 = finish(done_1, second_rows)
-    result_1 = lax.cond(
-        most > SIZE,
-        lambda ready, rows: whole_piece(gather(rows), rows_info, PIECES[1][0]),
-        lambda ready, rows: ready,
-        result_1,
-        owned_1,
-    )
-    out = permute_out(place, result_0, PIECES[0], slots)
-    return permute_out(place, result_1, PIECES[1], slots, out)
+        1,
+        done_0,
+    )
+
+    def unpacked(done, rows):
+        by_shift = jnp.stack([rows] + [shifted(rows, k) for k in range(1, mp_size)])
+        full = jnp.take(by_shift, turned, axis=0)
+        gated = by_quarter(attend_some(full, 0, users))
+        return project_out(gated, full, weights_out, scalars, 1, done)
+
+    done = lax.cond(
+        jnp.sum(groups) > SIZE, unpacked, lambda done, rows: done, done, owned_1
+    )
+    results = lax.all_to_all(
+        done.reshape((-1,) + done.shape[2:]), ("dp", "mp"), split_axis=0, concat_axis=0, tiled=True
+    )
+    return permute_out(place, results.reshape(done.shape))
 
 
 def solution(mesh):

time: 251 us -> 234 us (0.932)
  waiting for transfers between devices: 99.4 us -> 84.9 us
  starting transfers between devices: 64.3 us -> 51.1 us
  local copies, waits for them, and re-layouts: 14.6 us -> 22.6 us
    ppermute x9 -> x15, waiting for transfers between devices: 21.4 us -> 0.04 us  [shifted(): lax.ppermute(array, 'mp', [(i, (i + k) % mp_size) for i in range(mp_size)])]
    all_to_all x2 -> x1, waiting for transfers between devices: 16.1 us -> 30.8 us  [per_device(): lax.all_to_all(done.reshape((-1,) + done.shape[2:]), ('dp', 'mp'), split_...]
    all_to_all x2 -> x1, starting transfers between devices: 20.2 us -> 8.73 us  [per_device(): lax.all_to_all(done.reshape((-1,) + done.shape[2:]), ('dp', 'mp'), split_...]
    all_to_all x5 -> x4, starting transfers between devices: 30.7 us -> 22.3 us  [exchange(): return lax.all_to_all(rows, 'dp', split_axis=0, concat_axis=0, tiled=True)]
    unnamed x22 -> x38, local copies, waits for them, and re-layouts: 7.13 us -> 14.5 us
    ppermute x9 -> x15, starting transfers between devices: 13.2 us -> 20.1 us  [shifted(): lax.ppermute(array, 'mp', [(i, (i + k) % mp_size) for i in range(mp_size)])]
    all_to_all x5 -> x4, waiting for transfers between devices: 59.3 us -> 54 us  [exchange(): return lax.all_to_all(rows, 'dp', split_axis=0, concat_axis=0, tiled=True)]
    gather x0 -> x1, local copies, waits for them, and re-layouts: none -> 3.59 us  [per_device(): jnp.take(input_weight.reshape(mp_size, part, -1), turned, axis=0)]
  transfers between devices with their start and end apart: 18 -> 21, of which waited for: 10 -> 5; matrix products, arithmetic and copies ran while one was open for 5% -> 6% of each run, Pallas kernels for 17% -> 17%
where the time goes in v4:
time: 234 us; the launch traced here: 233 us
  waiting for transfers between devices  84.9 us (36%)
  starting transfers between devices  51.1 us (22%)
  Pallas kernels  49.7 us (21%)
  local copies, waits for them, and re-layouts  22.6 us (10%)
  between operations  15 us (6%)
  other arithmetic  9.38 us (4%)
    all_to_all x4, waiting for transfers between devices, exchange(): return lax.all_to_all(rows, 'dp', split_axis=0, concat_axis=0, tiled=True)  54 us
    all_to_all x1, waiting for transfers between devices, per_device(): lax.all_to_all(done.reshape((-1,) + done.shape[2:]), ('dp', 'mp'), split_...  30.8 us
    all_to_all x4, starting transfers between devices, exchange(): return lax.all_to_all(rows, 'dp', split_axis=0, concat_axis=0, tiled=True)  22.3 us
    ppermute x15, starting transfers between devices, shifted(): lax.ppermute(array, 'mp', [(i, (i + k) % mp_size) for i in range(mp_size)])  20.1 us
    pallas_call x2, Pallas kernels, attend(): pl.pallas_call(body, out_shape=[jax.ShapeDtypeStruct((users, quarter, wid...  18.1 us
    unnamed x38, local copies, waits for them, and re-layouts  14.5 us
    pallas_call x1, Pallas kernels, attend_packed(): pl.pallas_call(body, out_shape=[jax.ShapeDtypeStruct((users, quarter, wid...  11.8 us
    all_to_all x1, starting transfers between devices, per_device(): lax.all_to_all(done.reshape((-1,) + done.shape[2:]), ('dp', 'mp'), split_...  8.73 us
  transfers between devices with their start and end apart: 21, of which 5 were waited for; matrix products, arithmetic and copies ran while one was open for 6% of the time, Pallas kernels for 17%

profile of v4, /device:TPU:1, one launch (start us, length us, event | category | flops | bytes accessed | tf_op | source)
XLA Modules:
  0.0 232.8 jit_solution(11092883178180965240)
XLA Ops:
  6.5 0.7 compare_select_fusion.14
  7.2 0.7 add_select_fusion
  8.6 0.7 and_select_fusion.4
  9.4 1.6 copy-done.3
  11.6 1.7 shard_map.91
  13.3 9.7 %all-to-all-start = ((bf16[32,80,256]{2,1,0:T(8,128)(2,1)}), bf16[32,80,256]{2,1,0:T(8,128)(2,1)S(1)}, u32[]{:S(2)}, u32[]{:S(2)}) async-start(bf16[32,80,256]{2,1,0:T(8,128)(2,1)} %shard_map.91), calls=%async_computation | async-start | bytes 2621440 | tf_op jit(solution)/shard_map/all_to_all | solution.py:483
  23.1 1.3 collective-permute-start.6
  24.3 2.5 %collective-permute-start.7 = (bf16[256,1024]{1,0:T(8,128)(2,1)}, bf16[256,1024]{1,0:T(8,128)(2,1)}, u32[]{:S(2)}, u32[]{:S(2)}) collective-permute-start(bf16[256,1024]{1,0:T(8,128)(2,1)} %refs_12_.2), channel_id=1, source_target_pairs={{0,2},{1,3},{2,0},{3,1},{4,6},{5,7},{6,4},{7,5},{8,10},{9,11},{10,... | collective-permute-start | bytes 1572872 | tf_op jit(solution)/shard_map/ppermute | solution.py:488
  26.8 1.2 collective-permute-start.8
  28.2 0.7 gather_fusion.2
  29.9 13.0 %all-to-all-done.refs_0_ = bf16[32,80,256]{2,1,0:T(8,128)(2,1)S(1)} async-done(((bf16[32,80,256]{2,1,0:T(8,128)(2,1)}), bf16[32,80,256]{2,1,0:T(8,128)(2,1)S(1)}, u32[]{:S(2)}, u32[]{:S(2)}) %all-to-all-start) | async-done | bytes 1310752 | tf_op jit(solution)/shard_map/all_to_all | solution.py:483
  44.3 1.1 copy-done.5
  45.3 4.0 %all-to-all-start.1 = ((bf16[32,80,256]{2,1,0:T(8,128)(2,1)}), bf16[32,80,256]{2,1,0:T(8,128)(2,1)S(1)}, u32[]{:S(2)}, u32[]{:S(2)}) async-start(bf16[32,80,256]{2,1,0:T(8,128)(2,1)} %copy-done.5), calls=%async_computation.1 | async-start | bytes 2621440 | tf_op jit(solution)/shard_map/all_to_all | solution.py:483
  50.1 1.0 copy-done.6
  51.1 3.6 %gather_fusion.3 = bf16[4,256,1024]{2,1,0:T(8,128)(2,1)} fusion(bf16[4,256,1024]{2,1,0:T(8,128)(2,1)} %bitcast.28, s32[1024]{0:T(1024)S(1)} %pad_clamp_fusion.1), kind=kCustom, calls=%fused_computation.3 | custom fusion | bytes 4194320 | tf_op jit(solution)/shard_map/jit(_take)/gather | solution.py:553
  56.9 1.0 stack.23.info_ref.refs_9_
  58.0 1.9 bitcast_select_fusion.refs_8_
  59.8 9.4 %all-to-all-done.1.src = bf16[32,80,256]{2,1,0:T(8,128)(2,1)S(1)} async-done(((bf16[32,80,256]{2,1,0:T(8,128)(2,1)}), bf16[32,80,256]{2,1,0:T(8,128)(2,1)S(1)}, u32[]{:S(2)}, u32[]{:S(2)}) %all-to-all-start.1) | async-done | bytes 1310752 | tf_op jit(solution)/shard_map/all_to_all | solution.py:483
  69.3 1.0 copy-done.7
  70.4 4.6 %all-to-all-start.2 = ((bf16[32,64,256]{2,1,0:T(8,128)(2,1)}), bf16[32,64,256]{2,1,0:T(8,128)(2,1)}, u32[]{:S(2)}, u32[]{:S(2)}) async-start(bf16[32,64,256]{2,1,0:T(8,128)(2,1)} %copy-done.6), calls=%async_computation.2 | async-start | bytes 2097152 | tf_op jit(solution)/shard_map/all_to_all | solution.py:483
  75.7 16.4 %all-to-all-done.2.refs_0_ = bf16[32,64,256]{2,1,0:T(8,128)(2,1)} async-done(((bf16[32,64,256]{2,1,0:T(8,128)(2,1)}), bf16[32,64,256]{2,1,0:T(8,128)(2,1)}, u32[]{:S(2)}, u32[]{:S(2)}) %all-to-all-start.2) | async-done | bytes 1048608 | tf_op jit(solution)/shard_map/all_to_all | solution.py:483
  92.1 2.3 shard_map.95
  94.3 3.9 %all-to-all-start.3 = ((bf16[32,64,256]{2,1,0:T(8,128)(2,1)}), bf16[32,64,256]{2,1,0:T(8,128)(2,1)S(1)}, u32[]{:S(2)}, u32[]{:S(2)}) async-start(bf16[32,64,256]{2,1,0:T(8,128)(2,1)} %shard_map.95), calls=%async_computation.3 | async-start | bytes 2097152 | tf_op jit(solution)/shard_map/all_to_all | solution.py:483
  99.9 15.3 %all-to-all-done.3.rows_ref = bf16[32,64,256]{2,1,0:T(8,128)(2,1)S(1)} async-done(((bf16[32,64,256]{2,1,0:T(8,128)(2,1)}), bf16[32,64,256]{2,1,0:T(8,128)(2,1)S(1)}, u32[]{:S(2)}, u32[]{:S(2)}) %all-to-all-start.3) | async-done | bytes 1048608 | tf_op jit(solution)/shard_map/all_to_all | solution.py:483
  115.2 1.1 copy-done.17
  116.3 1.3 shard_map.96
  117.7 2.5 %collective-permute-start.10 = (bf16[544,256]{1,0:T(8,128)(2,1)S(1)}, bf16[544,256]{1,0:T(8,128)(2,1)S(1)}, u32[]{:S(2)}, u32[]{:S(2)}) collective-permute-start(bf16[544,256]{1,0:T(8,128)(2,1)S(1)} %get-tuple-element.92.refs_1_), channel_id=1, source_target_pairs={{0,3},{1,0},{2,1},{3,2},{4,7},{5,4},{6,5},{7,6},{8,11},{9,8},{10,9... | collective-permute-start | bytes 835592 | tf_op jit(solution)/shard_map/ppermute | solution.py:488
  120.4 2.5 %collective-permute-start.14 = (bf16[544,256]{1,0:T(8,128)(2,1)S(1)}, bf16[544,256]{1,0:T(8,128)(2,1)}, u32[]{:S(2)}, u32[]{:S(2)}) collective-permute-start(bf16[544,256]{1,0:T(8,128)(2,1)S(1)} %get-tuple-element.91.refs_0_), channel_id=1, source_target_pairs={{0,3},{1,0},{2,1},{3,2},{4,7},{5,4},{6,5},{7,6},{8,11},{9,8},{10,9... | collective-permute-start | bytes 835592 | tf_op jit(solution)/shard_map/ppermute | solution.py:488
  122.9 2.2 copy-done.1
  125.1 9.6 %shard_map.97 = (bf16[32,16,256]{2,1,0:T(8,128)(2,1)S(1)}, bf16[32,16,256]{2,1,0:T(8,128)(2,1)}, bf16[32,16,256]{2,1,0:T(8,128)(2,1)S(1)}, bf16[32,16,256]{2,1,0:T(8,128)(2,1)S(1)}) custom-call(s32[32]{0:T(128)S(1)} %select_reduce_fusion.4.order_ref, s32[1]{0:T(128)} %bitcast.13.rank_ref, bf16[4,32,64,256]{3,2,1,0:T(8,128)(2,1)S(1)} %bitcast.24, ...), custom_call_target="tpu_custom_call" | custom-call | tf_op jit(solution)/shard_map/pallas_call | solution.py:200
  134.8 2.7 %collective-permute-start.13 = (bf16[544,256]{1,0:T(8,128)(2,1)S(1)}, bf16[544,256]{1,0:T(8,128)(2,1)}, u32[]{:S(2)}, u32[]{:S(2)}) collective-permute-start(bf16[544,256]{1,0:T(8,128)(2,1)S(1)} %collective-permute-done.10.refs_7_), channel_id=1, source_target_pairs={{0,3},{1,0},{2,1},{3,2},{4,7},{5,4},{6,5},{7,6},{8,11},{9,8},{10,9... | collective-permute-start | bytes 835592 | tf_op jit(solution)/shard_map/ppermute | solution.py:488
  137.5 8.5 %shard_map.99 = (bf16[32,16,256]{2,1,0:T(8,128)(2,1)S(1)}, bf16[32,16,256]{2,1,0:T(8,128)(2,1)}, bf16[32,16,256]{2,1,0:T(8,128)(2,1)S(1)}, bf16[32,16,256]{2,1,0:T(8,128)(2,1)S(1)}) custom-call(s32[32]{0:T(128)S(1)} %select_reduce_fusion.4.order_ref, ...), custom_call_target="tpu_custom_call", output_to_operand_aliasing={{0}: (13, {}), {1}: (14, {}), {2}: (15, {}), {3}: (16, {})} | custom-call | tf_op jit(solution)/shard_map/pallas_call | solution.py:200
  146.0 0.7 copy-done.8
  146.7 0.7 copy-done.10
  147.4 0.7 copy-done.11
  148.7 1.5 collective-permute-start.19
  150.2 1.4 collective-permute-start.20
  151.6 11.8 %shard_map.98 = (bf16[32,16,256]{2,1,0:T(8,128)(2,1)S(1)}, bf16[32,16,256]{2,1,0:T(8,128)(2,1)}, bf16[32,16,256]{2,1,0:T(8,128)(2,1)}, bf16[32,16,256]{2,1,0:T(8,128)(2,1)}) custom-call(s32[32]{0:T(128)S(1)} %get-tuple-element.134.order_ref, s32[32]{0:T(128)S(1)} %broadcast_minimum_fusion.offsets_ref, s32[32]{0:T(128)S(1)} %get-tuple-element.136.slots_ref.seats_ref, ...), custom_call_target="tpu_custom_call" | custom-call | tf_op jit(solution)/shard_map/pallas_call | solution.py:315
  163.4 0.7 copy-done.12
  164.6 1.8 collective-permute-start.16
  166.4 2.1 collective-permute-start.17
  169.9 2.2 copy-done.2
  172.1 0.9 copy-done.9
  173.1 5.5 %shard_map.100.refs_16_ = bf16[32,4,2,16,256]{4,3,2,1,0:T(8,128)(2,1)} custom-call(s32[33]{0:T(128)S(1)} %pad_add_fusion.1.scalar_ref, bf16[4,32,64,256]{3,2,1,0:T(8,128)(2,1)S(1)} %bitcast.26, bf16[32,16,256]{2,1,0:T(8,128)(2,1)S(1)} %copy-done.9, bf16[32,16,256]{2,1,0:T(8,128)(2,1)} %collective-permute-done.18.refs_1_, ...), custom_call_target="tpu_custom_call" | custom-call | tf_op jit(solution)/shard_map/pallas_call | solution.py:369
  178.6 5.5 %shard_map.101 = bf16[32,4,2,16,256]{4,3,2,1,0:T(8,128)(2,1)} custom-call(s32[33]{0:T(128)S(1)} %pad_add_fusion.scalar_ref, s32[32]{0:T(128)S(1)} %get-tuple-element.136.slots_ref.seats_ref, s32[32]{0:T(128)S(1)} %broadcast_minimum_fusion.offsets_ref, bf16[544,256]{1,0:T(8,128)(2,1)S(1)} %get-tuple-element.91.refs_0_, ...), custom_call_target="tpu_custom_call", output_to_operand_aliasing={{}: (19, {})} | custom-call | tf_op jit(solution)/shard_map/pallas_call | solution.py:426
  184.1 8.7 %all-to-all-start.4 = ((bf16[128,2,16,256]{3,2,1,0:T(8,128)(2,1)}), bf16[128,2,16,256]{3,2,1,0:T(8,128)(2,1)S(1)}, u32[]{:S(2)}, u32[]{:S(2)}) async-start(bf16[128,2,16,256]{3,2,1,0:T(8,128)(2,1)} %bitcast.16), calls=%async_computation.4 | async-start | bytes 4194304 | tf_op jit(solution)/shard_map/all_to_all | solution.py:617
  193.0 30.8 %all-to-all-done.4 = bf16[128,2,16,256]{3,2,1,0:T(8,128)(2,1)S(1)} async-done(((bf16[128,2,16,256]{3,2,1,0:T(8,128)(2,1)}), bf16[128,2,16,256]{3,2,1,0:T(8,128)(2,1)S(1)}, u32[]{:S(2)}, u32[]{:S(2)}) %all-to-all-start.4) | async-done | bytes 2097184 | tf_op jit(solution)/shard_map/all_to_all | solution.py:617
  223.8 2.1 shard_map.102
  (92 shorter events, 11.2 us)
Async XLA Ops:
  6.5 21.6 %copy-start = (s32[32]{0:T(128)S(1)}, s32[32]{0:T(128)}, u32[]{:S(2)}) copy-start(s32[32]{0:T(128)} %param.16) | copy-start | bytes 388
  9.4 1.6 copy-start.3
  11.0 0.7 copy-start.14
  13.3 15.6 %copy-start.20 = (f32[2,16]{1,0:T(2,128)S(1)}, f32[2,16]{1,0:T(2,128)}, u32[]{:S(2)}) copy-start(f32[2,16]{1,0:T(2,128)} %param.18) | copy-start | bytes 388
  13.3 29.5 %all-to-all-start = ((bf16[32,80,256]{2,1,0:T(8,128)(2,1)}), bf16[32,80,256]{2,1,0:T(8,128)(2,1)S(1)}, u32[]{:S(2)}, u32[]{:S(2)}) async-start(bf16[32,80,256]{2,1,0:T(8,128)(2,1)} %shard_map.91), calls=%async_computation | async-start | bytes 2621440 | tf_op jit(solution)/shard_map/all_to_all | solution.py:483
  23.1 47.3 %collective-permute-start.6 = (bf16[256,1024]{1,0:T(8,128)(2,1)}, bf16[256,1024]{1,0:T(8,128)(2,1)}, u32[]{:S(2)}, u32[]{:S(2)}) collective-permute-start(bf16[256,1024]{1,0:T(8,128)(2,1)} %refs_12_.2), channel_id=1, source_target_pairs={{0,1},{1,2},{2,3},{3,0},{4,5},{5,6},{6,7},{7,4},{8,9},{9,10},{10,1... | collective-permute-start | bytes 1572872 | tf_op jit(solution)/shard_map/ppermute | solution.py:488
  24.3 46.0 %collective-permute-start.7 = (bf16[256,1024]{1,0:T(8,128)(2,1)}, bf16[256,1024]{1,0:T(8,128)(2,1)}, u32[]{:S(2)}, u32[]{:S(2)}) collective-permute-start(bf16[256,1024]{1,0:T(8,128)(2,1)} %refs_12_.2), channel_id=1, source_target_pairs={{0,2},{1,3},{2,0},{3,1},{4,6},{5,7},{6,4},{7,5},{8,10},{9,11},{10,... | collective-permute-start | bytes 1572872 | tf_op jit(solution)/shard_map/ppermute | solution.py:488
  26.8 43.5 %collective-permute-start.8 = (bf16[256,1024]{1,0:T(8,128)(2,1)}, bf16[256,1024]{1,0:T(8,128)(2,1)}, u32[]{:S(2)}, u32[]{:S(2)}) collective-permute-start(bf16[256,1024]{1,0:T(8,128)(2,1)} %refs_12_.2), channel_id=1, source_target_pairs={{0,3},{1,0},{2,1},{3,2},{4,7},{5,4},{6,5},{7,6},{8,11},{9,8},{10,9... | collective-permute-start | bytes 1572872 | tf_op jit(solution)/shard_map/ppermute | solution.py:488
  43.6 5.8 %copy-start.4 = (bf16[32,128,256]{2,1,0:T(8,128)(2,1)S(1)}, bf16[32,128,256]{2,1,0:T(8,128)(2,1)}, u32[]{:S(2)}) copy-start(bf16[32,128,256]{2,1,0:T(8,128)(2,1)} %refs_0_.3) | copy-start | bytes 6291460
  44.3 1.1 copy-start.5
  45.3 23.9 %all-to-all-start.1 = ((bf16[32,80,256]{2,1,0:T(8,128)(2,1)}), bf16[32,80,256]{2,1,0:T(8,128)(2,1)S(1)}, u32[]{:S(2)}, u32[]{:S(2)}) async-start(bf16[32,80,256]{2,1,0:T(8,128)(2,1)} %copy-done.5), calls=%async_computation.1 | async-start | bytes 2621440 | tf_op jit(solution)/shard_map/all_to_all | solution.py:483
  49.3 68.3 %all-gather.3.cloned.1.call-start = ((), (), s32[]{:S(2)}) async-start(), calls=%async_computation.5 | async-start | bytes 5242880 | tf_op jit(solution)/shard_map/all_gather | solution.py:550
  50.0 1.0 copy-start.6
  69.3 1.0 copy-start.7
  70.4 21.7 %all-to-all-start.2 = ((bf16[32,64,256]{2,1,0:T(8,128)(2,1)}), bf16[32,64,256]{2,1,0:T(8,128)(2,1)}, u32[]{:S(2)}, u32[]{:S(2)}) async-start(bf16[32,64,256]{2,1,0:T(8,128)(2,1)} %copy-done.6), calls=%async_computation.2 | async-start | bytes 2097152 | tf_op jit(solution)/shard_map/all_to_all | solution.py:483
  94.3 20.9 %all-to-all-start.3 = ((bf16[32,64,256]{2,1,0:T(8,128)(2,1)}), bf16[32,64,256]{2,1,0:T(8,128)(2,1)S(1)}, u32[]{:S(2)}, u32[]{:S(2)}) async-start(bf16[32,64,256]{2,1,0:T(8,128)(2,1)} %shard_map.95), calls=%async_computation.3 | async-start | bytes 2097152 | tf_op jit(solution)/shard_map/all_to_all | solution.py:483
  115.2 1.1 copy-start.17
  117.7 17.1 %collective-permute-start.10 = (bf16[544,256]{1,0:T(8,128)(2,1)S(1)}, bf16[544,256]{1,0:T(8,128)(2,1)S(1)}, u32[]{:S(2)}, u32[]{:S(2)}) collective-permute-start(bf16[544,256]{1,0:T(8,128)(2,1)S(1)} %get-tuple-element.92.refs_1_), channel_id=1, source_target_pairs={{0,3},{1,0},{2,1},{3,2},{4,7},{5,4},{6,5},{7,6},{8,11},{9,8},{10,9... | collective-permute-start | bytes 835592 | tf_op jit(solution)/shard_map/ppermute | solution.py:488
  120.2 14.6 %collective-permute-start.9 = (bf16[544,256]{1,0:T(8,128)(2,1)S(1)}, bf16[544,256]{1,0:T(8,128)(2,1)S(1)}, u32[]{:S(2)}, u32[]{:S(2)}) collective-permute-start(bf16[544,256]{1,0:T(8,128)(2,1)S(1)} %get-tuple-element.91.refs_0_), channel_id=1, source_target_pairs={{0,1},{1,2},{2,3},{3,0},{4,5},{5,6},{6,7},{7,4},{8,9},{9,10},{10,1... | collective-permute-start | bytes 835592 | tf_op jit(solution)/shard_map/ppermute | solution.py:488
  120.2 28.5 %collective-permute-start.11 = (bf16[544,256]{1,0:T(8,128)(2,1)S(1)}, bf16[544,256]{1,0:T(8,128)(2,1)S(1)}, u32[]{:S(2)}, u32[]{:S(2)}) collective-permute-start(bf16[544,256]{1,0:T(8,128)(2,1)S(1)} %get-tuple-element.92.refs_1_), channel_id=1, source_target_pairs={{0,1},{1,2},{2,3},{3,0},{4,5},{5,6},{6,7},{7,4},{8,9},{9,10},{10,1... | collective-permute-start | bytes 835592 | tf_op jit(solution)/shard_map/ppermute | solution.py:488
  120.4 29.8 %collective-permute-start.14 = (bf16[544,256]{1,0:T(8,128)(2,1)S(1)}, bf16[544,256]{1,0:T(8,128)(2,1)}, u32[]{:S(2)}, u32[]{:S(2)}) collective-permute-start(bf16[544,256]{1,0:T(8,128)(2,1)S(1)} %get-tuple-element.91.refs_0_), channel_id=1, source_target_pairs={{0,3},{1,0},{2,1},{3,2},{4,7},{5,4},{6,5},{7,6},{8,11},{9,8},{10,9... | collective-permute-start | bytes 835592 | tf_op jit(solution)/shard_map/ppermute | solution.py:488
  122.9 2.2 copy-start.1
  125.1 12.4 %copy-start.15 = (bf16[1024,1024]{1,0:T(8,128)(2,1)S(1)}, bf16[1024,1024]{1,0:T(8,128)(2,1)}, u32[]{:S(2)}) copy-start(bf16[1024,1024]{1,0:T(8,128)(2,1)} %weight_ref.3) | copy-start | bytes 6291460
  125.1 12.4 %copy-start.18 = (f32[32,8,256]{2,1,0:T(8,128)S(1)}, f32[32,8,256]{2,1,0:T(8,128)}, u32[]{:S(2)}) copy-start(f32[32,8,256]{2,1,0:T(8,128)} %stack.23.info_ref.refs_9_) | copy-start | bytes 786436
  134.7 16.8 %collective-permute-start.12 = (bf16[544,256]{1,0:T(8,128)(2,1)S(1)}, bf16[544,256]{1,0:T(8,128)(2,1)}, u32[]{:S(2)}, u32[]{:S(2)}) collective-permute-start(bf16[544,256]{1,0:T(8,128)(2,1)S(1)} %collective-permute-done.9.refs_2_), channel_id=1, source_target_pairs={{0,1},{1,2},{2,3},{3,0},{4,5},{5,6},{6,7},{7,4},{8,9},{9,10},{10,1... | collective-permute-start | bytes 835592 | tf_op jit(solution)/shard_map/ppermute | solution.py:488
  134.8 16.7 %collective-permute-start.13 = (bf16[544,256]{1,0:T(8,128)(2,1)S(1)}, bf16[544,256]{1,0:T(8,128)(2,1)}, u32[]{:S(2)}, u32[]{:S(2)}) collective-permute-start(bf16[544,256]{1,0:T(8,128)(2,1)S(1)} %collective-permute-done.10.refs_7_), channel_id=1, source_target_pairs={{0,3},{1,0},{2,1},{3,2},{4,7},{5,4},{6,5},{7,6},{8,11},{9,8},{10,9... | collective-permute-start | bytes 835592 | tf_op jit(solution)/shard_map/ppermute | solution.py:488
  146.0 0.7 copy-start.8
  146.7 0.7 copy-start.10
  147.4 0.7 copy-start.11
  148.1 18.3 %collective-permute-start.18 = (bf16[32,16,256]{2,1,0:T(8,128)(2,1)}, bf16[32,16,256]{2,1,0:T(8,128)(2,1)}, u32[]{:S(2)}, u32[]{:S(2)}) collective-permute-start(bf16[32,16,256]{2,1,0:T(8,128)(2,1)} %get-tuple-element.115), channel_id=1, source_target_pairs={{0,1},{1,2},{2,3},{3,0},{4,5},{5,6},{6,7},{7,4},{8,9},{9,10},{10,1... | collective-permute-start | bytes 786440 | tf_op jit(solution)/shard_map/ppermute | solution.py:488
  148.7 21.2 %collective-permute-start.19 = (bf16[32,16,256]{2,1,0:T(8,128)(2,1)}, bf16[32,16,256]{2,1,0:T(8,128)(2,1)}, u32[]{:S(2)}, u32[]{:S(2)}) collective-permute-start(bf16[32,16,256]{2,1,0:T(8,128)(2,1)} %copy-done.10), channel_id=1, source_target_pairs={{0,2},{1,3},{2,0},{3,1},{4,6},{5,7},{6,4},{7,5},{8,10},{9,11},{10,... | collective-permute-start | bytes 786440 | tf_op jit(solution)/shard_map/ppermute | solution.py:488
  150.2 19.7 %collective-permute-start.20 = (bf16[32,16,256]{2,1,0:T(8,128)(2,1)}, bf16[32,16,256]{2,1,0:T(8,128)(2,1)}, u32[]{:S(2)}, u32[]{:S(2)}) collective-permute-start(bf16[32,16,256]{2,1,0:T(8,128)(2,1)} %copy-done.11), channel_id=1, source_target_pairs={{0,3},{1,0},{2,1},{3,2},{4,7},{5,4},{6,5},{7,6},{8,11},{9,8},{10,9... | collective-permute-start | bytes 786440 | tf_op jit(solution)/shard_map/ppermute | solution.py:488
  163.4 0.7 copy-start.12
  164.1 14.4 %collective-permute-start.15 = (bf16[32,16,256]{2,1,0:T(8,128)(2,1)}, bf16[32,16,256]{2,1,0:T(8,128)(2,1)S(1)}, u32[]{:S(2)}, u32[]{:S(2)}) collective-permute-start(bf16[32,16,256]{2,1,0:T(8,128)(2,1)} %get-tuple-element.103), channel_id=1, source_target_pairs={{0,1},{1,2},{2,3},{3,0},{4,5},{5,6},{6,7},{7,4},{8,9},{9,10},{10,1... | collective-permute-start | bytes 786440 | tf_op jit(solution)/shard_map/ppermute | solution.py:488
  164.6 13.9 %collective-permute-start.16 = (bf16[32,16,256]{2,1,0:T(8,128)(2,1)}, bf16[32,16,256]{2,1,0:T(8,128)(2,1)S(1)}, u32[]{:S(2)}, u32[]{:S(2)}) collective-permute-start(bf16[32,16,256]{2,1,0:T(8,128)(2,1)} %get-tuple-element.104), channel_id=1, source_target_pairs={{0,2},{1,3},{2,0},{3,1},{4,6},{5,7},{6,4},{7,5},{8,10},{9,11},{10,... | collective-permute-start | bytes 786440 | tf_op jit(solution)/shard_map/ppermute | solution.py:488
  166.4 12.2 %collective-permute-start.17 = (bf16[32,16,256]{2,1,0:T(8,128)(2,1)}, bf16[32,16,256]{2,1,0:T(8,128)(2,1)S(1)}, u32[]{:S(2)}, u32[]{:S(2)}) collective-permute-start(bf16[32,16,256]{2,1,0:T(8,128)(2,1)} %get-tuple-element.105), channel_id=1, source_target_pairs={{0,3},{1,0},{2,1},{3,2},{4,7},{5,4},{6,5},{7,6},{8,11},{9,8},{10,9... | collective-permute-start | bytes 786440 | tf_op jit(solution)/shard_map/ppermute | solution.py:488
  169.9 2.2 copy-start.2
  172.1 0.9 copy-start.9
  173.1 5.5 %copy-start.13 = (bf16[32,16,256]{2,1,0:T(8,128)(2,1)S(1)}, bf16[32,16,256]{2,1,0:T(8,128)(2,1)}, u32[]{:S(2)}) copy-start(bf16[32,16,256]{2,1,0:T(8,128)(2,1)} %copy-done.12) | copy-start | bytes 786436
  184.1 39.7 %all-to-all-start.4 = ((bf16[128,2,16,256]{3,2,1,0:T(8,128)(2,1)}), bf16[128,2,16,256]{3,2,1,0:T(8,128)(2,1)S(1)}, u32[]{:S(2)}, u32[]{:S(2)}) async-start(bf16[128,2,16,256]{3,2,1,0:T(8,128)(2,1)} %bitcast.16), calls=%async_computation.4 | async-start | bytes 4194304 | tf_op jit(solution)/shard_map/all_to_all | solution.py:617
Sparse Core Ops, SparseCore 0:
  70.5 45.6 all-gather.2

commit v5 on v4

--- a/solution.py
+++ b/solution.py
@@ -75,18 +75,20 @@
     )(index, *tags, whole)
 
 
-def trim(rows, size):
+def halves(rows, size):
     users, _, width = rows.shape
-
-    def body(src, out):
-        for i in range(users):
-            out[i] = src[i, :size, :]
-
-    return pl.pallas_call(
-        body,
-        out_shape=jax.ShapeDtypeStruct((users, size, width), rows.dtype),
+    half = users // 2
+
+    def body(src, *outs):
+        for n in range(2):
+            for i in range(half):
+                outs[n][i] = src[n * half + i, :size, :]
+
+    return pl.pallas_call(
+        body,
+        out_shape=[jax.ShapeDtypeStruct((half, size, width), rows.dtype)] * 2,
         in_specs=[pl.BlockSpec(memory_space=pltpu.VMEM)],
-        out_specs=pl.BlockSpec(memory_space=pltpu.VMEM),
+        out_specs=[pl.BlockSpec(memory_space=pltpu.VMEM)] * 2,
         compiler_params=pltpu.CompilerParams(vmem_limit_bytes=VMEM),
     )(rows)
 
@@ -166,17 +168,21 @@
     )
 
 
-def attend(full, weight, history, order, rank, rows_info, heads, first, some, before=None):
-    mp, users, rows, part = full.shape
+def attend(full, weight, history, order, rank, rows_info, heads, first, before):
+    mp = len(full)
+    some, rows, part = full[0].shape
+    users = order.shape[0]
     events, kv_width = history.shape[1:]
     quarter = rows // mp
     total = BATCH * rows
+    skip = first // BATCH
     width = heads * HD
-    skip = first // BATCH
-
-    def body(order_ref, rank_ref, full_ref, weight_ref, info_ref, *refs):
-        hist_refs, out_refs, store = refs[:BATCH], refs[-1 - mp : -1], refs[-1]
-        normed = normalise([full_ref[k].reshape(total, part) for k in range(mp)])
+
+    def body(order_ref, rank_ref, *refs):
+        full_refs, weight_ref, info_ref = refs[:mp], refs[mp], refs[mp + 1]
+        hist_refs = refs[mp + 2 : mp + 2 + BATCH]
+        out_refs, store = refs[-1 - mp : -1], refs[-1]
+        normed = normalise([f[...].reshape(total, part) for f in full_refs])
         infos = [info_ref.at[b] for b in range(BATCH)]
         for h in range(heads):
             projected = silu_dot(normed, weight_ref[:, h * 4 * HD : (h + 1) * 4 * HD])
@@ -195,7 +201,7 @@
         )
 
     extra = () if before is None else tuple(before)
-    inputs = (order, rank, full, weight, rows_info, *([history] * BATCH), *extra)
+    inputs = (order, rank, *full, weight, rows_info, *([history] * BATCH), *extra)
     at = len(inputs) - len(extra)
     return pl.pallas_call(
         body,
@@ -203,8 +209,8 @@
         grid_spec=pltpu.PrefetchScalarGridSpec(
             num_scalar_prefetch=2,
             grid=(some // BATCH,),
-            in_specs=[
-                pl.BlockSpec((mp, BATCH, rows, part), lambda i, *_: (0, skip + i, 0, 0)),
+            in_specs=[pl.BlockSpec((BATCH, rows, part), lambda i, *_: (i, 0, 0)) for _ in full]
+            + [
                 pl.BlockSpec(weight.shape, lambda i, *_: (0, 0)),
                 pl.BlockSpec((BATCH,) + rows_info.shape[1:], lambda i, *_: (skip + i, 0, 0)),
             ]
@@ -347,24 +353,32 @@
     users, quarter, part = gated[0].shape
     out_part = weights[0].shape[1] // mp
     batch = 8
+    per_half = users // 2 // batch
     start = PIECES[piece][0]
     extra = () if before is None else (before,)
 
-    def body(scalar_ref, full_ref, *refs):
-        gated_refs, weight_refs, out_ref = refs[:mp], refs[mp : 2 * mp], refs[-1]
-        first = pl.program_id(0) * batch
-        acc = rank_dot(
-            [g[...].reshape(batch * quarter, part) for g in gated_refs],
-            [w[...] for w in weight_refs],
+    def body(scalar_ref, *refs):
+        full_refs, gated_refs = refs[: 2 * mp], refs[2 * mp : 3 * mp]
+        weight_refs, out_ref = refs[3 * mp : 4 * mp], refs[-1]
+        step = pl.program_id(0)
+        rank = scalar_ref[0]
+        rows = [g[...].reshape(batch * quarter, part) for g in gated_refs]
+        row = lax.broadcasted_iota(jnp.int32, (quarter, out_part), 0) + (start + rank * quarter)
+        for k in range(mp):
+            column = (rank + (mp - k)) % mp
+            at = pl.multiple_of(column * out_part, out_part)
+            acc = rank_dot(rows, [w[:, pl.ds(at, out_part)] for w in weight_refs])
+            for b in range(batch):
+                alive = row < scalar_ref[1 + step * batch + b]
+                residual = jnp.where(step < per_half, full_refs[k][b], full_refs[mp + k][b])
+                mine = acc[b * quarter : (b + 1) * quarter] + residual.astype(jnp.float32)
+                out_ref[b, column, 0] = jnp.where(alive, mine, 0.0).astype(jnp.bfloat16)
+
+    def full_spec(n):
+        return pl.BlockSpec(
+            (batch, quarter, part),
+            lambda i, s: (jnp.clip(i - n * per_half, 0, per_half - 1), s[0], 0),
         )
-        row = lax.broadcasted_iota(jnp.int32, (quarter, out_part), 0)
-        row = row + (start + scalar_ref[0] * quarter)
-        for b in range(batch):
-            alive = row < scalar_ref[1 + first + b]
-            for k in range(mp):
-                mine = acc[b * quarter : (b + 1) * quarter, k * out_part : (k + 1) * out_part]
-                mine = mine + full_ref[k, b].astype(jnp.float32)
-                out_ref[b, k, 0] = jnp.where(alive, mine, 0.0).astype(jnp.bfloat16)
 
     return pl.pallas_call(
         body,
@@ -372,7 +386,7 @@
         grid_spec=pltpu.PrefetchScalarGridSpec(
             num_scalar_prefetch=1,
             grid=(users // batch,),
-            in_specs=[pl.BlockSpec((mp, batch, quarter, part), lambda i, s: (0, i, s[0], 0))]
+            in_specs=[full_spec(n) for n in range(2) for _ in range(mp)]
             + [pl.BlockSpec((batch, quarter, part), lambda i, s: (i, 0, 0)) for _ in gated]
             + [pl.BlockSpec(w.shape, lambda i, s: (0, 0)) for w in weights]
             + [pl.BlockSpec(memory_space=pl.ANY) for _ in extra],
@@ -380,9 +394,9 @@
                 (batch, mp, 1, quarter, out_part), lambda i, s: (i, 0, piece, 0, 0)
             ),
         ),
-        input_output_aliases={2 + 2 * mp: 0} if extra else {},
-        compiler_params=pltpu.CompilerParams(vmem_limit_bytes=VMEM),
-    )(scalars, full, *gated, *weights, *extra)
+        input_output_aliases={1 + 4 * mp: 0} if extra else {},
+        compiler_params=pltpu.CompilerParams(vmem_limit_bytes=VMEM),
+    )(scalars, *full[0], *full[1], *gated, *weights, *extra)
 
 
 def project_out_packed(gated, full, weights, scalars, slots, offsets, piece, before):
@@ -496,7 +510,7 @@
         jnp.where(owner_rank[None, :] == ranks[:, None], ranks[None, :], 0), axis=1
     )
     tagged_0 = exchange(permute_in(send_second, scored_0, (0, first_rows + GROUP)))
-    owned_0 = trim(tagged_0, first_rows)
+    owned_0 = halves(tagged_0, first_rows)
     live = tagged_0[:, first_rows + GROUP // 2, 0].astype(jnp.int32)
 
     scored_here = scorer.reshape(dp_size, users) == dp_rank
@@ -546,9 +560,6 @@
     rank = mp_rank[None].astype(jnp.int32)
     seat_last = (jnp.maximum(count - 1, 0) // BATCH)[None].astype(jnp.int32)
 
-    def gather(rows):
-        return lax.all_gather(rows, "mp", axis=0, tiled=False)
-
     turned = (mp_rank + (mp_size - jnp.arange(mp_size, dtype=jnp.int32))) % mp_size
     weight_in = jnp.take(input_weight.reshape(mp_size, part, -1), turned, axis=0)
     weight_in = weight_in.reshape(input_weight.shape)
@@ -560,25 +571,27 @@
     rows_1, owned_0, rows_info, weight_in, *weights_out = lax.optimization_barrier(
         (rows_1, owned_0, rows_info, weight_in, *weights_out)
     )
-    full_0 = gather(owned_0)
+    low_0, high_0 = owned_0
+    full_low = [low_0, shifted(low_0, 1), None, shifted(low_0, 3)]
+    full_low[2] = shifted(full_low[1], 1)
+    full_high = [high_0, shifted(high_0, 1), None, shifted(high_0, 3)]
+    full_high[2] = shifted(full_high[3], 3)
     owned_1 = exchange(permute_in(send_second, exchange(rows_1), (0, second_rows)))
     owned_1, groups = lax.optimization_barrier((owned_1, groups))
     packed = pack(seat_slots, seat_offsets, owned_1, SIZE)
-    (low, high), full_0 = lax.optimization_barrier((packed, full_0))
-
+    low, high = packed
+
+    def attend_some(full, first, before=None):
+        return attend(
+            full, weight_in, history_cache, order, rank, rows_info, heads, first, before
+        )
+
+    gated_low = attend_some(full_low, 0)
     low_1, high_3 = shifted(low, 1), shifted(high, 3)
     high_1, low_3 = shifted(high, 1), shifted(low, 3)
-    half = users // 2
-
-    def attend_some(full, first, some, before=None):
-        return attend(
-            full, input_weight, history_cache, order, rank, rows_info, heads, first, some, before
-        )
-
-    gated_0 = attend_some(full_0, 0, half)
-    low_1, high_3, gated_0 = lax.optimization_barrier((low_1, high_3, gated_0))
+    low_1, high_3, gated_low = lax.optimization_barrier((low_1, high_3, gated_low))
     low_2, high_2 = shifted(low_1, 1), shifted(high_3, 3)
-    gated_0 = attend_some(full_0, half, users - half, gated_0)
+    gated_0 = attend_some(full_high, users // 2, gated_low)
     full_1 = [[low, high], [low_1, high_1], [low_2, high_2], [low_3, high_3]]
     gated_1 = attend_packed(
         full_1,
@@ -593,7 +606,9 @@
         second_rows,
         heads,
     )
-    done_0 = project_out(by_quarter(gated_0), full_0, weights_out, scalars, 0)
+    done_0 = project_out(
+        by_quarter(gated_0), (full_low, full_high), weights_out, scalars, 0
+    )
     done = project_out_packed(
         by_quarter(gated_1),
         full_1,
@@ -606,10 +621,11 @@
     )
 
     def unpacked(done, rows):
-        by_shift = jnp.stack([rows] + [shifted(rows, k) for k in range(1, mp_size)])
-        full = jnp.take(by_shift, turned, axis=0)
-        gated = by_quarter(attend_some(full, 0, users))
-        return project_out(gated, full, weights_out, scalars, 1, done)
+        every = [rows] + [shifted(rows, k) for k in range(1, mp_size)]
+        both = [[r[: users // 2] for r in every], [r[users // 2 :] for r in every]]
+        gated = attend_some(both[0], 0)
+        gated = by_quarter(attend_some(both[1], users // 2, gated))
+        return project_out(gated, both, weights_out, scalars, 1, done)
 
     done = lax.cond(
         jnp.sum(groups) > SIZE, unpacked, lambda done, rows: done, done, owned_1

time: 234 us -> 223 us (0.953)
  between operations: 15 us -> 1.8 us
  waiting for transfers between devices: 84.9 us -> 72.1 us
  starting transfers between devices: 51.1 us -> 58.6 us
  Pallas kernels: 49.7 us -> 53.7 us
    all_to_all x4, waiting for transfers between devices: 54 us -> 41.3 us  [exchange(): return lax.all_to_all(rows, 'dp', split_axis=0, concat_axis=0, tiled=True)]
    ppermute x15 -> x21, starting transfers between devices: 20.1 us -> 27.8 us  [shifted(): lax.ppermute(array, 'mp', [(i, (i + k) % mp_size) for i in range(mp_size)])]
    unnamed x38 -> x52, local copies, waits for them, and re-layouts: 14.5 us -> 15.2 us
  transfers between devices with their start and end apart: 21 -> 26, of which waited for: 5 -> 6; matrix products, arithmetic and copies ran while one was open for 6% -> 8% of each run, Pallas kernels for 17% -> 20%
where the time goes in v5:
time: 223 us; the launch traced here: 222 us
  waiting for transfers between devices  72.1 us (32%)
  starting transfers between devices  58.6 us (26%)
  Pallas kernels  53.7 us (24%)
  local copies, waits for them, and re-layouts  24.4 us (11%)
  other arithmetic  10.8 us (5%)
    all_to_all x4, waiting for transfers between devices, exchange(): return lax.all_to_all(rows, 'dp', split_axis=0, concat_axis=0, tiled=True)  41.3 us
    all_to_all x1, waiting for transfers between devices, per_device(): lax.all_to_all(done.reshape((-1,) + done.shape[2:]), ('dp', 'mp'), split_...  30.6 us
    ppermute x21, starting transfers between devices, shifted(): lax.ppermute(array, 'mp', [(i, (i + k) % mp_size) for i in range(mp_size)])  27.8 us
    all_to_all x4, starting transfers between devices, exchange(): return lax.all_to_all(rows, 'dp', split_axis=0, concat_axis=0, tiled=True)  23 us
    pallas_call x2, Pallas kernels, attend(): pl.pallas_call(body, out_shape=[jax.ShapeDtypeStruct((users, quarter, wid...  18.7 us
    unnamed x52, local copies, waits for them, and re-layouts  15.2 us
    pallas_call x1, Pallas kernels, attend_packed(): pl.pallas_call(body, out_shape=[jax.ShapeDtypeStruct((users, quarter, wid...  13.6 us
    all_to_all x1, starting transfers between devices, per_device(): lax.all_to_all(done.reshape((-1,) + done.shape[2:]), ('dp', 'mp'), split_...  7.81 us
  transfers between devices with their start and end apart: 26, of which 6 were waited for; matrix products, arithmetic and copies ran while one was open for 8% of the time, Pallas kernels for 20%

profile of v5, /device:TPU:1, one launch (start us, length us, event | category | flops | bytes accessed | tf_op | source)
XLA Modules:
  0.0 221.5 jit_solution(4926911750648331603)
XLA Ops:
  0.0 0.8 compare_select_fusion.13
  3.0 1.6 copy-done.1
  5.9 1.0 copy-done.4
  6.9 9.7 %all-to-all-start = ((bf16[32,80,256]{2,1,0:T(8,128)(2,1)}), bf16[32,80,256]{2,1,0:T(8,128)(2,1)S(1)}, u32[]{:S(2)}, u32[]{:S(2)}) async-start(bf16[32,80,256]{2,1,0:T(8,128)(2,1)} %copy-done.4), calls=%async_computation | async-start | bytes 2621440 | tf_op jit(solution)/shard_map/all_to_all | solution.py:497
  16.7 2.8 %collective-permute-start.7 = (bf16[256,1024]{1,0:T(8,128)(2,1)}, bf16[256,1024]{1,0:T(8,128)(2,1)}, u32[]{:S(2)}, u32[]{:S(2)}) collective-permute-start(bf16[256,1024]{1,0:T(8,128)(2,1)} %refs_12_.7), channel_id=1, source_target_pairs={{0,2},{1,3},{2,0},{3,1},{4,6},{5,7},{6,4},{7,5},{8,10},{9,11},{10,... | collective-permute-start | bytes 1572872 | tf_op jit(solution)/shard_map/ppermute | solution.py:502
  19.8 2.4 %collective-permute-start.8 = (bf16[256,1024]{1,0:T(8,128)(2,1)}, bf16[256,1024]{1,0:T(8,128)(2,1)}, u32[]{:S(2)}, u32[]{:S(2)}) collective-permute-start(bf16[256,1024]{1,0:T(8,128)(2,1)} %refs_12_.7), channel_id=1, source_target_pairs={{0,3},{1,0},{2,1},{3,2},{4,7},{5,4},{6,5},{7,6},{8,11},{9,8},{10,9... | collective-permute-start | bytes 1572872 | tf_op jit(solution)/shard_map/ppermute | solution.py:502
  24.2 12.3 %all-to-all-done.refs_0_ = bf16[32,80,256]{2,1,0:T(8,128)(2,1)S(1)} async-done(((bf16[32,80,256]{2,1,0:T(8,128)(2,1)}), bf16[32,80,256]{2,1,0:T(8,128)(2,1)S(1)}, u32[]{:S(2)}, u32[]{:S(2)}) %all-to-all-start) | async-done | bytes 1310752 | tf_op jit(solution)/shard_map/all_to_all | solution.py:497
  37.9 1.1 copy-done.3
  39.0 4.0 %all-to-all-start.1 = ((bf16[32,80,256]{2,1,0:T(8,128)(2,1)}), bf16[32,80,256]{2,1,0:T(8,128)(2,1)S(1)}, u32[]{:S(2)}, u32[]{:S(2)}) async-start(bf16[32,80,256]{2,1,0:T(8,128)(2,1)} %copy-done.3), calls=%async_computation.1 | async-start | bytes 2621440 | tf_op jit(solution)/shard_map/all_to_all | solution.py:497
  43.0 1.6 copy-done.2
  45.2 1.0 copy-done.5
  46.3 2.0 gather_fusion.2
  51.1 1.3 broadcast_in_dim.394
  52.4 1.8 stack.8.refs_5_.refs_9_
  54.2 3.2 %bitcast_select_fusion.refs_4_.refs_8_ = bf16[1024,1024]{1,0:T(8,128)(2,1)} fusion(bf16[4,256,1024]{2,1,0:T(8,128)(2,1)} %gather_fusion.2, pred[1024]{0:T(1024)(128)(4,1)S(1)} %broadcast_in_dim.400), kind=kLoop, calls=%fused_computation.3 | loop fusion | flops 1048576 | bytes 4195328 | tf_op jit(solution)/shard_map/jit(_take)/select_n | solution.py:564
  57.4 5.5 %all-to-all-done.1.src = bf16[32,80,256]{2,1,0:T(8,128)(2,1)S(1)} async-done(((bf16[32,80,256]{2,1,0:T(8,128)(2,1)}), bf16[32,80,256]{2,1,0:T(8,128)(2,1)S(1)}, u32[]{:S(2)}, u32[]{:S(2)}) %all-to-all-start.1) | async-done | bytes 1310752 | tf_op jit(solution)/shard_map/all_to_all | solution.py:497
  63.0 0.8 copy-done.6
  63.7 0.8 copy-done.8
  64.5 4.6 %all-to-all-start.2 = ((bf16[32,64,256]{2,1,0:T(8,128)(2,1)}), bf16[32,64,256]{2,1,0:T(8,128)(2,1)}, u32[]{:S(2)}, u32[]{:S(2)}) async-start(bf16[32,64,256]{2,1,0:T(8,128)(2,1)} %copy-done.5), calls=%async_computation.2 | async-start | bytes 2097152 | tf_op jit(solution)/shard_map/all_to_all | solution.py:497
  69.2 2.5 %collective-permute-start.13 = (bf16[16,64,256]{2,1,0:T(8,128)(2,1)}, bf16[16,64,256]{2,1,0:T(8,128)(2,1)}, u32[]{:S(2)}, u32[]{:S(2)}) collective-permute-start(bf16[16,64,256]{2,1,0:T(8,128)(2,1)} %copy-done.6), channel_id=1, source_target_pairs={{0,3},{1,0},{2,1},{3,2},{4,7},{5,4},{6,5},{7,6},{8,11},{9,8},{10,9... | collective-permute-start | bytes 1572872 | tf_op jit(solution)/shard_map/ppermute | solution.py:502
  71.7 2.7 %collective-permute-start.22 = (bf16[16,64,256]{2,1,0:T(8,128)(2,1)}, bf16[16,64,256]{2,1,0:T(8,128)(2,1)}, u32[]{:S(2)}, u32[]{:S(2)}) collective-permute-start(bf16[16,64,256]{2,1,0:T(8,128)(2,1)} %copy-done.8), channel_id=1, source_target_pairs={{0,3},{1,0},{2,1},{3,2},{4,7},{5,4},{6,5},{7,6},{8,11},{9,8},{10,9... | collective-permute-start | bytes 1572872 | tf_op jit(solution)/shard_map/ppermute | solution.py:502
  75.1 11.2 %all-to-all-done.2.refs_0_ = bf16[32,64,256]{2,1,0:T(8,128)(2,1)} async-done(((bf16[32,64,256]{2,1,0:T(8,128)(2,1)}), bf16[32,64,256]{2,1,0:T(8,128)(2,1)}, u32[]{:S(2)}, u32[]{:S(2)}) %all-to-all-start.2) | async-done | bytes 1048608 | tf_op jit(solution)/shard_map/all_to_all | solution.py:497
  86.2 2.3 %shard_map.95 = bf16[32,64,256]{2,1,0:T(8,128)(2,1)} custom-call(s32[32]{0:T(128)S(1)} %select_reduce_fusion.5.index_ref, bf16[32,64,256]{2,1,0:T(8,128)(2,1)} %all-to-all-done.2.refs_0_), custom_call_target="tpu_custom_call" | custom-call | tf_op jit(solution)/shard_map/pallas_call | solution.py:68
  88.5 4.6 %all-to-all-start.3 = ((bf16[32,64,256]{2,1,0:T(8,128)(2,1)}), bf16[32,64,256]{2,1,0:T(8,128)(2,1)}, u32[]{:S(2)}, u32[]{:S(2)}) async-start(bf16[32,64,256]{2,1,0:T(8,128)(2,1)} %shard_map.95), calls=%async_computation.3 | async-start | bytes 2097152 | tf_op jit(solution)/shard_map/all_to_all | solution.py:497
  94.5 1.3 collective-permute-start.12
  95.8 1.8 collective-permute-start.23
  97.7 12.4 %all-to-all-done.3.rows_ref = bf16[32,64,256]{2,1,0:T(8,128)(2,1)} async-done(((bf16[32,64,256]{2,1,0:T(8,128)(2,1)}), bf16[32,64,256]{2,1,0:T(8,128)(2,1)}, u32[]{:S(2)}, u32[]{:S(2)}) %all-to-all-start.3) | async-done | bytes 1048608 | tf_op jit(solution)/shard_map/all_to_all | solution.py:497
  110.1 2.1 shard_map.96
  112.1 1.2 collective-permute-start.9
  113.4 1.5 collective-permute-start.10
  114.9 0.8 copy-done.10
  115.7 1.0 copy-done.11
  116.7 10.0 %shard_map.97 = (bf16[32,16,256]{2,1,0:T(8,128)(2,1)S(1)}, bf16[32,16,256]{2,1,0:T(8,128)(2,1)}, bf16[32,16,256]{2,1,0:T(8,128)(2,1)S(1)}, bf16[32,16,256]{2,1,0:T(8,128)(2,1)S(1)}) custom-call(s32[32]{0:T(128)S(1)} %select_reduce_fusion.4.order_ref, s32[1]{0:T(128)} %bitcast.9.rank_ref, bf16[16,64,256]{2,1,0:T(8,128)(2,1)S(1)} %copy-done.7, ...), custom_call_target="tpu_custom_call" | custom-call | tf_op jit(solution)/shard_map/pallas_call | solution.py:206
  126.7 1.2 collective-permute-start.17
  128.2 2.6 %collective-permute-start.16 = (bf16[544,256]{1,0:T(8,128)(2,1)}, bf16[544,256]{1,0:T(8,128)(2,1)}, u32[]{:S(2)}, u32[]{:S(2)}) collective-permute-start(bf16[544,256]{1,0:T(8,128)(2,1)} %collective-permute-done.10.refs_7_), channel_id=1, source_target_pairs={{0,3},{1,0},{2,1},{3,2},{4,7},{5,4},{6,5},{7,6},{8,11},{9,8},{10,9... | collective-permute-start | bytes 835592 | tf_op jit(solution)/shard_map/ppermute | solution.py:502
  130.9 8.7 %shard_map.99 = (bf16[32,16,256]{2,1,0:T(8,128)(2,1)S(1)}, bf16[32,16,256]{2,1,0:T(8,128)(2,1)}, bf16[32,16,256]{2,1,0:T(8,128)(2,1)S(1)}, bf16[32,16,256]{2,1,0:T(8,128)(2,1)S(1)}) custom-call(s32[32]{0:T(128)S(1)} %select_reduce_fusion.4.order_ref, s32[1]{0:T(128)} %bitcast.9.rank_ref, ...), custom_call_target="tpu_custom_call", output_to_operand_aliasing={{0}: (16, {}), {1}: (17, {}), {2}: (18, {}), {3}: (19, {})} | custom-call | tf_op jit(solution)/shard_map/pallas_call | solution.py:206
  142.2 2.5 %collective-permute-start.25 = (bf16[32,16,256]{2,1,0:T(8,128)(2,1)}, bf16[32,16,256]{2,1,0:T(8,128)(2,1)}, u32[]{:S(2)}, u32[]{:S(2)}) collective-permute-start(bf16[32,16,256]{2,1,0:T(8,128)(2,1)} %copy-done.15), channel_id=1, source_target_pairs={{0,2},{1,3},{2,0},{3,1},{4,6},{5,7},{6,4},{7,5},{8,10},{9,11},{10,... | collective-permute-start | bytes 786440 | tf_op jit(solution)/shard_map/ppermute | solution.py:502
  145.4 13.6 %shard_map.98 = (bf16[32,16,256]{2,1,0:T(8,128)(2,1)S(1)}, bf16[32,16,256]{2,1,0:T(8,128)(2,1)}, bf16[32,16,256]{2,1,0:T(8,128)(2,1)}, bf16[32,16,256]{2,1,0:T(8,128)(2,1)}) custom-call(s32[32]{0:T(128)S(1)} %get-tuple-element.135.order_ref, s32[32]{0:T(128)S(1)} %broadcast_minimum_fusion.offsets_ref, s32[32]{0:T(128)S(1)} %get-tuple-element.137.slots_ref.seats_ref, ...), custom_call_target="tpu_custom_call" | custom-call | tf_op jit(solution)/shard_map/pallas_call | solution.py:321
  159.7 0.8 collective-permute-start.18
  160.5 1.2 collective-permute-start.19
  161.7 2.1 collective-permute-start.20
  165.3 1.0 copy-done.12
  166.4 0.9 copy-done.14
  167.3 6.0 %shard_map.100.refs_16_ = bf16[32,4,2,16,256]{4,3,2,1,0:T(8,128)(2,1)} custom-call(s32[33]{0:T(128)S(1)} %pad_add_fusion.1.scalar_ref, bf16[16,64,256]{2,1,0:T(8,128)(2,1)S(1)} %copy-done.7, bf16[16,64,256]{2,1,0:T(8,128)(2,1)} %collective-permute-done.11.refs_1_, bf16[16,64,256]{2,1,0:T(8,128)(2,1)S(1)} %copy-done.12, ...), custom_call_target="tpu_custom_call" | custom-call | tf_op jit(solution)/shard_map/pallas_call | solution.py:383
  173.5 6.0 %shard_map.101 = bf16[32,4,2,16,256]{4,3,2,1,0:T(8,128)(2,1)} custom-call(s32[33]{0:T(128)S(1)} %pad_add_fusion.scalar_ref, s32[32]{0:T(128)S(1)} %get-tuple-element.137.slots_ref.seats_ref, s32[32]{0:T(128)S(1)} %broadcast_minimum_fusion.offsets_ref, bf16[544,256]{1,0:T(8,128)(2,1)S(1)} %get-tuple-element.91.refs_0_, ...), custom_call_target="tpu_custom_call", output_to_operand_aliasing={{}: (19, {})} | custom-call | tf_op jit(solution)/shard_map/pallas_call | solution.py:440
  179.6 7.8 %all-to-all-start.4 = ((bf16[128,2,16,256]{3,2,1,0:T(8,128)(2,1)}), bf16[128,2,16,256]{3,2,1,0:T(8,128)(2,1)}, u32[]{:S(2)}, u32[]{:S(2)}) async-start(bf16[128,2,16,256]{3,2,1,0:T(8,128)(2,1)} %bitcast.11), calls=%async_computation.4 | async-start | bytes 4194304 | tf_op jit(solution)/shard_map/all_to_all | solution.py:633
  187.6 30.6 %all-to-all-done.4 = bf16[128,2,16,256]{3,2,1,0:T(8,128)(2,1)} async-done(((bf16[128,2,16,256]{3,2,1,0:T(8,128)(2,1)}), bf16[128,2,16,256]{3,2,1,0:T(8,128)(2,1)}, u32[]{:S(2)}, u32[]{:S(2)}) %all-to-all-start.4) | async-done | bytes 2097184 | tf_op jit(solution)/shard_map/all_to_all | solution.py:633
  218.2 3.2 %shard_map.102 = bf16[32,128,256]{2,1,0:T(8,128)(2,1)} custom-call(s32[32]{0:T(128)S(1)} %broadcast_subtract_fusion.index_ref, bf16[32,4,2,16,256]{4,3,2,1,0:T(8,128)(2,1)} %bitcast.12.src), custom_call_target="tpu_custom_call" | custom-call | tf_op jit(solution)/shard_map/pallas_call | solution.py:37
  (114 shorter events, 18.0 us)
Async XLA Ops:
  0.0 46.3 %copy-start = (bf16[1024,1024]{1,0:T(8,128)(2,1)S(1)}, bf16[1024,1024]{1,0:T(8,128)(2,1)}, u32[]{:S(2)}) copy-start(bf16[1024,1024]{1,0:T(8,128)(2,1)} %param.17) | copy-start | bytes 6291460
  3.0 1.6 copy-start.1
  5.9 1.1 copy-start.4
  6.9 15.5 %copy-start.21 = (s32[32]{0:T(128)S(1)}, s32[32]{0:T(128)}, u32[]{:S(2)}) copy-start(s32[32]{0:T(128)} %param.16) | copy-start | bytes 388
  6.9 16.2 %copy-start.27 = (f32[2,16]{1,0:T(2,128)S(1)}, f32[2,16]{1,0:T(2,128)}, u32[]{:S(2)}) copy-start(f32[2,16]{1,0:T(2,128)} %param.18) | copy-start | bytes 388
  6.9 29.5 %all-to-all-start = ((bf16[32,80,256]{2,1,0:T(8,128)(2,1)}), bf16[32,80,256]{2,1,0:T(8,128)(2,1)S(1)}, u32[]{:S(2)}, u32[]{:S(2)}) async-start(bf16[32,80,256]{2,1,0:T(8,128)(2,1)} %copy-done.4), calls=%async_computation | async-start | bytes 2621440 | tf_op jit(solution)/shard_map/all_to_all | solution.py:497
  16.7 47.9 %collective-permute-start.7 = (bf16[256,1024]{1,0:T(8,128)(2,1)}, bf16[256,1024]{1,0:T(8,128)(2,1)}, u32[]{:S(2)}, u32[]{:S(2)}) collective-permute-start(bf16[256,1024]{1,0:T(8,128)(2,1)} %refs_12_.7), channel_id=1, source_target_pairs={{0,2},{1,3},{2,0},{3,1},{4,6},{5,7},{6,4},{7,5},{8,10},{9,11},{10,... | collective-permute-start | bytes 1572872 | tf_op jit(solution)/shard_map/ppermute | solution.py:502
  19.5 45.0 %collective-permute-start.6 = (bf16[256,1024]{1,0:T(8,128)(2,1)}, bf16[256,1024]{1,0:T(8,128)(2,1)}, u32[]{:S(2)}, u32[]{:S(2)}) collective-permute-start(bf16[256,1024]{1,0:T(8,128)(2,1)} %refs_12_.7), channel_id=1, source_target_pairs={{0,1},{1,2},{2,3},{3,0},{4,5},{5,6},{6,7},{7,4},{8,9},{9,10},{10,1... | collective-permute-start | bytes 1572872 | tf_op jit(solution)/shard_map/ppermute | solution.py:502
  19.8 44.7 %collective-permute-start.8 = (bf16[256,1024]{1,0:T(8,128)(2,1)}, bf16[256,1024]{1,0:T(8,128)(2,1)}, u32[]{:S(2)}, u32[]{:S(2)}) collective-permute-start(bf16[256,1024]{1,0:T(8,128)(2,1)} %refs_12_.7), channel_id=1, source_target_pairs={{0,3},{1,0},{2,1},{3,2},{4,7},{5,4},{6,5},{7,6},{8,11},{9,8},{10,9... | collective-permute-start | bytes 1572872 | tf_op jit(solution)/shard_map/ppermute | solution.py:502
  37.9 1.1 copy-start.3
  39.0 23.9 %all-to-all-start.1 = ((bf16[32,80,256]{2,1,0:T(8,128)(2,1)}), bf16[32,80,256]{2,1,0:T(8,128)(2,1)S(1)}, u32[]{:S(2)}, u32[]{:S(2)}) async-start(bf16[32,80,256]{2,1,0:T(8,128)(2,1)} %copy-done.3), calls=%async_computation.1 | async-start | bytes 2621440 | tf_op jit(solution)/shard_map/all_to_all | solution.py:497
  43.0 1.6 copy-start.2
  45.2 1.0 copy-start.5
  62.9 0.8 copy-start.6
  63.7 0.8 copy-start.8
  64.5 21.7 %all-to-all-start.2 = ((bf16[32,64,256]{2,1,0:T(8,128)(2,1)}), bf16[32,64,256]{2,1,0:T(8,128)(2,1)}, u32[]{:S(2)}, u32[]{:S(2)}) async-start(bf16[32,64,256]{2,1,0:T(8,128)(2,1)} %copy-done.5), calls=%async_computation.2 | async-start | bytes 2097152 | tf_op jit(solution)/shard_map/all_to_all | solution.py:497
  69.2 44.2 %collective-permute-start.13 = (bf16[16,64,256]{2,1,0:T(8,128)(2,1)}, bf16[16,64,256]{2,1,0:T(8,128)(2,1)}, u32[]{:S(2)}, u32[]{:S(2)}) collective-permute-start(bf16[16,64,256]{2,1,0:T(8,128)(2,1)} %copy-done.6), channel_id=1, source_target_pairs={{0,3},{1,0},{2,1},{3,2},{4,7},{5,4},{6,5},{7,6},{8,11},{9,8},{10,9... | collective-permute-start | bytes 1572872 | tf_op jit(solution)/shard_map/ppermute | solution.py:502
  71.7 22.8 %collective-permute-start.11 = (bf16[16,64,256]{2,1,0:T(8,128)(2,1)}, bf16[16,64,256]{2,1,0:T(8,128)(2,1)}, u32[]{:S(2)}, u32[]{:S(2)}) collective-permute-start(bf16[16,64,256]{2,1,0:T(8,128)(2,1)} %copy-done.6), channel_id=1, source_target_pairs={{0,1},{1,2},{2,3},{3,0},{4,5},{5,6},{6,7},{7,4},{8,9},{9,10},{10,1... | collective-permute-start | bytes 1572872 | tf_op jit(solution)/shard_map/ppermute | solution.py:502
  71.7 24.1 %collective-permute-start.22 = (bf16[16,64,256]{2,1,0:T(8,128)(2,1)}, bf16[16,64,256]{2,1,0:T(8,128)(2,1)}, u32[]{:S(2)}, u32[]{:S(2)}) collective-permute-start(bf16[16,64,256]{2,1,0:T(8,128)(2,1)} %copy-done.8), channel_id=1, source_target_pairs={{0,3},{1,0},{2,1},{3,2},{4,7},{5,4},{6,5},{7,6},{8,11},{9,8},{10,9... | collective-permute-start | bytes 1572872 | tf_op jit(solution)/shard_map/ppermute | solution.py:502
  74.4 53.8 %collective-permute-start.21 = (bf16[16,64,256]{2,1,0:T(8,128)(2,1)}, bf16[16,64,256]{2,1,0:T(8,128)(2,1)}, u32[]{:S(2)}, u32[]{:S(2)}) collective-permute-start(bf16[16,64,256]{2,1,0:T(8,128)(2,1)} %copy-done.8), channel_id=1, source_target_pairs={{0,1},{1,2},{2,3},{3,0},{4,5},{5,6},{6,7},{7,4},{8,9},{9,10},{10,1... | collective-permute-start | bytes 1572872 | tf_op jit(solution)/shard_map/ppermute | solution.py:502
  88.5 27.2 %copy-start.7 = (bf16[16,64,256]{2,1,0:T(8,128)(2,1)S(1)}, bf16[16,64,256]{2,1,0:T(8,128)(2,1)}, u32[]{:S(2)}) copy-start(bf16[16,64,256]{2,1,0:T(8,128)(2,1)} %copy-done.6) | copy-start | bytes 1572868
  88.5 21.6 %all-to-all-start.3 = ((bf16[32,64,256]{2,1,0:T(8,128)(2,1)}), bf16[32,64,256]{2,1,0:T(8,128)(2,1)}, u32[]{:S(2)}, u32[]{:S(2)}) async-start(bf16[32,64,256]{2,1,0:T(8,128)(2,1)} %shard_map.95), calls=%async_computation.3 | async-start | bytes 2097152 | tf_op jit(solution)/shard_map/all_to_all | solution.py:497
  94.5 20.3 %collective-permute-start.12 = (bf16[16,64,256]{2,1,0:T(8,128)(2,1)}, bf16[16,64,256]{2,1,0:T(8,128)(2,1)S(1)}, u32[]{:S(2)}, u32[]{:S(2)}) collective-permute-start(bf16[16,64,256]{2,1,0:T(8,128)(2,1)} %collective-permute-done.11.refs_1_), channel_id=1, source_target_pairs={{0,1},{1,2},{2,3},{3,0},{4,5},{5,6},{6,7},{7,4},{8,9},{9,10},{10,1... | collective-permute-start | bytes 1572872 | tf_op jit(solution)/shard_map/ppermute | solution.py:502
  95.8 35.0 %collective-permute-start.23 = (bf16[16,64,256]{2,1,0:T(8,128)(2,1)}, bf16[16,64,256]{2,1,0:T(8,128)(2,1)}, u32[]{:S(2)}, u32[]{:S(2)}) collective-permute-start(bf16[16,64,256]{2,1,0:T(8,128)(2,1)} %collective-permute-done.22.refs_3_.refs_7_), channel_id=1, source_target_pairs={{0,3},{1,0},{2,1},{3,2},{4,7},{5,4},{6,5},{7,6},{8,11},{9,8},{10,9... | collective-permute-start | bytes 1572872 | tf_op jit(solution)/shard_map/ppermute | solution.py:502
  112.1 15.8 %collective-permute-start.9 = (bf16[544,256]{1,0:T(8,128)(2,1)S(1)}, bf16[544,256]{1,0:T(8,128)(2,1)}, u32[]{:S(2)}, u32[]{:S(2)}) collective-permute-start(bf16[544,256]{1,0:T(8,128)(2,1)S(1)} %get-tuple-element.91.refs_0_), channel_id=1, source_target_pairs={{0,1},{1,2},{2,3},{3,0},{4,5},{5,6},{6,7},{7,4},{8,9},{9,10},{10,1... | collective-permute-start | bytes 835592 | tf_op jit(solution)/shard_map/ppermute | solution.py:502
  113.4 14.8 %collective-permute-start.10 = (bf16[544,256]{1,0:T(8,128)(2,1)}, bf16[544,256]{1,0:T(8,128)(2,1)}, u32[]{:S(2)}, u32[]{:S(2)}) collective-permute-start(bf16[544,256]{1,0:T(8,128)(2,1)} %get-tuple-element.92.refs_1_), channel_id=1, source_target_pairs={{0,3},{1,0},{2,1},{3,2},{4,7},{5,4},{6,5},{7,6},{8,11},{9,8},{10,9... | collective-permute-start | bytes 835592 | tf_op jit(solution)/shard_map/ppermute | solution.py:502
  114.9 0.8 copy-start.10
  115.7 1.0 copy-start.11
  116.7 14.1 %copy-start.9 = (bf16[16,64,256]{2,1,0:T(8,128)(2,1)S(1)}, bf16[16,64,256]{2,1,0:T(8,128)(2,1)}, u32[]{:S(2)}) copy-start(bf16[16,64,256]{2,1,0:T(8,128)(2,1)} %copy-done.8) | copy-start | bytes 1572868
  116.7 14.1 %copy-start.22 = (bf16[1024,1024]{1,0:T(8,128)(2,1)S(1)}, bf16[1024,1024]{1,0:T(8,128)(2,1)}, u32[]{:S(2)}) copy-start(bf16[1024,1024]{1,0:T(8,128)(2,1)} %bitcast_select_fusion.refs_4_.refs_8_) | copy-start | bytes 6291460
  116.7 14.1 %copy-start.23 = (f32[32,8,256]{2,1,0:T(8,128)S(1)}, f32[32,8,256]{2,1,0:T(8,128)}, u32[]{:S(2)}) copy-start(f32[32,8,256]{2,1,0:T(8,128)} %stack.8.refs_5_.refs_9_) | copy-start | bytes 786436
  126.7 15.6 %collective-permute-start.17 = (bf16[544,256]{1,0:T(8,128)(2,1)S(1)}, bf16[544,256]{1,0:T(8,128)(2,1)}, u32[]{:S(2)}, u32[]{:S(2)}) collective-permute-start(bf16[544,256]{1,0:T(8,128)(2,1)S(1)} %get-tuple-element.91.refs_0_), channel_id=1, source_target_pairs={{0,3},{1,0},{2,1},{3,2},{4,7},{5,4},{6,5},{7,6},{8,11},{9,8},{10,9... | collective-permute-start | bytes 835592 | tf_op jit(solution)/shard_map/ppermute | solution.py:502
  127.9 16.8 %collective-permute-start.14 = (bf16[544,256]{1,0:T(8,128)(2,1)}, bf16[544,256]{1,0:T(8,128)(2,1)}, u32[]{:S(2)}, u32[]{:S(2)}) collective-permute-start(bf16[544,256]{1,0:T(8,128)(2,1)} %get-tuple-element.92.refs_1_), channel_id=1, source_target_pairs={{0,1},{1,2},{2,3},{3,0},{4,5},{5,6},{6,7},{7,4},{8,9},{9,10},{10,1... | collective-permute-start | bytes 835592 | tf_op jit(solution)/shard_map/ppermute | solution.py:502
  128.2 17.2 %collective-permute-start.15 = (bf16[544,256]{1,0:T(8,128)(2,1)}, bf16[544,256]{1,0:T(8,128)(2,1)}, u32[]{:S(2)}, u32[]{:S(2)}) collective-permute-start(bf16[544,256]{1,0:T(8,128)(2,1)} %collective-permute-done.9.refs_2_), channel_id=1, source_target_pairs={{0,1},{1,2},{2,3},{3,0},{4,5},{5,6},{6,7},{7,4},{8,9},{9,10},{10,1... | collective-permute-start | bytes 835592 | tf_op jit(solution)/shard_map/ppermute | solution.py:502
  128.2 17.1 %collective-permute-start.16 = (bf16[544,256]{1,0:T(8,128)(2,1)}, bf16[544,256]{1,0:T(8,128)(2,1)}, u32[]{:S(2)}, u32[]{:S(2)}) collective-permute-start(bf16[544,256]{1,0:T(8,128)(2,1)} %collective-permute-done.10.refs_7_), channel_id=1, source_target_pairs={{0,3},{1,0},{2,1},{3,2},{4,7},{5,4},{6,5},{7,6},{8,11},{9,8},{10,9... | collective-permute-start | bytes 835592 | tf_op jit(solution)/shard_map/ppermute | solution.py:502
  141.0 0.7 copy-start.16
  141.7 20.0 %collective-permute-start.24 = (bf16[32,16,256]{2,1,0:T(8,128)(2,1)}, bf16[32,16,256]{2,1,0:T(8,128)(2,1)}, u32[]{:S(2)}, u32[]{:S(2)}) collective-permute-start(bf16[32,16,256]{2,1,0:T(8,128)(2,1)} %get-tuple-element.116), channel_id=1, source_target_pairs={{0,1},{1,2},{2,3},{3,0},{4,5},{5,6},{6,7},{7,4},{8,9},{9,10},{10,1... | collective-permute-start | bytes 786440 | tf_op jit(solution)/shard_map/ppermute | solution.py:502
  142.2 23.1 %collective-permute-start.25 = (bf16[32,16,256]{2,1,0:T(8,128)(2,1)}, bf16[32,16,256]{2,1,0:T(8,128)(2,1)}, u32[]{:S(2)}, u32[]{:S(2)}) collective-permute-start(bf16[32,16,256]{2,1,0:T(8,128)(2,1)} %copy-done.15), channel_id=1, source_target_pairs={{0,2},{1,3},{2,0},{3,1},{4,6},{5,7},{6,4},{7,5},{8,10},{9,11},{10,... | collective-permute-start | bytes 786440 | tf_op jit(solution)/shard_map/ppermute | solution.py:502
  144.7 20.6 %collective-permute-start.26 = (bf16[32,16,256]{2,1,0:T(8,128)(2,1)}, bf16[32,16,256]{2,1,0:T(8,128)(2,1)}, u32[]{:S(2)}, u32[]{:S(2)}) collective-permute-start(bf16[32,16,256]{2,1,0:T(8,128)(2,1)} %copy-done.16), channel_id=1, source_target_pairs={{0,3},{1,0},{2,1},{3,2},{4,7},{5,4},{6,5},{7,6},{8,11},{9,8},{10,9... | collective-permute-start | bytes 786440 | tf_op jit(solution)/shard_map/ppermute | solution.py:502
  159.7 13.7 %collective-permute-start.18 = (bf16[32,16,256]{2,1,0:T(8,128)(2,1)}, bf16[32,16,256]{2,1,0:T(8,128)(2,1)}, u32[]{:S(2)}, u32[]{:S(2)}) collective-permute-start(bf16[32,16,256]{2,1,0:T(8,128)(2,1)} %get-tuple-element.103), channel_id=1, source_target_pairs={{0,1},{1,2},{2,3},{3,0},{4,5},{5,6},{6,7},{7,4},{8,9},{9,10},{10,1... | collective-permute-start | bytes 786440 | tf_op jit(solution)/shard_map/ppermute | solution.py:502
  160.5 12.9 %collective-permute-start.19 = (bf16[32,16,256]{2,1,0:T(8,128)(2,1)}, bf16[32,16,256]{2,1,0:T(8,128)(2,1)}, u32[]{:S(2)}, u32[]{:S(2)}) collective-permute-start(bf16[32,16,256]{2,1,0:T(8,128)(2,1)} %get-tuple-element.104), channel_id=1, source_target_pairs={{0,2},{1,3},{2,0},{3,1},{4,6},{5,7},{6,4},{7,5},{8,10},{9,11},{10,... | collective-permute-start | bytes 786440 | tf_op jit(solution)/shard_map/ppermute | solution.py:502
  161.7 11.8 %collective-permute-start.20 = (bf16[32,16,256]{2,1,0:T(8,128)(2,1)}, bf16[32,16,256]{2,1,0:T(8,128)(2,1)}, u32[]{:S(2)}, u32[]{:S(2)}) collective-permute-start(bf16[32,16,256]{2,1,0:T(8,128)(2,1)} %get-tuple-element.105), channel_id=1, source_target_pairs={{0,3},{1,0},{2,1},{3,2},{4,7},{5,4},{6,5},{7,6},{8,11},{9,8},{10,9... | collective-permute-start | bytes 786440 | tf_op jit(solution)/shard_map/ppermute | solution.py:502
  165.3 1.0 copy-start.12
  166.4 0.9 copy-start.14
  167.3 6.2 %copy-start.18 = (bf16[32,16,256]{2,1,0:T(8,128)(2,1)S(1)}, bf16[32,16,256]{2,1,0:T(8,128)(2,1)}, u32[]{:S(2)}) copy-start(bf16[32,16,256]{2,1,0:T(8,128)(2,1)} %copy-done.17) | copy-start | bytes 786436
  167.3 6.2 %copy-start.25 = (bf16[256,1024]{1,0:T(8,128)(2,1)S(1)}, bf16[256,1024]{1,0:T(8,128)(2,1)}, u32[]{:S(2)}) copy-start(bf16[256,1024]{1,0:T(8,128)(2,1)} %refs_12_.7) | copy-start | bytes 1572868
  173.5 6.0 %copy-start.24 = (f32[32,8,256]{2,1,0:T(8,128)S(1)}, f32[32,8,256]{2,1,0:T(8,128)}, u32[]{:S(2)}) copy-start(f32[32,8,256]{2,1,0:T(8,128)} %stack.8.refs_5_.refs_9_) | copy-start | bytes 786436
  179.6 38.6 %all-to-all-start.4 = ((bf16[128,2,16,256]{3,2,1,0:T(8,128)(2,1)}), bf16[128,2,16,256]{3,2,1,0:T(8,128)(2,1)}, u32[]{:S(2)}, u32[]{:S(2)}) async-start(bf16[128,2,16,256]{3,2,1,0:T(8,128)(2,1)} %bitcast.11), calls=%async_computation.4 | async-start | bytes 4194304 | tf_op jit(solution)/shard_map/all_to_all | solution.py:633
  (4 other events, 2.8 us)

commit v6 on v5

--- a/solution.py
+++ b/solution.py
@@ -79,16 +79,24 @@
     users, _, width = rows.shape
     half = users // 2
 
-    def body(src, *outs):
-        for n in range(2):
-            for i in range(half):
-                outs[n][i] = src[n * half + i, :size, :]
-
-    return pl.pallas_call(
-        body,
-        out_shape=[jax.ShapeDtypeStruct((half, size, width), rows.dtype)] * 2,
+    def body(src, low, high, sem):
+        copies = [
+            pltpu.make_async_copy(
+                src.at[pl.ds(n * half, half), pl.ds(0, size)], (low, high)[n], sem.at[n]
+            )
+            for n in range(2)
+        ]
+        for copy in copies:
+            copy.start()
+        for copy in copies:
+            copy.wait()
+
+    return pl.pallas_call(
+        body,
+        out_shape=[pltpu.HBM((half, size, width), rows.dtype)] * 2,
         in_specs=[pl.BlockSpec(memory_space=pltpu.VMEM)],
-        out_specs=[pl.BlockSpec(memory_space=pltpu.VMEM)] * 2,
+        out_specs=[pl.BlockSpec(memory_space=pltpu.HBM)] * 2,
+        scratch_shapes=[pltpu.SemaphoreType.DMA((2,))],
         compiler_params=pltpu.CompilerParams(vmem_limit_bytes=VMEM),
     )(rows)
 
@@ -205,7 +213,7 @@
     at = len(inputs) - len(extra)
     return pl.pallas_call(
         body,
-        out_shape=[jax.ShapeDtypeStruct((users, quarter, width), jnp.bfloat16)] * mp,
+        out_shape=[pltpu.HBM((users, quarter, width), jnp.bfloat16)] * mp,
         grid_spec=pltpu.PrefetchScalarGridSpec(
             num_scalar_prefetch=2,
             grid=(some // BATCH,),
@@ -228,23 +236,32 @@
     users, count, width = rows.shape
     half = size // 2
 
-    def body(slots_ref, offsets_ref, rows_ref, low, high, buffer):
+    def body(slots_ref, offsets_ref, rows_ref, low, high, buffer, sem):
         for j in range(users):
             at = pl.multiple_of(offsets_ref[j], GROUP)
             buffer[pl.ds(at, count), :] = rows_ref[slots_ref[j]]
-        low[...] = buffer[:half, :]
-        high[...] = buffer[half:size, :]
-
-    return pl.pallas_call(
-        body,
-        out_shape=[jax.ShapeDtypeStruct((half, width), rows.dtype)] * 2,
+        copies = [
+            pltpu.make_async_copy(buffer.at[pl.ds(n * half, half)], (low, high)[n], sem.at[n])
+            for n in range(2)
+        ]
+        for copy in copies:
+            copy.start()
+        for copy in copies:
+            copy.wait()
+
+    return pl.pallas_call(
+        body,
+        out_shape=[pltpu.HBM((half, width), rows.dtype)] * 2,
         in_specs=[
             pl.BlockSpec(memory_space=pltpu.SMEM),
             pl.BlockSpec(memory_space=pltpu.SMEM),
             pl.BlockSpec(memory_space=pltpu.VMEM),
         ],
-        out_specs=[pl.BlockSpec(memory_space=pltpu.VMEM)] * 2,
-        scratch_shapes=[pltpu.VMEM((size + count, width), rows.dtype)],
+        out_specs=[pl.BlockSpec(memory_space=pltpu.HBM)] * 2,
+        scratch_shapes=[
+            pltpu.VMEM((size + count, width), rows.dtype),
+            pltpu.SemaphoreType.DMA((2,)),
+        ],
         compiler_params=pltpu.CompilerParams(vmem_limit_bytes=VMEM),
     )(slots, offsets, rows)
 
@@ -320,7 +337,7 @@
     width = heads * HD
     return pl.pallas_call(
         body,
-        out_shape=[jax.ShapeDtypeStruct((users, quarter, width), jnp.bfloat16)] * mp,
+        out_shape=[pltpu.HBM((users, quarter, width), jnp.bfloat16)] * mp,
         grid_spec=pltpu.PrefetchScalarGridSpec(
             num_scalar_prefetch=5,
             grid=(blocks + users // BATCH,),
@@ -402,65 +419,54 @@
 def project_out_packed(gated, full, weights, scalars, slots, offsets, piece, before):
     mp = len(gated)
     users, quarter, part = gated[0].shape
-    size = sum(array.shape[0] for array in full[0])
+    half = full[0][0].shape[0]
     out_part = weights[0].shape[1] // mp
     start = PIECES[piece][0]
-    count = sum(len(arrays) for arrays in full)
-
-    def column_of(k, rank):
-        return (rank + (mp - k)) % mp
 
     def body(scalar_ref, slots_ref, offsets_ref, *refs):
-        gated_refs, weight_refs = refs[count : count + mp], refs[count + mp : count + 2 * mp]
-        out_ref, whole = refs[-2], refs[-1]
+        full_refs, gated_refs = refs[: 2 * mp], refs[2 * mp : 3 * mp]
+        weight_refs = refs[3 * mp : 4 * mp]
+        out_ref, whole, store, sem = refs[-4:]
         rank = scalar_ref[0]
-        first = 0
-        for k, arrays in enumerate(full):
-
-            @pl.when(pl.program_id(0) == k)
-            def _():
-                at = 0
-                for n, array in enumerate(arrays):
-                    whole[at : at + array.shape[0], :] = refs[first + n][...]
-                    at = at + array.shape[0]
-
-            first = first + len(arrays)
-        acc = rank_dot(
-            [g[...].reshape(users * quarter, part) for g in gated_refs],
-            [w[...] for w in weight_refs],
-        )
+        rows = [g[...].reshape(users * quarter, part) for g in gated_refs]
         row = lax.broadcasted_iota(jnp.int32, (quarter, out_part), 0) + (start + rank * quarter)
-        for j in range(users):
-            at = jnp.minimum(offsets_ref[j] + rank * quarter, size - quarter)
-            residual = whole[pl.ds(pl.multiple_of(at, GROUP), quarter), :]
-            mine = acc[j * quarter : (j + 1) * quarter] + residual.astype(jnp.float32)
-            alive = row < scalar_ref[1 + j]
-            out_ref[slots_ref[j], 0, 0] = jnp.where(alive, mine, 0.0).astype(jnp.bfloat16)
-
+
+        def copy(k):
+            column = (rank + (mp - k)) % mp
+            return pltpu.make_async_copy(store.at[k], out_ref.at[:, column, piece], sem.at[k])
+
+        for k in range(mp):
+            whole[:half, :] = full_refs[2 * k][...]
+            whole[half:, :] = full_refs[2 * k + 1][...]
+            column = (rank + (mp - k)) % mp
+            first = pl.multiple_of(column * out_part, out_part)
+            acc = rank_dot(rows, [w[:, pl.ds(first, out_part)] for w in weight_refs])
+            for j in range(users):
+                at = jnp.minimum(offsets_ref[j] + rank * quarter, 2 * half - quarter)
+                residual = whole[pl.ds(pl.multiple_of(at, GROUP), quarter), :]
+                mine = acc[j * quarter : (j + 1) * quarter] + residual.astype(jnp.float32)
+                alive = row < scalar_ref[1 + j]
+                store[k, slots_ref[j]] = jnp.where(alive, mine, 0.0).astype(jnp.bfloat16)
+            copy(k).start()
+        for k in range(mp):
+            copy(k).wait()
+
+    arrays = [array for arrays in full for array in arrays]
     return pl.pallas_call(
         body,
         out_shape=jax.ShapeDtypeStruct((users, mp, len(PIECES), quarter, out_part), jnp.bfloat16),
-        grid_spec=pltpu.PrefetchScalarGridSpec(
-            num_scalar_prefetch=3,
-            grid=(mp,),
-            in_specs=[
-                pl.BlockSpec(array.shape, lambda i, *_: (0, 0)) for arrays in full for array in arrays
-            ]
-            + [pl.BlockSpec((users, quarter, part), lambda i, *_: (0, 0, 0)) for _ in gated]
-            + [
-                pl.BlockSpec((part, out_part), lambda i, s, *_: (0, column_of(i, s[0])))
-                for _ in weights
-            ]
-            + [pl.BlockSpec(memory_space=pl.ANY)],
-            out_specs=pl.BlockSpec(
-                (users, 1, 1, quarter, out_part),
-                lambda i, s, *_: (0, column_of(i, s[0]), piece, 0, 0),
-            ),
-            scratch_shapes=[pltpu.VMEM((size, part), jnp.bfloat16)],
-        ),
-        input_output_aliases={3 + count + 2 * mp: 0},
-        compiler_params=pltpu.CompilerParams(vmem_limit_bytes=VMEM),
-    )(scalars, slots, offsets, *sum(full, []), *gated, *weights, before)
+        in_specs=[pl.BlockSpec(memory_space=pltpu.SMEM)] * 3
+        + [pl.BlockSpec(memory_space=pltpu.VMEM)] * (4 * mp)
+        + [pl.BlockSpec(memory_space=pl.ANY)],
+        out_specs=pl.BlockSpec(memory_space=pl.ANY),
+        scratch_shapes=[
+            pltpu.VMEM((2 * half, part), jnp.bfloat16),
+            pltpu.VMEM((mp, users, quarter, out_part), jnp.bfloat16),
+            pltpu.SemaphoreType.DMA((mp,)),
+        ],
+        input_output_aliases={3 + 4 * mp: 0},
+        compiler_params=pltpu.CompilerParams(vmem_limit_bytes=VMEM),
+    )(scalars, slots, offsets, *arrays, *gated, *weights, before)
 
 
 def bucket_bias(distance, time_bias):

time: 223 us -> 219 us (0.982)
  local copies, waits for them, and re-layouts: 24.4 us -> 20.2 us
    unnamed x52 -> x42, local copies, waits for them, and re-layouts: 15.2 us -> 10.8 us
where the time goes in v6:
time: 219 us; the launch traced here: 217 us
  waiting for transfers between devices  71.8 us (33%)
  starting transfers between devices  59.9 us (27%)
  Pallas kernels  52.5 us (24%)
  local copies, waits for them, and re-layouts  20.2 us (9%)
  other arithmetic  11 us (5%)
    all_to_all x4, waiting for transfers between devices, exchange(): return lax.all_to_all(rows, 'dp', split_axis=0, concat_axis=0, tiled=True)  41.3 us
    all_to_all x1, waiting for transfers between devices, per_device(): lax.all_to_all(done.reshape((-1,) + done.shape[2:]), ('dp', 'mp'), split_...  30.4 us
    ppermute x21, starting transfers between devices, shifted(): lax.ppermute(array, 'mp', [(i, (i + k) % mp_size) for i in range(mp_size)])  27.9 us
    all_to_all x4, starting transfers between devices, exchange(): return lax.all_to_all(rows, 'dp', split_axis=0, concat_axis=0, tiled=True)  23 us
    pallas_call x2, Pallas kernels, attend(): pl.pallas_call(body, out_shape=[pltpu.HBM((users, quarter, width), jnp.bf...  18.7 us
    pallas_call x1, Pallas kernels, attend_packed(): pl.pallas_call(body, out_shape=[pltpu.HBM((users, quarter, width), jnp.bf...  12.7 us
    unnamed x42, local copies, waits for them, and re-layouts  10.8 us
    all_to_all x1, starting transfers between devices, per_device(): lax.all_to_all(done.reshape((-1,) + done.shape[2:]), ('dp', 'mp'), split_...  9.07 us
  transfers between devices with their start and end apart: 26, of which 6 were waited for; matrix products, arithmetic and copies ran while one was open for 8% of the time, Pallas kernels for 20%

profile of v6, /device:TPU:1, one launch (start us, length us, event | category | flops | bytes accessed | tf_op | source)
XLA Modules:
  0.0 217.4 jit_solution(3344236497866420466)
XLA Ops:
  0.0 0.8 compare_select_fusion.13
  3.0 1.6 copy-done.1
  5.9 1.0 copy-done.4
  6.9 9.7 %all-to-all-start = ((bf16[32,80,256]{2,1,0:T(8,128)(2,1)}), bf16[32,80,256]{2,1,0:T(8,128)(2,1)S(1)}, u32[]{:S(2)}, u32[]{:S(2)}) async-start(bf16[32,80,256]{2,1,0:T(8,128)(2,1)} %copy-done.4), calls=%async_computation | async-start | bytes 2621440 | tf_op jit(solution)/shard_map/all_to_all | solution.py:503
  16.7 2.8 %collective-permute-start.7 = (bf16[256,1024]{1,0:T(8,128)(2,1)}, bf16[256,1024]{1,0:T(8,128)(2,1)}, u32[]{:S(2)}, u32[]{:S(2)}) collective-permute-start(bf16[256,1024]{1,0:T(8,128)(2,1)} %refs_12_.7), channel_id=1, source_target_pairs={{0,2},{1,3},{2,0},{3,1},{4,6},{5,7},{6,4},{7,5},{8,10},{9,11},{10,... | collective-permute-start | bytes 1572872 | tf_op jit(solution)/shard_map/ppermute | solution.py:508
  19.8 2.4 %collective-permute-start.8 = (bf16[256,1024]{1,0:T(8,128)(2,1)}, bf16[256,1024]{1,0:T(8,128)(2,1)}, u32[]{:S(2)}, u32[]{:S(2)}) collective-permute-start(bf16[256,1024]{1,0:T(8,128)(2,1)} %refs_12_.7), channel_id=1, source_target_pairs={{0,3},{1,0},{2,1},{3,2},{4,7},{5,4},{6,5},{7,6},{8,11},{9,8},{10,9... | collective-permute-start | bytes 1572872 | tf_op jit(solution)/shard_map/ppermute | solution.py:508
  24.2 12.3 %all-to-all-done.refs_0_ = bf16[32,80,256]{2,1,0:T(8,128)(2,1)S(1)} async-done(((bf16[32,80,256]{2,1,0:T(8,128)(2,1)}), bf16[32,80,256]{2,1,0:T(8,128)(2,1)S(1)}, u32[]{:S(2)}, u32[]{:S(2)}) %all-to-all-start) | async-done | bytes 1310752 | tf_op jit(solution)/shard_map/all_to_all | solution.py:503
  37.9 1.1 copy-done.3
  39.0 4.0 %all-to-all-start.1 = ((bf16[32,80,256]{2,1,0:T(8,128)(2,1)}), bf16[32,80,256]{2,1,0:T(8,128)(2,1)S(1)}, u32[]{:S(2)}, u32[]{:S(2)}) async-start(bf16[32,80,256]{2,1,0:T(8,128)(2,1)} %copy-done.3), calls=%async_computation.1 | async-start | bytes 2621440 | tf_op jit(solution)/shard_map/all_to_all | solution.py:503
  43.0 1.6 copy-done.2
  45.2 1.0 copy-done.5
  46.3 2.0 gather_fusion.2
  51.2 1.3 broadcast_in_dim.394
  52.5 1.8 stack.8.refs_5_.refs_9_
  54.3 3.2 %bitcast_select_fusion.refs_4_.refs_8_ = bf16[1024,1024]{1,0:T(8,128)(2,1)} fusion(bf16[4,256,1024]{2,1,0:T(8,128)(2,1)} %gather_fusion.2, pred[1024]{0:T(1024)(128)(4,1)S(1)} %broadcast_in_dim.400), kind=kLoop, calls=%fused_computation.3 | loop fusion | flops 1048576 | bytes 4195328 | tf_op jit(solution)/shard_map/jit(_take)/select_n | solution.py:570
  57.4 5.4 %all-to-all-done.1.src = bf16[32,80,256]{2,1,0:T(8,128)(2,1)S(1)} async-done(((bf16[32,80,256]{2,1,0:T(8,128)(2,1)}), bf16[32,80,256]{2,1,0:T(8,128)(2,1)S(1)}, u32[]{:S(2)}, u32[]{:S(2)}) %all-to-all-start.1) | async-done | bytes 1310752 | tf_op jit(solution)/shard_map/all_to_all | solution.py:503
  62.9 1.0 shard_map.94
  64.0 4.6 %all-to-all-start.2 = ((bf16[32,64,256]{2,1,0:T(8,128)(2,1)}), bf16[32,64,256]{2,1,0:T(8,128)(2,1)}, u32[]{:S(2)}, u32[]{:S(2)}) async-start(bf16[32,64,256]{2,1,0:T(8,128)(2,1)} %copy-done.5), calls=%async_computation.2 | async-start | bytes 2097152 | tf_op jit(solution)/shard_map/all_to_all | solution.py:503
  68.6 2.5 %collective-permute-start.13 = (bf16[16,64,256]{2,1,0:T(8,128)(2,1)}, bf16[16,64,256]{2,1,0:T(8,128)(2,1)}, u32[]{:S(2)}, u32[]{:S(2)}) collective-permute-start(bf16[16,64,256]{2,1,0:T(8,128)(2,1)} %get-tuple-element.93.refs_0_), channel_id=1, source_target_pairs={{0,3},{1,0},{2,1},{3,2},{4,7},{5,4},{6,5},{7,6},{8,11},{9,8},{10,9... | collective-permute-start | bytes 1572872 | tf_op jit(solution)/shard_map/ppermute | solution.py:508
  71.2 2.7 %collective-permute-start.22 = (bf16[16,64,256]{2,1,0:T(8,128)(2,1)}, bf16[16,64,256]{2,1,0:T(8,128)(2,1)}, u32[]{:S(2)}, u32[]{:S(2)}) collective-permute-start(bf16[16,64,256]{2,1,0:T(8,128)(2,1)} %get-tuple-element.110.refs_0_.refs_4_), channel_id=1, source_target_pairs={{0,3},{1,0},{2,1},{3,2},{4,7},{5,4},{6,5},{7,6},{8,11},{9,8},{10,9... | collective-permute-start | bytes 1572872 | tf_op jit(solution)/shard_map/ppermute | solution.py:508
  74.5 11.2 %all-to-all-done.2.refs_0_ = bf16[32,64,256]{2,1,0:T(8,128)(2,1)} async-done(((bf16[32,64,256]{2,1,0:T(8,128)(2,1)}), bf16[32,64,256]{2,1,0:T(8,128)(2,1)}, u32[]{:S(2)}, u32[]{:S(2)}) %all-to-all-start.2) | async-done | bytes 1048608 | tf_op jit(solution)/shard_map/all_to_all | solution.py:503
  85.7 2.3 %shard_map.95 = bf16[32,64,256]{2,1,0:T(8,128)(2,1)} custom-call(s32[32]{0:T(128)S(1)} %select_reduce_fusion.5.index_ref, bf16[32,64,256]{2,1,0:T(8,128)(2,1)} %all-to-all-done.2.refs_0_), custom_call_target="tpu_custom_call" | custom-call | tf_op jit(solution)/shard_map/pallas_call | solution.py:68
  87.9 4.6 %all-to-all-start.3 = ((bf16[32,64,256]{2,1,0:T(8,128)(2,1)}), bf16[32,64,256]{2,1,0:T(8,128)(2,1)}, u32[]{:S(2)}, u32[]{:S(2)}) async-start(bf16[32,64,256]{2,1,0:T(8,128)(2,1)} %shard_map.95), calls=%async_computation.3 | async-start | bytes 2097152 | tf_op jit(solution)/shard_map/all_to_all | solution.py:503
  92.5 0.7 convert_reduce_fusion.2
  94.2 1.3 collective-permute-start.12
  95.5 1.5 collective-permute-start.23
  97.2 12.4 %all-to-all-done.3.rows_ref = bf16[32,64,256]{2,1,0:T(8,128)(2,1)} async-done(((bf16[32,64,256]{2,1,0:T(8,128)(2,1)}), bf16[32,64,256]{2,1,0:T(8,128)(2,1)}, u32[]{:S(2)}, u32[]{:S(2)}) %all-to-all-start.3) | async-done | bytes 1048608 | tf_op jit(solution)/shard_map/all_to_all | solution.py:503
  109.5 2.2 %shard_map.96 = (bf16[544,256]{1,0:T(8,128)(2,1)}, bf16[544,256]{1,0:T(8,128)(2,1)}) custom-call(s32[32]{0:T(128)S(1)} %get-tuple-element.137.slots_ref.seats_ref, s32[32]{0:T(128)S(1)} %broadcast_minimum_fusion.offsets_ref, bf16[32,64,256]{2,1,0:T(8,128)(2,1)} %all-to-all-done.3.rows_ref), custom_call_target="tpu_custom_call" | custom-call | tf_op jit(solution)/shard_map/pallas_call | solution.py:252
  111.7 1.3 collective-permute-start.9
  113.0 1.5 collective-permute-start.10
  114.6 0.8 copy-done.8
  115.4 1.0 copy-done.9
  116.4 9.9 %shard_map.97 = (bf16[32,16,256]{2,1,0:T(8,128)(2,1)}, bf16[32,16,256]{2,1,0:T(8,128)(2,1)}, bf16[32,16,256]{2,1,0:T(8,128)(2,1)}, bf16[32,16,256]{2,1,0:T(8,128)(2,1)}) custom-call(s32[32]{0:T(128)S(1)} %select_reduce_fusion.4.order_ref, s32[1]{0:T(128)} %bitcast.9.rank_ref, bf16[16,64,256]{2,1,0:T(8,128)(2,1)S(1)} %copy-done.6, ...), custom_call_target="tpu_custom_call" | custom-call | tf_op jit(solution)/shard_map/pallas_call | solution.py:214
  126.4 1.3 collective-permute-start.17
  128.0 2.6 %collective-permute-start.16 = (bf16[544,256]{1,0:T(8,128)(2,1)}, bf16[544,256]{1,0:T(8,128)(2,1)}, u32[]{:S(2)}, u32[]{:S(2)}) collective-permute-start(bf16[544,256]{1,0:T(8,128)(2,1)} %collective-permute-done.10.refs_7_), channel_id=1, source_target_pairs={{0,3},{1,0},{2,1},{3,2},{4,7},{5,4},{6,5},{7,6},{8,11},{9,8},{10,9... | collective-permute-start | bytes 835592 | tf_op jit(solution)/shard_map/ppermute | solution.py:508
  130.6 8.8 %shard_map.99 = (bf16[32,16,256]{2,1,0:T(8,128)(2,1)}, bf16[32,16,256]{2,1,0:T(8,128)(2,1)}, bf16[32,16,256]{2,1,0:T(8,128)(2,1)}, bf16[32,16,256]{2,1,0:T(8,128)(2,1)}) custom-call(s32[32]{0:T(128)S(1)} %select_reduce_fusion.4.order_ref, s32[1]{0:T(128)} %bitcast.9.rank_ref, ...), custom_call_target="tpu_custom_call", output_to_operand_aliasing={{0}: (16, {}), {1}: (17, {}), {2}: (18, {}), {3}: (19, {})} | custom-call | tf_op jit(solution)/shard_map/pallas_call | solution.py:214
  140.2 2.5 %collective-permute-start.25 = (bf16[32,16,256]{2,1,0:T(8,128)(2,1)}, bf16[32,16,256]{2,1,0:T(8,128)(2,1)}, u32[]{:S(2)}, u32[]{:S(2)}) collective-permute-start(bf16[32,16,256]{2,1,0:T(8,128)(2,1)} %get-tuple-element.117), channel_id=1, source_target_pairs={{0,2},{1,3},{2,0},{3,1},{4,6},{5,7},{6,4},{7,5},{8,10},{9,11},{10,... | collective-permute-start | bytes 786440 | tf_op jit(solution)/shard_map/ppermute | solution.py:508
  143.3 12.7 %shard_map.98 = (bf16[32,16,256]{2,1,0:T(8,128)(2,1)}, bf16[32,16,256]{2,1,0:T(8,128)(2,1)}, bf16[32,16,256]{2,1,0:T(8,128)(2,1)}, bf16[32,16,256]{2,1,0:T(8,128)(2,1)}) custom-call(s32[32]{0:T(128)S(1)} %get-tuple-element.135.order_ref, s32[32]{0:T(128)S(1)} %broadcast_minimum_fusion.offsets_ref, s32[32]{0:T(128)S(1)} %get-tuple-element.137.slots_ref.seats_ref, ...), custom_call_target="tpu_custom_call" | custom-call | tf_op jit(solution)/shard_map/pallas_call | solution.py:338
  156.0 0.9 collective-permute-start.18
  156.9 1.3 collective-permute-start.19
  158.2 2.0 collective-permute-start.20
  161.7 1.0 copy-done.10
  162.8 0.9 copy-done.12
  163.7 6.0 %shard_map.100.refs_16_ = bf16[32,4,2,16,256]{4,3,2,1,0:T(8,128)(2,1)} custom-call(s32[33]{0:T(128)S(1)} %pad_add_fusion.1.scalar_ref, bf16[16,64,256]{2,1,0:T(8,128)(2,1)S(1)} %copy-done.6, bf16[16,64,256]{2,1,0:T(8,128)(2,1)} %collective-permute-done.11.refs_1_, bf16[16,64,256]{2,1,0:T(8,128)(2,1)S(1)} %copy-done.10, ...), custom_call_target="tpu_custom_call" | custom-call | tf_op jit(solution)/shard_map/pallas_call | solution.py:400
  169.9 4.5 %shard_map.101 = bf16[32,4,2,16,256]{4,3,2,1,0:T(8,128)(2,1)} custom-call(s32[33]{0:T(128)S(1)} %pad_add_fusion.scalar_ref, s32[32]{0:T(128)S(1)} %get-tuple-element.137.slots_ref.seats_ref, s32[32]{0:T(128)S(1)} %broadcast_minimum_fusion.offsets_ref, bf16[544,256]{1,0:T(8,128)(2,1)S(1)} %copy-done.11, ...), custom_call_target="tpu_custom_call", output_to_operand_aliasing={{}: (19, {})} | custom-call | tf_op jit(solution)/shard_map/pallas_call | solution.py:455
  174.4 9.1 %all-to-all-start.4 = ((bf16[128,2,16,256]{3,2,1,0:T(8,128)(2,1)}), bf16[128,2,16,256]{3,2,1,0:T(8,128)(2,1)}, u32[]{:S(2)}, u32[]{:S(2)}) async-start(bf16[128,2,16,256]{3,2,1,0:T(8,128)(2,1)} %bitcast.11), calls=%async_computation.4 | async-start | bytes 4194304 | tf_op jit(solution)/shard_map/all_to_all | solution.py:639
  183.6 30.4 %all-to-all-done.4 = bf16[128,2,16,256]{3,2,1,0:T(8,128)(2,1)} async-done(((bf16[128,2,16,256]{3,2,1,0:T(8,128)(2,1)}), bf16[128,2,16,256]{3,2,1,0:T(8,128)(2,1)}, u32[]{:S(2)}, u32[]{:S(2)}) %all-to-all-start.4) | async-done | bytes 2097184 | tf_op jit(solution)/shard_map/all_to_all | solution.py:639
  214.1 3.2 %shard_map.102 = bf16[32,128,256]{2,1,0:T(8,128)(2,1)} custom-call(s32[32]{0:T(128)S(1)} %broadcast_subtract_fusion.index_ref, bf16[32,4,2,16,256]{4,3,2,1,0:T(8,128)(2,1)} %bitcast.12.src), custom_call_target="tpu_custom_call" | custom-call | tf_op jit(solution)/shard_map/pallas_call | solution.py:37
  (104 shorter events, 14.8 us)
Async XLA Ops:
  0.0 46.3 %copy-start = (bf16[1024,1024]{1,0:T(8,128)(2,1)S(1)}, bf16[1024,1024]{1,0:T(8,128)(2,1)}, u32[]{:S(2)}) copy-start(bf16[1024,1024]{1,0:T(8,128)(2,1)} %param.17) | copy-start | bytes 6291460
  3.0 1.6 copy-start.1
  4.6 0.7 copy-start.15
  5.9 1.1 copy-start.4
  6.9 15.5 %copy-start.17 = (s32[32]{0:T(128)S(1)}, s32[32]{0:T(128)}, u32[]{:S(2)}) copy-start(s32[32]{0:T(128)} %param.16) | copy-start | bytes 388
  6.9 16.2 %copy-start.24 = (f32[2,16]{1,0:T(2,128)S(1)}, f32[2,16]{1,0:T(2,128)}, u32[]{:S(2)}) copy-start(f32[2,16]{1,0:T(2,128)} %param.18) | copy-start | bytes 388
  6.9 29.5 %all-to-all-start = ((bf16[32,80,256]{2,1,0:T(8,128)(2,1)}), bf16[32,80,256]{2,1,0:T(8,128)(2,1)S(1)}, u32[]{:S(2)}, u32[]{:S(2)}) async-start(bf16[32,80,256]{2,1,0:T(8,128)(2,1)} %copy-done.4), calls=%async_computation | async-start | bytes 2621440 | tf_op jit(solution)/shard_map/all_to_all | solution.py:503
  16.7 47.3 %collective-permute-start.7 = (bf16[256,1024]{1,0:T(8,128)(2,1)}, bf16[256,1024]{1,0:T(8,128)(2,1)}, u32[]{:S(2)}, u32[]{:S(2)}) collective-permute-start(bf16[256,1024]{1,0:T(8,128)(2,1)} %refs_12_.7), channel_id=1, source_target_pairs={{0,2},{1,3},{2,0},{3,1},{4,6},{5,7},{6,4},{7,5},{8,10},{9,11},{10,... | collective-permute-start | bytes 1572872 | tf_op jit(solution)/shard_map/ppermute | solution.py:508
  19.5 44.4 %collective-permute-start.6 = (bf16[256,1024]{1,0:T(8,128)(2,1)}, bf16[256,1024]{1,0:T(8,128)(2,1)}, u32[]{:S(2)}, u32[]{:S(2)}) collective-permute-start(bf16[256,1024]{1,0:T(8,128)(2,1)} %refs_12_.7), channel_id=1, source_target_pairs={{0,1},{1,2},{2,3},{3,0},{4,5},{5,6},{6,7},{7,4},{8,9},{9,10},{10,1... | collective-permute-start | bytes 1572872 | tf_op jit(solution)/shard_map/ppermute | solution.py:508
  19.8 44.1 %collective-permute-start.8 = (bf16[256,1024]{1,0:T(8,128)(2,1)}, bf16[256,1024]{1,0:T(8,128)(2,1)}, u32[]{:S(2)}, u32[]{:S(2)}) collective-permute-start(bf16[256,1024]{1,0:T(8,128)(2,1)} %refs_12_.7), channel_id=1, source_target_pairs={{0,3},{1,0},{2,1},{3,2},{4,7},{5,4},{6,5},{7,6},{8,11},{9,8},{10,9... | collective-permute-start | bytes 1572872 | tf_op jit(solution)/shard_map/ppermute | solution.py:508
  37.9 1.1 copy-start.3
  39.0 23.9 %all-to-all-start.1 = ((bf16[32,80,256]{2,1,0:T(8,128)(2,1)}), bf16[32,80,256]{2,1,0:T(8,128)(2,1)S(1)}, u32[]{:S(2)}, u32[]{:S(2)}) async-start(bf16[32,80,256]{2,1,0:T(8,128)(2,1)} %copy-done.3), calls=%async_computation.1 | async-start | bytes 2621440 | tf_op jit(solution)/shard_map/all_to_all | solution.py:503
  43.0 1.6 copy-start.2
  45.2 1.0 copy-start.5
  64.0 21.7 %all-to-all-start.2 = ((bf16[32,64,256]{2,1,0:T(8,128)(2,1)}), bf16[32,64,256]{2,1,0:T(8,128)(2,1)}, u32[]{:S(2)}, u32[]{:S(2)}) async-start(bf16[32,64,256]{2,1,0:T(8,128)(2,1)} %copy-done.5), calls=%async_computation.2 | async-start | bytes 2097152 | tf_op jit(solution)/shard_map/all_to_all | solution.py:503
  68.6 44.4 %collective-permute-start.13 = (bf16[16,64,256]{2,1,0:T(8,128)(2,1)}, bf16[16,64,256]{2,1,0:T(8,128)(2,1)}, u32[]{:S(2)}, u32[]{:S(2)}) collective-permute-start(bf16[16,64,256]{2,1,0:T(8,128)(2,1)} %get-tuple-element.93.refs_0_), channel_id=1, source_target_pairs={{0,3},{1,0},{2,1},{3,2},{4,7},{5,4},{6,5},{7,6},{8,11},{9,8},{10,9... | collective-permute-start | bytes 1572872 | tf_op jit(solution)/shard_map/ppermute | solution.py:508
  71.2 23.0 %collective-permute-start.11 = (bf16[16,64,256]{2,1,0:T(8,128)(2,1)}, bf16[16,64,256]{2,1,0:T(8,128)(2,1)}, u32[]{:S(2)}, u32[]{:S(2)}) collective-permute-start(bf16[16,64,256]{2,1,0:T(8,128)(2,1)} %get-tuple-element.93.refs_0_), channel_id=1, source_target_pairs={{0,1},{1,2},{2,3},{3,0},{4,5},{5,6},{6,7},{7,4},{8,9},{9,10},{10,1... | collective-permute-start | bytes 1572872 | tf_op jit(solution)/shard_map/ppermute | solution.py:508
  71.2 24.3 %collective-permute-start.22 = (bf16[16,64,256]{2,1,0:T(8,128)(2,1)}, bf16[16,64,256]{2,1,0:T(8,128)(2,1)}, u32[]{:S(2)}, u32[]{:S(2)}) collective-permute-start(bf16[16,64,256]{2,1,0:T(8,128)(2,1)} %get-tuple-element.110.refs_0_.refs_4_), channel_id=1, source_target_pairs={{0,3},{1,0},{2,1},{3,2},{4,7},{5,4},{6,5},{7,6},{8,11},{9,8},{10,9... | collective-permute-start | bytes 1572872 | tf_op jit(solution)/shard_map/ppermute | solution.py:508
  73.8 54.1 %collective-permute-start.21 = (bf16[16,64,256]{2,1,0:T(8,128)(2,1)}, bf16[16,64,256]{2,1,0:T(8,128)(2,1)}, u32[]{:S(2)}, u32[]{:S(2)}) collective-permute-start(bf16[16,64,256]{2,1,0:T(8,128)(2,1)} %get-tuple-element.110.refs_0_.refs_4_), channel_id=1, source_target_pairs={{0,1},{1,2},{2,3},{3,0},{4,5},{5,6},{6,7},{7,4},{8,9},{9,10},{10,1... | collective-permute-start | bytes 1572872 | tf_op jit(solution)/shard_map/ppermute | solution.py:508
  87.9 27.4 %copy-start.6 = (bf16[16,64,256]{2,1,0:T(8,128)(2,1)S(1)}, bf16[16,64,256]{2,1,0:T(8,128)(2,1)}, u32[]{:S(2)}) copy-start(bf16[16,64,256]{2,1,0:T(8,128)(2,1)} %get-tuple-element.93.refs_0_) | copy-start | bytes 1572868
  87.9 21.6 %all-to-all-start.3 = ((bf16[32,64,256]{2,1,0:T(8,128)(2,1)}), bf16[32,64,256]{2,1,0:T(8,128)(2,1)}, u32[]{:S(2)}, u32[]{:S(2)}) async-start(bf16[32,64,256]{2,1,0:T(8,128)(2,1)} %shard_map.95), calls=%async_computation.3 | async-start | bytes 2097152 | tf_op jit(solution)/shard_map/all_to_all | solution.py:503
  94.2 20.4 %collective-permute-start.12 = (bf16[16,64,256]{2,1,0:T(8,128)(2,1)}, bf16[16,64,256]{2,1,0:T(8,128)(2,1)S(1)}, u32[]{:S(2)}, u32[]{:S(2)}) collective-permute-start(bf16[16,64,256]{2,1,0:T(8,128)(2,1)} %collective-permute-done.11.refs_1_), channel_id=1, source_target_pairs={{0,1},{1,2},{2,3},{3,0},{4,5},{5,6},{6,7},{7,4},{8,9},{9,10},{10,1... | collective-permute-start | bytes 1572872 | tf_op jit(solution)/shard_map/ppermute | solution.py:508
  95.5 35.1 %collective-permute-start.23 = (bf16[16,64,256]{2,1,0:T(8,128)(2,1)}, bf16[16,64,256]{2,1,0:T(8,128)(2,1)}, u32[]{:S(2)}, u32[]{:S(2)}) collective-permute-start(bf16[16,64,256]{2,1,0:T(8,128)(2,1)} %collective-permute-done.22.refs_3_.refs_7_), channel_id=1, source_target_pairs={{0,3},{1,0},{2,1},{3,2},{4,7},{5,4},{6,5},{7,6},{8,11},{9,8},{10,9... | collective-permute-start | bytes 1572872 | tf_op jit(solution)/shard_map/ppermute | solution.py:508
  111.7 15.9 %collective-permute-start.9 = (bf16[544,256]{1,0:T(8,128)(2,1)}, bf16[544,256]{1,0:T(8,128)(2,1)}, u32[]{:S(2)}, u32[]{:S(2)}) collective-permute-start(bf16[544,256]{1,0:T(8,128)(2,1)} %get-tuple-element.91.refs_0_), channel_id=1, source_target_pairs={{0,1},{1,2},{2,3},{3,0},{4,5},{5,6},{6,7},{7,4},{8,9},{9,10},{10,1... | collective-permute-start | bytes 835592 | tf_op jit(solution)/shard_map/ppermute | solution.py:508
  113.0 14.9 %collective-permute-start.10 = (bf16[544,256]{1,0:T(8,128)(2,1)}, bf16[544,256]{1,0:T(8,128)(2,1)}, u32[]{:S(2)}, u32[]{:S(2)}) collective-permute-start(bf16[544,256]{1,0:T(8,128)(2,1)} %get-tuple-element.92.refs_1_), channel_id=1, source_target_pairs={{0,3},{1,0},{2,1},{3,2},{4,7},{5,4},{6,5},{7,6},{8,11},{9,8},{10,9... | collective-permute-start | bytes 835592 | tf_op jit(solution)/shard_map/ppermute | solution.py:508
  114.6 0.8 copy-start.8
  115.4 1.0 copy-start.9
  116.4 10.0 %copy-start.11 = (bf16[544,256]{1,0:T(8,128)(2,1)S(1)}, bf16[544,256]{1,0:T(8,128)(2,1)}, u32[]{:S(2)}) copy-start(bf16[544,256]{1,0:T(8,128)(2,1)} %get-tuple-element.91.refs_0_) | copy-start | bytes 835588
  116.4 14.2 %copy-start.7 = (bf16[16,64,256]{2,1,0:T(8,128)(2,1)S(1)}, bf16[16,64,256]{2,1,0:T(8,128)(2,1)}, u32[]{:S(2)}) copy-start(bf16[16,64,256]{2,1,0:T(8,128)(2,1)} %get-tuple-element.110.refs_0_.refs_4_) | copy-start | bytes 1572868
  116.4 14.2 %copy-start.18 = (bf16[1024,1024]{1,0:T(8,128)(2,1)S(1)}, bf16[1024,1024]{1,0:T(8,128)(2,1)}, u32[]{:S(2)}) copy-start(bf16[1024,1024]{1,0:T(8,128)(2,1)} %bitcast_select_fusion.refs_4_.refs_8_) | copy-start | bytes 6291460
  116.4 14.2 %copy-start.19 = (f32[32,8,256]{2,1,0:T(8,128)S(1)}, f32[32,8,256]{2,1,0:T(8,128)}, u32[]{:S(2)}) copy-start(f32[32,8,256]{2,1,0:T(8,128)} %stack.8.refs_5_.refs_9_) | copy-start | bytes 786436
  126.4 13.8 %collective-permute-start.17 = (bf16[544,256]{1,0:T(8,128)(2,1)S(1)}, bf16[544,256]{1,0:T(8,128)(2,1)}, u32[]{:S(2)}, u32[]{:S(2)}) collective-permute-start(bf16[544,256]{1,0:T(8,128)(2,1)S(1)} %copy-done.11), channel_id=1, source_target_pairs={{0,3},{1,0},{2,1},{3,2},{4,7},{5,4},{6,5},{7,6},{8,11},{9,8},{10,9... | collective-permute-start | bytes 835592 | tf_op jit(solution)/shard_map/ppermute | solution.py:508
  127.6 15.0 %collective-permute-start.14 = (bf16[544,256]{1,0:T(8,128)(2,1)}, bf16[544,256]{1,0:T(8,128)(2,1)}, u32[]{:S(2)}, u32[]{:S(2)}) collective-permute-start(bf16[544,256]{1,0:T(8,128)(2,1)} %get-tuple-element.92.refs_1_), channel_id=1, source_target_pairs={{0,1},{1,2},{2,3},{3,0},{4,5},{5,6},{6,7},{7,4},{8,9},{9,10},{10,1... | collective-permute-start | bytes 835592 | tf_op jit(solution)/shard_map/ppermute | solution.py:508
  127.9 15.4 %collective-permute-start.15 = (bf16[544,256]{1,0:T(8,128)(2,1)}, bf16[544,256]{1,0:T(8,128)(2,1)}, u32[]{:S(2)}, u32[]{:S(2)}) collective-permute-start(bf16[544,256]{1,0:T(8,128)(2,1)} %collective-permute-done.9.refs_2_), channel_id=1, source_target_pairs={{0,1},{1,2},{2,3},{3,0},{4,5},{5,6},{6,7},{7,4},{8,9},{9,10},{10,1... | collective-permute-start | bytes 835592 | tf_op jit(solution)/shard_map/ppermute | solution.py:508
  128.0 15.3 %collective-permute-start.16 = (bf16[544,256]{1,0:T(8,128)(2,1)}, bf16[544,256]{1,0:T(8,128)(2,1)}, u32[]{:S(2)}, u32[]{:S(2)}) collective-permute-start(bf16[544,256]{1,0:T(8,128)(2,1)} %collective-permute-done.10.refs_7_), channel_id=1, source_target_pairs={{0,3},{1,0},{2,1},{3,2},{4,7},{5,4},{6,5},{7,6},{8,11},{9,8},{10,9... | collective-permute-start | bytes 835592 | tf_op jit(solution)/shard_map/ppermute | solution.py:508
  139.4 18.8 %collective-permute-start.24 = (bf16[32,16,256]{2,1,0:T(8,128)(2,1)}, bf16[32,16,256]{2,1,0:T(8,128)(2,1)}, u32[]{:S(2)}, u32[]{:S(2)}) collective-permute-start(bf16[32,16,256]{2,1,0:T(8,128)(2,1)} %get-tuple-element.116), channel_id=1, source_target_pairs={{0,1},{1,2},{2,3},{3,0},{4,5},{5,6},{6,7},{7,4},{8,9},{9,10},{10,1... | collective-permute-start | bytes 786440 | tf_op jit(solution)/shard_map/ppermute | solution.py:508
  140.2 21.5 %collective-permute-start.25 = (bf16[32,16,256]{2,1,0:T(8,128)(2,1)}, bf16[32,16,256]{2,1,0:T(8,128)(2,1)}, u32[]{:S(2)}, u32[]{:S(2)}) collective-permute-start(bf16[32,16,256]{2,1,0:T(8,128)(2,1)} %get-tuple-element.117), channel_id=1, source_target_pairs={{0,2},{1,3},{2,0},{3,1},{4,6},{5,7},{6,4},{7,5},{8,10},{9,11},{10,... | collective-permute-start | bytes 786440 | tf_op jit(solution)/shard_map/ppermute | solution.py:508
  142.6 19.1 %collective-permute-start.26 = (bf16[32,16,256]{2,1,0:T(8,128)(2,1)}, bf16[32,16,256]{2,1,0:T(8,128)(2,1)}, u32[]{:S(2)}, u32[]{:S(2)}) collective-permute-start(bf16[32,16,256]{2,1,0:T(8,128)(2,1)} %get-tuple-element.118), channel_id=1, source_target_pairs={{0,3},{1,0},{2,1},{3,2},{4,7},{5,4},{6,5},{7,6},{8,11},{9,8},{10,9... | collective-permute-start | bytes 786440 | tf_op jit(solution)/shard_map/ppermute | solution.py:508
  156.0 13.8 %collective-permute-start.18 = (bf16[32,16,256]{2,1,0:T(8,128)(2,1)}, bf16[32,16,256]{2,1,0:T(8,128)(2,1)}, u32[]{:S(2)}, u32[]{:S(2)}) collective-permute-start(bf16[32,16,256]{2,1,0:T(8,128)(2,1)} %get-tuple-element.103), channel_id=1, source_target_pairs={{0,1},{1,2},{2,3},{3,0},{4,5},{5,6},{6,7},{7,4},{8,9},{9,10},{10,1... | collective-permute-start | bytes 786440 | tf_op jit(solution)/shard_map/ppermute | solution.py:508
  156.9 12.9 %collective-permute-start.19 = (bf16[32,16,256]{2,1,0:T(8,128)(2,1)}, bf16[32,16,256]{2,1,0:T(8,128)(2,1)}, u32[]{:S(2)}, u32[]{:S(2)}) collective-permute-start(bf16[32,16,256]{2,1,0:T(8,128)(2,1)} %get-tuple-element.104), channel_id=1, source_target_pairs={{0,2},{1,3},{2,0},{3,1},{4,6},{5,7},{6,4},{7,5},{8,10},{9,11},{10,... | collective-permute-start | bytes 786440 | tf_op jit(solution)/shard_map/ppermute | solution.py:508
  158.2 11.7 %collective-permute-start.20 = (bf16[32,16,256]{2,1,0:T(8,128)(2,1)}, bf16[32,16,256]{2,1,0:T(8,128)(2,1)}, u32[]{:S(2)}, u32[]{:S(2)}) collective-permute-start(bf16[32,16,256]{2,1,0:T(8,128)(2,1)} %get-tuple-element.105), channel_id=1, source_target_pairs={{0,3},{1,0},{2,1},{3,2},{4,7},{5,4},{6,5},{7,6},{8,11},{9,8},{10,9... | collective-permute-start | bytes 786440 | tf_op jit(solution)/shard_map/ppermute | solution.py:508
  161.7 1.0 copy-start.10
  162.8 0.9 copy-start.12
  163.7 6.1 %copy-start.14 = (bf16[32,16,256]{2,1,0:T(8,128)(2,1)S(1)}, bf16[32,16,256]{2,1,0:T(8,128)(2,1)}, u32[]{:S(2)}) copy-start(bf16[32,16,256]{2,1,0:T(8,128)(2,1)} %get-tuple-element.102.refs_8_) | copy-start | bytes 786436
  163.7 6.1 %copy-start.21 = (bf16[256,1024]{1,0:T(8,128)(2,1)S(1)}, bf16[256,1024]{1,0:T(8,128)(2,1)}, u32[]{:S(2)}) copy-start(bf16[256,1024]{1,0:T(8,128)(2,1)} %refs_12_.7) | copy-start | bytes 1572868
  169.8 4.5 %copy-start.20 = (f32[32,8,256]{2,1,0:T(8,128)S(1)}, f32[32,8,256]{2,1,0:T(8,128)}, u32[]{:S(2)}) copy-start(f32[32,8,256]{2,1,0:T(8,128)} %stack.8.refs_5_.refs_9_) | copy-start | bytes 786436
  174.4 39.7 %all-to-all-start.4 = ((bf16[128,2,16,256]{3,2,1,0:T(8,128)(2,1)}), bf16[128,2,16,256]{3,2,1,0:T(8,128)(2,1)}, u32[]{:S(2)}, u32[]{:S(2)}) async-start(bf16[128,2,16,256]{3,2,1,0:T(8,128)(2,1)} %bitcast.11), calls=%async_computation.4 | async-start | bytes 4194304 | tf_op jit(solution)/shard_map/all_to_all | solution.py:639

commit v7 on v6

--- a/solution.py
+++ b/solution.py
@@ -176,21 +176,23 @@
     )
 
 
-def attend(full, weight, history, order, rank, rows_info, heads, first, before):
-    mp = len(full)
-    some, rows, part = full[0].shape
+def attend(full, weight, history, order, rank, rows_info, heads):
+    mp = len(full[0])
+    half, rows, part = full[0][0].shape
     users = order.shape[0]
     events, kv_width = history.shape[1:]
     quarter = rows // mp
     total = BATCH * rows
-    skip = first // BATCH
     width = heads * HD
+    per_half = half // BATCH
 
     def body(order_ref, rank_ref, *refs):
-        full_refs, weight_ref, info_ref = refs[:mp], refs[mp], refs[mp + 1]
-        hist_refs = refs[mp + 2 : mp + 2 + BATCH]
+        full_refs, weight_ref, info_ref = refs[: 2 * mp], refs[2 * mp], refs[2 * mp + 1]
+        hist_refs = refs[2 * mp + 2 : 2 * mp + 2 + BATCH]
         out_refs, store = refs[-1 - mp : -1], refs[-1]
-        normed = normalise([f[...].reshape(total, part) for f in full_refs])
+        low = pl.program_id(0) < per_half
+        parts = [jnp.where(low, full_refs[k][...], full_refs[mp + k][...]) for k in range(mp)]
+        normed = normalise([p.reshape(total, part) for p in parts])
         infos = [info_ref.at[b] for b in range(BATCH)]
         for h in range(heads):
             projected = silu_dot(normed, weight_ref[:, h * 4 * HD : (h + 1) * 4 * HD])
@@ -203,64 +205,56 @@
             )
         spread_quarters(store, out_refs, rows, rank_ref[0])
 
+    def full_spec(n):
+        return pl.BlockSpec(
+            (BATCH, rows, part), lambda i, *_: (jnp.clip(i - n * per_half, 0, per_half - 1), 0, 0)
+        )
+
     def hist_spec(b):
-        return pl.BlockSpec(
-            (1, events, kv_width), lambda i, order, _: (order[(skip + i) * BATCH + b], 0, 0)
-        )
-
-    extra = () if before is None else tuple(before)
-    inputs = (order, rank, *full, weight, rows_info, *([history] * BATCH), *extra)
-    at = len(inputs) - len(extra)
+        return pl.BlockSpec((1, events, kv_width), lambda i, order, _: (order[i * BATCH + b], 0, 0))
+
     return pl.pallas_call(
         body,
         out_shape=[pltpu.HBM((users, quarter, width), jnp.bfloat16)] * mp,
         grid_spec=pltpu.PrefetchScalarGridSpec(
             num_scalar_prefetch=2,
-            grid=(some // BATCH,),
-            in_specs=[pl.BlockSpec((BATCH, rows, part), lambda i, *_: (i, 0, 0)) for _ in full]
+            grid=(users // BATCH,),
+            in_specs=[full_spec(n) for n in range(2) for _ in range(mp)]
             + [
                 pl.BlockSpec(weight.shape, lambda i, *_: (0, 0)),
-                pl.BlockSpec((BATCH,) + rows_info.shape[1:], lambda i, *_: (skip + i, 0, 0)),
+                pl.BlockSpec((BATCH,) + rows_info.shape[1:], lambda i, *_: (i, 0, 0)),
             ]
-            + [hist_spec(b) for b in range(BATCH)]
-            + [pl.BlockSpec(memory_space=pl.ANY) for _ in extra],
-            out_specs=[pl.BlockSpec((BATCH, quarter, width), lambda i, *_: (skip + i, 0, 0))] * mp,
+            + [hist_spec(b) for b in range(BATCH)],
+            out_specs=[pl.BlockSpec((BATCH, quarter, width), lambda i, *_: (i, 0, 0))] * mp,
             scratch_shapes=[pltpu.VMEM((total, width), jnp.bfloat16)],
         ),
-        input_output_aliases={at + k: k for k in range(len(extra))},
-        compiler_params=pltpu.CompilerParams(vmem_limit_bytes=VMEM),
-    )(*inputs)
+        compiler_params=pltpu.CompilerParams(vmem_limit_bytes=VMEM),
+    )(order, rank, *full[0], *full[1], weight, rows_info, *([history] * BATCH))
 
 
 def pack(slots, offsets, rows, size):
     users, count, width = rows.shape
-    half = size // 2
-
-    def body(slots_ref, offsets_ref, rows_ref, low, high, buffer, sem):
+
+    def body(slots_ref, offsets_ref, rows_ref, out, buffer, sem):
         for j in range(users):
             at = pl.multiple_of(offsets_ref[j], GROUP)
             buffer[pl.ds(at, count), :] = rows_ref[slots_ref[j]]
-        copies = [
-            pltpu.make_async_copy(buffer.at[pl.ds(n * half, half)], (low, high)[n], sem.at[n])
-            for n in range(2)
-        ]
-        for copy in copies:
-            copy.start()
-        for copy in copies:
-            copy.wait()
-
-    return pl.pallas_call(
-        body,
-        out_shape=[pltpu.HBM((half, width), rows.dtype)] * 2,
+        copy = pltpu.make_async_copy(buffer.at[pl.ds(0, size)], out, sem)
+        copy.start()
+        copy.wait()
+
+    return pl.pallas_call(
+        body,
+        out_shape=pltpu.HBM((size, width), rows.dtype),
         in_specs=[
             pl.BlockSpec(memory_space=pltpu.SMEM),
             pl.BlockSpec(memory_space=pltpu.SMEM),
             pl.BlockSpec(memory_space=pltpu.VMEM),
         ],
-        out_specs=[pl.BlockSpec(memory_space=pltpu.HBM)] * 2,
+        out_specs=pl.BlockSpec(memory_space=pltpu.HBM),
         scratch_shapes=[
             pltpu.VMEM((size + count, width), rows.dtype),
-            pltpu.SemaphoreType.DMA((2,)),
+            pltpu.SemaphoreType.DMA,
         ],
         compiler_params=pltpu.CompilerParams(vmem_limit_bytes=VMEM),
     )(slots, offsets, rows)
@@ -419,14 +413,14 @@
 def project_out_packed(gated, full, weights, scalars, slots, offsets, piece, before):
     mp = len(gated)
     users, quarter, part = gated[0].shape
-    half = full[0][0].shape[0]
+    size = full[0][0].shape[0]
     out_part = weights[0].shape[1] // mp
     start = PIECES[piece][0]
 
     def body(scalar_ref, slots_ref, offsets_ref, *refs):
-        full_refs, gated_refs = refs[: 2 * mp], refs[2 * mp : 3 * mp]
-        weight_refs = refs[3 * mp : 4 * mp]
-        out_ref, whole, store, sem = refs[-4:]
+        full_refs, gated_refs = refs[:mp], refs[mp : 2 * mp]
+        weight_refs = refs[2 * mp : 3 * mp]
+        out_ref, store, sem = refs[-3:]
         rank = scalar_ref[0]
         rows = [g[...].reshape(users * quarter, part) for g in gated_refs]
         row = lax.broadcasted_iota(jnp.int32, (quarter, out_part), 0) + (start + rank * quarter)
@@ -436,14 +430,12 @@
             return pltpu.make_async_copy(store.at[k], out_ref.at[:, column, piece], sem.at[k])
 
         for k in range(mp):
-            whole[:half, :] = full_refs[2 * k][...]
-            whole[half:, :] = full_refs[2 * k + 1][...]
             column = (rank + (mp - k)) % mp
             first = pl.multiple_of(column * out_part, out_part)
             acc = rank_dot(rows, [w[:, pl.ds(first, out_part)] for w in weight_refs])
             for j in range(users):
-                at = jnp.minimum(offsets_ref[j] + rank * quarter, 2 * half - quarter)
-                residual = whole[pl.ds(pl.multiple_of(at, GROUP), quarter), :]
+                at = jnp.minimum(offsets_ref[j] + rank * quarter, size - quarter)
+                residual = full_refs[k][pl.ds(pl.multiple_of(at, GROUP), quarter), :]
                 mine = acc[j * quarter : (j + 1) * quarter] + residual.astype(jnp.float32)
                 alive = row < scalar_ref[1 + j]
                 store[k, slots_ref[j]] = jnp.where(alive, mine, 0.0).astype(jnp.bfloat16)
@@ -456,15 +448,14 @@
         body,
         out_shape=jax.ShapeDtypeStruct((users, mp, len(PIECES), quarter, out_part), jnp.bfloat16),
         in_specs=[pl.BlockSpec(memory_space=pltpu.SMEM)] * 3
-        + [pl.BlockSpec(memory_space=pltpu.VMEM)] * (4 * mp)
+        + [pl.BlockSpec(memory_space=pltpu.VMEM)] * (3 * mp)
         + [pl.BlockSpec(memory_space=pl.ANY)],
         out_specs=pl.BlockSpec(memory_space=pl.ANY),
         scratch_shapes=[
-            pltpu.VMEM((2 * half, part), jnp.bfloat16),
             pltpu.VMEM((mp, users, quarter, out_part), jnp.bfloat16),
             pltpu.SemaphoreType.DMA((mp,)),
         ],
-        input_output_aliases={3 + 4 * mp: 0},
+        input_output_aliases={3 + 3 * mp: 0},
         compiler_params=pltpu.CompilerParams(vmem_limit_bytes=VMEM),
     )(scalars, slots, offsets, *arrays, *gated, *weights, before)
 
@@ -585,20 +576,11 @@
     owned_1 = exchange(permute_in(send_second, exchange(rows_1), (0, second_rows)))
     owned_1, groups = lax.optimization_barrier((owned_1, groups))
     packed = pack(seat_slots, seat_offsets, owned_1, SIZE)
-    low, high = packed
-
-    def attend_some(full, first, before=None):
-        return attend(
-            full, weight_in, history_cache, order, rank, rows_info, heads, first, before
-        )
-
-    gated_low = attend_some(full_low, 0)
-    low_1, high_3 = shifted(low, 1), shifted(high, 3)
-    high_1, low_3 = shifted(high, 1), shifted(low, 3)
-    low_1, high_3, gated_low = lax.optimization_barrier((low_1, high_3, gated_low))
-    low_2, high_2 = shifted(low_1, 1), shifted(high_3, 3)
-    gated_0 = attend_some(full_high, users // 2, gated_low)
-    full_1 = [[low, high], [low_1, high_1], [low_2, high_2], [low_3, high_3]]
+    def attend_all(full):
+        return attend(full, weight_in, history_cache, order, rank, rows_info, heads)
+
+    full_1 = [[packed]] + [[shifted(packed, k)] for k in range(1, mp_size)]
+    gated_0 = attend_all((full_low, full_high))
     gated_1 = attend_packed(
         full_1,
         weight_in,
@@ -629,8 +611,7 @@
     def unpacked(done, rows):
         every = [rows] + [shifted(rows, k) for k in range(1, mp_size)]
         both = [[r[: users // 2] for r in every], [r[users // 2 :] for r in every]]
-        gated = attend_some(both[0], 0)
-        gated = by_quarter(attend_some(both[1], users // 2, gated))
+        gated = by_quarter(attend_all(both))
         return project_out(gated, both, weights_out, scalars, 1, done)
 
     done = lax.cond(

time: 219 us -> 216 us (0.986)
  waiting for transfers between devices: 71.8 us -> 77.4 us
  starting transfers between devices: 59.9 us -> 54.4 us
  Pallas kernels: 52.5 us -> 49.5 us
    ppermute x21 -> x18, waiting for transfers between devices: 0.14 us -> 3.85 us  [shifted(): lax.ppermute(array, 'mp', [(i, (i + k) % mp_size) for i in range(mp_size)])]
    ppermute x21 -> x18, starting transfers between devices: 27.9 us -> 24.6 us  [shifted(): lax.ppermute(array, 'mp', [(i, (i + k) % mp_size) for i in range(mp_size)])]
    pallas_call x2 -> x1, Pallas kernels: 18.7 us -> 15.8 us  [attend(): pl.pallas_call(body, out_shape=[pltpu.HBM((users, quarter, width), jnp.bf...]
    all_to_all x1, starting transfers between devices: 9.07 us -> 6.82 us  [per_device(): lax.all_to_all(done.reshape((-1,) + done.shape[2:]), ('dp', 'mp'), split_...]
    unnamed x42 -> x44, local copies, waits for them, and re-layouts: 10.8 us -> 11.8 us
  transfers between devices with their start and end apart: 26 -> 23, of which waited for: 6 -> 8; matrix products, arithmetic and copies ran while one was open for 8% -> 8% of each run, Pallas kernels for 20% -> 19%
where the time goes in v7:
time: 216 us; the launch traced here: 215 us
  waiting for transfers between devices  77.4 us (36%)
  starting transfers between devices  54.4 us (25%)
  Pallas kernels  49.5 us (23%)
  local copies, waits for them, and re-layouts  21.1 us (10%)
  other arithmetic  10.8 us (5%)
    all_to_all x4, waiting for transfers between devices, exchange(): return lax.all_to_all(rows, 'dp', split_axis=0, concat_axis=0, tiled=True)  43.1 us
    all_to_all x1, waiting for transfers between devices, per_device(): lax.all_to_all(done.reshape((-1,) + done.shape[2:]), ('dp', 'mp'), split_...  30.4 us
    ppermute x18, starting transfers between devices, shifted(): lax.ppermute(array, 'mp', [(i, (i + k) % mp_size) for i in range(mp_size)])  24.6 us
    all_to_all x4, starting transfers between devices, exchange(): return lax.all_to_all(rows, 'dp', split_axis=0, concat_axis=0, tiled=True)  23 us
    pallas_call x1, Pallas kernels, attend(): pl.pallas_call(body, out_shape=[pltpu.HBM((users, quarter, width), jnp.bf...  15.8 us
    pallas_call x1, Pallas kernels, attend_packed(): pl.pallas_call(body, out_shape=[pltpu.HBM((users, quarter, width), jnp.bf...  13.1 us
    unnamed x44, local copies, waits for them, and re-layouts  11.8 us
    all_to_all x1, starting transfers between devices, per_device(): lax.all_to_all(done.reshape((-1,) + done.shape[2:]), ('dp', 'mp'), split_...  6.82 us
  transfers between devices with their start and end apart: 23, of which 8 were waited for; matrix products, arithmetic and copies ran while one was open for 8% of the time, Pallas kernels for 19%

profile of v7, /device:TPU:1, one launch (start us, length us, event | category | flops | bytes accessed | tf_op | source)
XLA Modules:
  0.0 214.8 jit_solution(17956115108900609473)
XLA Ops:
  0.0 0.8 compare_select_fusion.13
  3.0 1.6 copy-done.1
  5.9 1.0 copy-done.4
  6.9 9.7 %all-to-all-start = ((bf16[32,80,256]{2,1,0:T(8,128)(2,1)}), bf16[32,80,256]{2,1,0:T(8,128)(2,1)S(1)}, u32[]{:S(2)}, u32[]{:S(2)}) async-start(bf16[32,80,256]{2,1,0:T(8,128)(2,1)} %copy-done.4), calls=%async_computation | async-start | bytes 2621440 | tf_op jit(solution)/shard_map/all_to_all | solution.py:494
  16.7 1.3 collective-permute-start.6
  18.0 2.5 %collective-permute-start.7 = (bf16[256,1024]{1,0:T(8,128)(2,1)}, bf16[256,1024]{1,0:T(8,128)(2,1)}, u32[]{:S(2)}, u32[]{:S(2)}) collective-permute-start(bf16[256,1024]{1,0:T(8,128)(2,1)} %refs_8_.2), channel_id=1, source_target_pairs={{0,2},{1,3},{2,0},{3,1},{4,6},{5,7},{6,4},{7,5},{8,10},{9,11},{10,... | collective-permute-start | bytes 1572872 | tf_op jit(solution)/shard_map/ppermute | solution.py:499
  20.4 1.2 collective-permute-start.8
  23.6 12.9 %all-to-all-done.refs_0_ = bf16[32,80,256]{2,1,0:T(8,128)(2,1)S(1)} async-done(((bf16[32,80,256]{2,1,0:T(8,128)(2,1)}), bf16[32,80,256]{2,1,0:T(8,128)(2,1)S(1)}, u32[]{:S(2)}, u32[]{:S(2)}) %all-to-all-start) | async-done | bytes 1310752 | tf_op jit(solution)/shard_map/all_to_all | solution.py:494
  37.9 1.1 copy-done.3
  39.0 4.0 %all-to-all-start.1 = ((bf16[32,80,256]{2,1,0:T(8,128)(2,1)}), bf16[32,80,256]{2,1,0:T(8,128)(2,1)S(1)}, u32[]{:S(2)}, u32[]{:S(2)}) async-start(bf16[32,80,256]{2,1,0:T(8,128)(2,1)} %copy-done.3), calls=%async_computation.1 | async-start | bytes 2621440 | tf_op jit(solution)/shard_map/all_to_all | solution.py:494
  43.0 1.6 copy-done.2
  45.2 1.0 copy-done.6
  46.3 2.0 gather_fusion.2
  49.9 1.3 broadcast_in_dim.394
  51.1 1.3 broadcast_in_dim.396
  52.4 1.8 stack.8.refs_5_.refs_9_
  54.2 3.2 %bitcast_select_fusion.refs_4_.refs_8_ = bf16[1024,1024]{1,0:T(8,128)(2,1)} fusion(bf16[4,256,1024]{2,1,0:T(8,128)(2,1)} %gather_fusion.2, pred[1024]{0:T(1024)(128)(4,1)S(1)} %broadcast_in_dim.400), kind=kLoop, calls=%fused_computation.3 | loop fusion | flops 1048576 | bytes 4195328 | tf_op jit(solution)/shard_map/jit(_take)/select_n | solution.py:561
  57.4 5.5 %all-to-all-done.1.src = bf16[32,80,256]{2,1,0:T(8,128)(2,1)S(1)} async-done(((bf16[32,80,256]{2,1,0:T(8,128)(2,1)}), bf16[32,80,256]{2,1,0:T(8,128)(2,1)S(1)}, u32[]{:S(2)}, u32[]{:S(2)}) %all-to-all-start.1) | async-done | bytes 1310752 | tf_op jit(solution)/shard_map/all_to_all | solution.py:494
  62.9 1.1 shard_map.94
  64.0 4.7 %all-to-all-start.2 = ((bf16[32,64,256]{2,1,0:T(8,128)(2,1)}), bf16[32,64,256]{2,1,0:T(8,128)(2,1)}, u32[]{:S(2)}, u32[]{:S(2)}) async-start(bf16[32,64,256]{2,1,0:T(8,128)(2,1)} %copy-done.6), calls=%async_computation.2 | async-start | bytes 2097152 | tf_op jit(solution)/shard_map/all_to_all | solution.py:494
  68.6 1.3 collective-permute-start.15
  69.9 1.5 collective-permute-start.17
  71.4 1.3 collective-permute-start.19
  73.5 12.2 %all-to-all-done.2.refs_0_ = bf16[32,64,256]{2,1,0:T(8,128)(2,1)} async-done(((bf16[32,64,256]{2,1,0:T(8,128)(2,1)}), bf16[32,64,256]{2,1,0:T(8,128)(2,1)}, u32[]{:S(2)}, u32[]{:S(2)}) %all-to-all-start.2) | async-done | bytes 1048608 | tf_op jit(solution)/shard_map/all_to_all | solution.py:494
  85.7 2.3 %shard_map.95 = bf16[32,64,256]{2,1,0:T(8,128)(2,1)} custom-call(s32[32]{0:T(128)S(1)} %select_reduce_fusion.5.index_ref, bf16[32,64,256]{2,1,0:T(8,128)(2,1)} %all-to-all-done.2.refs_0_), custom_call_target="tpu_custom_call" | custom-call | tf_op jit(solution)/shard_map/pallas_call | solution.py:68
  87.9 4.6 %all-to-all-start.3 = ((bf16[32,64,256]{2,1,0:T(8,128)(2,1)}), bf16[32,64,256]{2,1,0:T(8,128)(2,1)}, u32[]{:S(2)}, u32[]{:S(2)}) async-start(bf16[32,64,256]{2,1,0:T(8,128)(2,1)} %shard_map.95), calls=%async_computation.3 | async-start | bytes 2097152 | tf_op jit(solution)/shard_map/all_to_all | solution.py:494
  94.0 1.3 collective-permute-start.16
  95.3 1.6 collective-permute-start.20
  97.0 12.5 %all-to-all-done.3.rows_ref = bf16[32,64,256]{2,1,0:T(8,128)(2,1)} async-done(((bf16[32,64,256]{2,1,0:T(8,128)(2,1)}), bf16[32,64,256]{2,1,0:T(8,128)(2,1)}, u32[]{:S(2)}, u32[]{:S(2)}) %all-to-all-start.3) | async-done | bytes 1048608 | tf_op jit(solution)/shard_map/all_to_all | solution.py:494
  109.5 2.1 shard_map.96.refs_0_
  111.7 2.8 %collective-permute-start.10 = (bf16[1088,256]{1,0:T(8,128)(2,1)}, bf16[1088,256]{1,0:T(8,128)(2,1)S(1)}, u32[]{:S(2)}, u32[]{:S(2)}) collective-permute-start(bf16[1088,256]{1,0:T(8,128)(2,1)} %shard_map.96.refs_0_), channel_id=1, source_target_pairs={{0,2},{1,3},{2,0},{3,1},{4,6},{5,7},{6,4},{7,5},{8,10},{9,11},{10,... | collective-permute-start | bytes 1671176 | tf_op jit(solution)/shard_map/ppermute | solution.py:499
  114.5 0.9 collective-permute-start.11
  116.8 1.0 copy-done.7
  117.8 1.0 copy-done.9
  118.8 1.0 copy-done.12
  119.9 15.8 %shard_map.98 = (bf16[32,16,256]{2,1,0:T(8,128)(2,1)}, bf16[32,16,256]{2,1,0:T(8,128)(2,1)}, bf16[32,16,256]{2,1,0:T(8,128)(2,1)}, bf16[32,16,256]{2,1,0:T(8,128)(2,1)}) custom-call(s32[32]{0:T(128)S(1)} %select_reduce_fusion.4.order_ref, s32[1]{0:T(128)} %bitcast.9.rank_ref, bf16[16,64,256]{2,1,0:T(8,128)(2,1)S(1)} %copy-done.7, ...), custom_call_target="tpu_custom_call" | custom-call | tf_op jit(solution)/shard_map/pallas_call | solution.py:216
  136.6 3.0 %collective-permute-start.22 = (bf16[32,16,256]{2,1,0:T(8,128)(2,1)}, bf16[32,16,256]{2,1,0:T(8,128)(2,1)}, u32[]{:S(2)}, u32[]{:S(2)}) collective-permute-start(bf16[32,16,256]{2,1,0:T(8,128)(2,1)} %get-tuple-element.89), channel_id=1, source_target_pairs={{0,2},{1,3},{2,0},{3,1},{4,6},{5,7},{6,4},{7,5},{8,10},{9,11},{10,... | collective-permute-start | bytes 786440 | tf_op jit(solution)/shard_map/ppermute | solution.py:499
  140.1 13.1 %shard_map.97 = (bf16[32,16,256]{2,1,0:T(8,128)(2,1)}, bf16[32,16,256]{2,1,0:T(8,128)(2,1)}, bf16[32,16,256]{2,1,0:T(8,128)(2,1)}, bf16[32,16,256]{2,1,0:T(8,128)(2,1)}) custom-call(s32[32]{0:T(128)S(1)} %get-tuple-element.107.order_ref, s32[32]{0:T(128)S(1)} %broadcast_minimum_fusion.offsets_ref, s32[32]{0:T(128)S(1)} %get-tuple-element.109.slots_ref.seats_ref, ...), custom_call_target="tpu_custom_call" | custom-call | tf_op jit(solution)/shard_map/pallas_call | solution.py:332
  153.2 1.3 collective-permute-start.12
  154.5 2.5 %collective-permute-start.13 = (bf16[32,16,256]{2,1,0:T(8,128)(2,1)}, bf16[32,16,256]{2,1,0:T(8,128)(2,1)}, u32[]{:S(2)}, u32[]{:S(2)}) collective-permute-start(bf16[32,16,256]{2,1,0:T(8,128)(2,1)} %get-tuple-element.79), channel_id=1, source_target_pairs={{0,2},{1,3},{2,0},{3,1},{4,6},{5,7},{6,4},{7,5},{8,10},{9,11},{10,... | collective-permute-start | bytes 786440 | tf_op jit(solution)/shard_map/ppermute | solution.py:499
  156.9 1.2 collective-permute-start.14
  158.3 5.8 %shard_map.99.refs_12_ = bf16[32,4,2,16,256]{4,3,2,1,0:T(8,128)(2,1)} custom-call(s32[33]{0:T(128)S(1)} %pad_add_fusion.1.scalar_ref, bf16[16,64,256]{2,1,0:T(8,128)(2,1)S(1)} %copy-done.8, bf16[16,64,256]{2,1,0:T(8,128)(2,1)} %collective-permute-done.15.refs_1_, bf16[16,64,256]{2,1,0:T(8,128)(2,1)S(1)} %copy-done.13, ...), custom_call_target="tpu_custom_call" | custom-call | tf_op jit(solution)/shard_map/pallas_call | solution.py:394
  165.4 3.4 %collective-permute-done.13.refs_6_ = bf16[32,16,256]{2,1,0:T(8,128)(2,1)} collective-permute-done((bf16[32,16,256]{2,1,0:T(8,128)(2,1)}, bf16[32,16,256]{2,1,0:T(8,128)(2,1)}, u32[]{:S(2)}, u32[]{:S(2)}) %collective-permute-start.13) | collective-permute-done | bytes 262176 | tf_op jit(solution)/shard_map/ppermute | solution.py:499
  168.8 0.9 copy-done.15
  169.8 4.3 %shard_map.100 = bf16[32,4,2,16,256]{4,3,2,1,0:T(8,128)(2,1)} custom-call(s32[33]{0:T(128)S(1)} %pad_add_fusion.scalar_ref, s32[32]{0:T(128)S(1)} %get-tuple-element.109.slots_ref.seats_ref, s32[32]{0:T(128)S(1)} %broadcast_minimum_fusion.offsets_ref, bf16[1088,256]{1,0:T(8,128)(2,1)S(1)} %copy-done.5, ...), custom_call_target="tpu_custom_call", output_to_operand_aliasing={{}: (15, {})} | custom-call | tf_op jit(solution)/shard_map/pallas_call | solution.py:447
  174.0 6.8 %all-to-all-start.4 = ((bf16[128,2,16,256]{3,2,1,0:T(8,128)(2,1)}), bf16[128,2,16,256]{3,2,1,0:T(8,128)(2,1)}, u32[]{:S(2)}, u32[]{:S(2)}) async-start(bf16[128,2,16,256]{3,2,1,0:T(8,128)(2,1)} %bitcast.20), calls=%async_computation.4 | async-start | bytes 4194304 | tf_op jit(solution)/shard_map/all_to_all | solution.py:620
  181.1 30.4 %all-to-all-done.4 = bf16[128,2,16,256]{3,2,1,0:T(8,128)(2,1)} async-done(((bf16[128,2,16,256]{3,2,1,0:T(8,128)(2,1)}), bf16[128,2,16,256]{3,2,1,0:T(8,128)(2,1)}, u32[]{:S(2)}, u32[]{:S(2)}) %all-to-all-start.4) | async-done | bytes 2097184 | tf_op jit(solution)/shard_map/all_to_all | solution.py:620
  211.5 3.2 %shard_map.101 = bf16[32,128,256]{2,1,0:T(8,128)(2,1)} custom-call(s32[32]{0:T(128)S(1)} %broadcast_subtract_fusion.index_ref, bf16[32,4,2,16,256]{4,3,2,1,0:T(8,128)(2,1)} %bitcast.12.src), custom_call_target="tpu_custom_call" | custom-call | tf_op jit(solution)/shard_map/pallas_call | solution.py:37
  (99 shorter events, 14.8 us)
Async XLA Ops:
  0.0 46.3 %copy-start = (bf16[1024,1024]{1,0:T(8,128)(2,1)S(1)}, bf16[1024,1024]{1,0:T(8,128)(2,1)}, u32[]{:S(2)}) copy-start(bf16[1024,1024]{1,0:T(8,128)(2,1)} %param.17) | copy-start | bytes 6291460
  3.0 1.6 copy-start.1
  4.6 0.7 copy-start.17
  5.9 1.1 copy-start.4
  6.9 14.8 %copy-start.19 = (s32[32]{0:T(128)S(1)}, s32[32]{0:T(128)}, u32[]{:S(2)}) copy-start(s32[32]{0:T(128)} %param.16) | copy-start | bytes 388
  6.9 15.6 %copy-start.24 = (f32[2,16]{1,0:T(2,128)S(1)}, f32[2,16]{1,0:T(2,128)}, u32[]{:S(2)}) copy-start(f32[2,16]{1,0:T(2,128)} %param.18) | copy-start | bytes 388
  6.9 29.5 %all-to-all-start = ((bf16[32,80,256]{2,1,0:T(8,128)(2,1)}), bf16[32,80,256]{2,1,0:T(8,128)(2,1)S(1)}, u32[]{:S(2)}, u32[]{:S(2)}) async-start(bf16[32,80,256]{2,1,0:T(8,128)(2,1)} %copy-done.4), calls=%async_computation | async-start | bytes 2621440 | tf_op jit(solution)/shard_map/all_to_all | solution.py:494
  16.7 47.3 %collective-permute-start.6 = (bf16[256,1024]{1,0:T(8,128)(2,1)}, bf16[256,1024]{1,0:T(8,128)(2,1)}, u32[]{:S(2)}, u32[]{:S(2)}) collective-permute-start(bf16[256,1024]{1,0:T(8,128)(2,1)} %refs_8_.2), channel_id=1, source_target_pairs={{0,1},{1,2},{2,3},{3,0},{4,5},{5,6},{6,7},{7,4},{8,9},{9,10},{10,1... | collective-permute-start | bytes 1572872 | tf_op jit(solution)/shard_map/ppermute | solution.py:499
  18.0 46.0 %collective-permute-start.7 = (bf16[256,1024]{1,0:T(8,128)(2,1)}, bf16[256,1024]{1,0:T(8,128)(2,1)}, u32[]{:S(2)}, u32[]{:S(2)}) collective-permute-start(bf16[256,1024]{1,0:T(8,128)(2,1)} %refs_8_.2), channel_id=1, source_target_pairs={{0,2},{1,3},{2,0},{3,1},{4,6},{5,7},{6,4},{7,5},{8,10},{9,11},{10,... | collective-permute-start | bytes 1572872 | tf_op jit(solution)/shard_map/ppermute | solution.py:499
  20.4 43.6 %collective-permute-start.8 = (bf16[256,1024]{1,0:T(8,128)(2,1)}, bf16[256,1024]{1,0:T(8,128)(2,1)}, u32[]{:S(2)}, u32[]{:S(2)}) collective-permute-start(bf16[256,1024]{1,0:T(8,128)(2,1)} %refs_8_.2), channel_id=1, source_target_pairs={{0,3},{1,0},{2,1},{3,2},{4,7},{5,4},{6,5},{7,6},{8,11},{9,8},{10,9... | collective-permute-start | bytes 1572872 | tf_op jit(solution)/shard_map/ppermute | solution.py:499
  37.9 1.1 copy-start.3
  39.0 23.9 %all-to-all-start.1 = ((bf16[32,80,256]{2,1,0:T(8,128)(2,1)}), bf16[32,80,256]{2,1,0:T(8,128)(2,1)S(1)}, u32[]{:S(2)}, u32[]{:S(2)}) async-start(bf16[32,80,256]{2,1,0:T(8,128)(2,1)} %copy-done.3), calls=%async_computation.1 | async-start | bytes 2621440 | tf_op jit(solution)/shard_map/all_to_all | solution.py:494
  43.0 1.6 copy-start.2
  45.2 1.0 copy-start.6
  64.0 21.7 %all-to-all-start.2 = ((bf16[32,64,256]{2,1,0:T(8,128)(2,1)}), bf16[32,64,256]{2,1,0:T(8,128)(2,1)}, u32[]{:S(2)}, u32[]{:S(2)}) async-start(bf16[32,64,256]{2,1,0:T(8,128)(2,1)} %copy-done.6), calls=%async_computation.2 | async-start | bytes 2097152 | tf_op jit(solution)/shard_map/all_to_all | solution.py:494
  68.6 25.3 %collective-permute-start.15 = (bf16[16,64,256]{2,1,0:T(8,128)(2,1)}, bf16[16,64,256]{2,1,0:T(8,128)(2,1)}, u32[]{:S(2)}, u32[]{:S(2)}) collective-permute-start(bf16[16,64,256]{2,1,0:T(8,128)(2,1)} %get-tuple-element.85.refs_0_), channel_id=1, source_target_pairs={{0,1},{1,2},{2,3},{3,0},{4,5},{5,6},{6,7},{7,4},{8,9},{9,10},{10,1... | collective-permute-start | bytes 1572872 | tf_op jit(solution)/shard_map/ppermute | solution.py:499
  69.9 44.6 %collective-permute-start.17 = (bf16[16,64,256]{2,1,0:T(8,128)(2,1)}, bf16[16,64,256]{2,1,0:T(8,128)(2,1)}, u32[]{:S(2)}, u32[]{:S(2)}) collective-permute-start(bf16[16,64,256]{2,1,0:T(8,128)(2,1)} %get-tuple-element.85.refs_0_), channel_id=1, source_target_pairs={{0,3},{1,0},{2,1},{3,2},{4,7},{5,4},{6,5},{7,6},{8,11},{9,8},{10,9... | collective-permute-start | bytes 1572872 | tf_op jit(solution)/shard_map/ppermute | solution.py:499
  71.4 23.9 %collective-permute-start.19 = (bf16[16,64,256]{2,1,0:T(8,128)(2,1)}, bf16[16,64,256]{2,1,0:T(8,128)(2,1)}, u32[]{:S(2)}, u32[]{:S(2)}) collective-permute-start(bf16[16,64,256]{2,1,0:T(8,128)(2,1)} %get-tuple-element.86.refs_4_), channel_id=1, source_target_pairs={{0,3},{1,0},{2,1},{3,2},{4,7},{5,4},{6,5},{7,6},{8,11},{9,8},{10,9... | collective-permute-start | bytes 1572872 | tf_op jit(solution)/shard_map/ppermute | solution.py:499
  72.6 42.7 %collective-permute-start.18 = (bf16[16,64,256]{2,1,0:T(8,128)(2,1)}, bf16[16,64,256]{2,1,0:T(8,128)(2,1)}, u32[]{:S(2)}, u32[]{:S(2)}) collective-permute-start(bf16[16,64,256]{2,1,0:T(8,128)(2,1)} %get-tuple-element.86.refs_4_), channel_id=1, source_target_pairs={{0,1},{1,2},{2,3},{3,0},{4,5},{5,6},{6,7},{7,4},{8,9},{9,10},{10,1... | collective-permute-start | bytes 1572872 | tf_op jit(solution)/shard_map/ppermute | solution.py:499
  87.9 28.8 %copy-start.22 = (f32[32,8,256]{2,1,0:T(8,128)S(1)}, f32[32,8,256]{2,1,0:T(8,128)}, u32[]{:S(2)}) copy-start(f32[32,8,256]{2,1,0:T(8,128)} %stack.8.refs_5_.refs_9_) | copy-start | bytes 786436
  87.9 21.6 %all-to-all-start.3 = ((bf16[32,64,256]{2,1,0:T(8,128)(2,1)}), bf16[32,64,256]{2,1,0:T(8,128)(2,1)}, u32[]{:S(2)}, u32[]{:S(2)}) async-start(bf16[32,64,256]{2,1,0:T(8,128)(2,1)} %shard_map.95), calls=%async_computation.3 | async-start | bytes 2097152 | tf_op jit(solution)/shard_map/all_to_all | solution.py:494
  94.0 22.0 %collective-permute-start.16 = (bf16[16,64,256]{2,1,0:T(8,128)(2,1)}, bf16[16,64,256]{2,1,0:T(8,128)(2,1)S(1)}, u32[]{:S(2)}, u32[]{:S(2)}) collective-permute-start(bf16[16,64,256]{2,1,0:T(8,128)(2,1)} %collective-permute-done.15.refs_1_), channel_id=1, source_target_pairs={{0,1},{1,2},{2,3},{3,0},{4,5},{5,6},{6,7},{7,4},{8,9},{9,10},{10,1... | collective-permute-start | bytes 1572872 | tf_op jit(solution)/shard_map/ppermute | solution.py:499
  95.3 21.5 %collective-permute-start.20 = (bf16[16,64,256]{2,1,0:T(8,128)(2,1)}, bf16[16,64,256]{2,1,0:T(8,128)(2,1)}, u32[]{:S(2)}, u32[]{:S(2)}) collective-permute-start(bf16[16,64,256]{2,1,0:T(8,128)(2,1)} %collective-permute-done.19.refs_7_), channel_id=1, source_target_pairs={{0,3},{1,0},{2,1},{3,2},{4,7},{5,4},{6,5},{7,6},{8,11},{9,8},{10,9... | collective-permute-start | bytes 1572872 | tf_op jit(solution)/shard_map/ppermute | solution.py:499
  111.7 28.0 %collective-permute-start.10 = (bf16[1088,256]{1,0:T(8,128)(2,1)}, bf16[1088,256]{1,0:T(8,128)(2,1)S(1)}, u32[]{:S(2)}, u32[]{:S(2)}) collective-permute-start(bf16[1088,256]{1,0:T(8,128)(2,1)} %shard_map.96.refs_0_), channel_id=1, source_target_pairs={{0,2},{1,3},{2,0},{3,1},{4,6},{5,7},{6,4},{7,5},{8,10},{9,11},{10,... | collective-permute-start | bytes 1671176 | tf_op jit(solution)/shard_map/ppermute | solution.py:499
  114.5 25.2 %collective-permute-start.11 = (bf16[1088,256]{1,0:T(8,128)(2,1)}, bf16[1088,256]{1,0:T(8,128)(2,1)}, u32[]{:S(2)}, u32[]{:S(2)}) collective-permute-start(bf16[1088,256]{1,0:T(8,128)(2,1)} %shard_map.96.refs_0_), channel_id=1, source_target_pairs={{0,3},{1,0},{2,1},{3,2},{4,7},{5,4},{6,5},{7,6},{8,11},{9,8},{10,9... | collective-permute-start | bytes 1671176 | tf_op jit(solution)/shard_map/ppermute | solution.py:499
  115.3 24.7 %collective-permute-start.9 = (bf16[1088,256]{1,0:T(8,128)(2,1)}, bf16[1088,256]{1,0:T(8,128)(2,1)}, u32[]{:S(2)}, u32[]{:S(2)}) collective-permute-start(bf16[1088,256]{1,0:T(8,128)(2,1)} %shard_map.96.refs_0_), channel_id=1, source_target_pairs={{0,1},{1,2},{2,3},{3,0},{4,5},{5,6},{6,7},{7,4},{8,9},{9,10},{10,1... | collective-permute-start | bytes 1671176 | tf_op jit(solution)/shard_map/ppermute | solution.py:499
  116.0 0.8 copy-start.11
  116.8 1.0 copy-start.7
  117.8 1.0 copy-start.9
  118.8 1.0 copy-start.12
  119.9 20.2 %copy-start.5 = (bf16[1088,256]{1,0:T(8,128)(2,1)S(1)}, bf16[1088,256]{1,0:T(8,128)(2,1)}, u32[]{:S(2)}) copy-start(bf16[1088,256]{1,0:T(8,128)(2,1)} %shard_map.96.refs_0_) | copy-start | bytes 1671172
  135.7 21.3 %collective-permute-start.21 = (bf16[32,16,256]{2,1,0:T(8,128)(2,1)}, bf16[32,16,256]{2,1,0:T(8,128)(2,1)S(1)}, u32[]{:S(2)}, u32[]{:S(2)}) collective-permute-start(bf16[32,16,256]{2,1,0:T(8,128)(2,1)} %get-tuple-element.88), channel_id=1, source_target_pairs={{0,1},{1,2},{2,3},{3,0},{4,5},{5,6},{6,7},{7,4},{8,9},{9,10},{10,1... | collective-permute-start | bytes 786440 | tf_op jit(solution)/shard_map/ppermute | solution.py:499
  136.6 21.6 %collective-permute-start.22 = (bf16[32,16,256]{2,1,0:T(8,128)(2,1)}, bf16[32,16,256]{2,1,0:T(8,128)(2,1)}, u32[]{:S(2)}, u32[]{:S(2)}) collective-permute-start(bf16[32,16,256]{2,1,0:T(8,128)(2,1)} %get-tuple-element.89), channel_id=1, source_target_pairs={{0,2},{1,3},{2,0},{3,1},{4,6},{5,7},{6,4},{7,5},{8,10},{9,11},{10,... | collective-permute-start | bytes 786440 | tf_op jit(solution)/shard_map/ppermute | solution.py:499
  139.6 18.6 %collective-permute-start.23 = (bf16[32,16,256]{2,1,0:T(8,128)(2,1)}, bf16[32,16,256]{2,1,0:T(8,128)(2,1)}, u32[]{:S(2)}, u32[]{:S(2)}) collective-permute-start(bf16[32,16,256]{2,1,0:T(8,128)(2,1)} %get-tuple-element.90), channel_id=1, source_target_pairs={{0,3},{1,0},{2,1},{3,2},{4,7},{5,4},{6,5},{7,6},{8,11},{9,8},{10,9... | collective-permute-start | bytes 786440 | tf_op jit(solution)/shard_map/ppermute | solution.py:499
  140.0 18.2 %copy-start.8 = (bf16[16,64,256]{2,1,0:T(8,128)(2,1)S(1)}, bf16[16,64,256]{2,1,0:T(8,128)(2,1)}, u32[]{:S(2)}) copy-start(bf16[16,64,256]{2,1,0:T(8,128)(2,1)} %get-tuple-element.85.refs_0_) | copy-start | bytes 1572868
  140.0 18.2 %copy-start.10 = (bf16[16,64,256]{2,1,0:T(8,128)(2,1)S(1)}, bf16[16,64,256]{2,1,0:T(8,128)(2,1)}, u32[]{:S(2)}) copy-start(bf16[16,64,256]{2,1,0:T(8,128)(2,1)} %get-tuple-element.86.refs_4_) | copy-start | bytes 1572868
  140.0 18.2 %copy-start.13 = (bf16[16,64,256]{2,1,0:T(8,128)(2,1)S(1)}, bf16[16,64,256]{2,1,0:T(8,128)(2,1)}, u32[]{:S(2)}) copy-start(bf16[16,64,256]{2,1,0:T(8,128)(2,1)} %copy-done.11) | copy-start | bytes 1572868
  140.1 18.2 %copy-start.14 = (bf16[32,16,256]{2,1,0:T(8,128)(2,1)S(1)}, bf16[32,16,256]{2,1,0:T(8,128)(2,1)}, u32[]{:S(2)}) copy-start(bf16[32,16,256]{2,1,0:T(8,128)(2,1)} %get-tuple-element.87.refs_8_) | copy-start | bytes 786436
  140.1 18.2 %copy-start.20 = (bf16[256,1024]{1,0:T(8,128)(2,1)S(1)}, bf16[256,1024]{1,0:T(8,128)(2,1)}, u32[]{:S(2)}) copy-start(bf16[256,1024]{1,0:T(8,128)(2,1)} %refs_8_.2) | copy-start | bytes 1572868
  153.2 12.2 %collective-permute-start.12 = (bf16[32,16,256]{2,1,0:T(8,128)(2,1)}, bf16[32,16,256]{2,1,0:T(8,128)(2,1)}, u32[]{:S(2)}, u32[]{:S(2)}) collective-permute-start(bf16[32,16,256]{2,1,0:T(8,128)(2,1)} %get-tuple-element.78), channel_id=1, source_target_pairs={{0,1},{1,2},{2,3},{3,0},{4,5},{5,6},{6,7},{7,4},{8,9},{9,10},{10,1... | collective-permute-start | bytes 786440 | tf_op jit(solution)/shard_map/ppermute | solution.py:499
  154.5 14.3 %collective-permute-start.13 = (bf16[32,16,256]{2,1,0:T(8,128)(2,1)}, bf16[32,16,256]{2,1,0:T(8,128)(2,1)}, u32[]{:S(2)}, u32[]{:S(2)}) collective-permute-start(bf16[32,16,256]{2,1,0:T(8,128)(2,1)} %get-tuple-element.79), channel_id=1, source_target_pairs={{0,2},{1,3},{2,0},{3,1},{4,6},{5,7},{6,4},{7,5},{8,10},{9,11},{10,... | collective-permute-start | bytes 786440 | tf_op jit(solution)/shard_map/ppermute | solution.py:499
  156.9 11.9 %collective-permute-start.14 = (bf16[32,16,256]{2,1,0:T(8,128)(2,1)}, bf16[32,16,256]{2,1,0:T(8,128)(2,1)}, u32[]{:S(2)}, u32[]{:S(2)}) collective-permute-start(bf16[32,16,256]{2,1,0:T(8,128)(2,1)} %get-tuple-element.80), channel_id=1, source_target_pairs={{0,3},{1,0},{2,1},{3,2},{4,7},{5,4},{6,5},{7,6},{8,11},{9,8},{10,9... | collective-permute-start | bytes 786440 | tf_op jit(solution)/shard_map/ppermute | solution.py:499
  168.8 1.0 copy-start.15
  169.8 4.3 %copy-start.23 = (f32[32,8,256]{2,1,0:T(8,128)S(1)}, f32[32,8,256]{2,1,0:T(8,128)}, u32[]{:S(2)}) copy-start(f32[32,8,256]{2,1,0:T(8,128)} %stack.8.refs_5_.refs_9_) | copy-start | bytes 786436
  174.0 37.5 %all-to-all-start.4 = ((bf16[128,2,16,256]{3,2,1,0:T(8,128)(2,1)}), bf16[128,2,16,256]{3,2,1,0:T(8,128)(2,1)}, u32[]{:S(2)}, u32[]{:S(2)}) async-start(bf16[128,2,16,256]{3,2,1,0:T(8,128)(2,1)} %bitcast.20), calls=%async_computation.4 | async-start | bytes 4194304 | tf_op jit(solution)/shard_map/all_to_all | solution.py:620

commit v8 on v7

--- a/solution.py
+++ b/solution.py
@@ -269,7 +269,7 @@
     users = order.shape[0]
     events, kv_width = history.shape[1:]
     quarter = rows // mp
-    blocks = 4
+    blocks = 2
     block = size // blocks
     count = sum(len(arrays) for arrays in full)
 

time: 216 us -> 215 us (level)
  no operation moved by 1% of the time
where the time goes in v8:
time: 215 us; the launch traced here: 214 us
  waiting for transfers between devices  76.4 us (36%)
  starting transfers between devices  55.7 us (26%)
  Pallas kernels  47.8 us (22%)
  local copies, waits for them, and re-layouts  21.1 us (10%)
  other arithmetic  10.8 us (5%)
    all_to_all x4, waiting for transfers between devices, exchange(): return lax.all_to_all(rows, 'dp', split_axis=0, concat_axis=0, tiled=True)  43.1 us
    all_to_all x1, waiting for transfers between devices, per_device(): lax.all_to_all(done.reshape((-1,) + done.shape[2:]), ('dp', 'mp'), split_...  30.4 us
    ppermute x18, starting transfers between devices, shifted(): lax.ppermute(array, 'mp', [(i, (i + k) % mp_size) for i in range(mp_size)])  24.6 us
    all_to_all x4, starting transfers between devices, exchange(): return lax.all_to_all(rows, 'dp', split_axis=0, concat_axis=0, tiled=True)  23 us
    pallas_call x1, Pallas kernels, attend(): pl.pallas_call(body, out_shape=[pltpu.HBM((users, quarter, width), jnp.bf...  15.8 us
    unnamed x44, local copies, waits for them, and re-layouts  11.8 us
    pallas_call x1, Pallas kernels, attend_packed(): pl.pallas_call(body, out_shape=[pltpu.HBM((users, quarter, width), jnp.bf...  11.5 us
    all_to_all x1, starting transfers between devices, per_device(): lax.all_to_all(done.reshape((-1,) + done.shape[2:]), ('dp', 'mp'), split_...  8.17 us
  transfers between devices with their start and end apart: 23, of which 8 were waited for; matrix products, arithmetic and copies ran while one was open for 8% of the time, Pallas kernels for 19%

profile of v8, /device:TPU:1, one launch (start us, length us, event | category | flops | bytes accessed | tf_op | source)
XLA Modules:
  0.0 213.6 jit_solution(5113169083209799630)
XLA Ops:
  0.0 0.8 compare_select_fusion.13
  3.0 1.6 copy-done.1
  5.9 1.0 copy-done.4
  6.9 9.7 %all-to-all-start = ((bf16[32,80,256]{2,1,0:T(8,128)(2,1)}), bf16[32,80,256]{2,1,0:T(8,128)(2,1)S(1)}, u32[]{:S(2)}, u32[]{:S(2)}) async-start(bf16[32,80,256]{2,1,0:T(8,128)(2,1)} %copy-done.4), calls=%async_computation | async-start | bytes 2621440 | tf_op jit(solution)/shard_map/all_to_all | solution.py:494
  16.7 1.3 collective-permute-start.6
  18.0 2.5 %collective-permute-start.7 = (bf16[256,1024]{1,0:T(8,128)(2,1)}, bf16[256,1024]{1,0:T(8,128)(2,1)}, u32[]{:S(2)}, u32[]{:S(2)}) collective-permute-start(bf16[256,1024]{1,0:T(8,128)(2,1)} %refs_8_.2), channel_id=1, source_target_pairs={{0,2},{1,3},{2,0},{3,1},{4,6},{5,7},{6,4},{7,5},{8,10},{9,11},{10,... | collective-permute-start | bytes 1572872 | tf_op jit(solution)/shard_map/ppermute | solution.py:499
  20.4 1.2 collective-permute-start.8
  23.6 12.9 %all-to-all-done.refs_0_ = bf16[32,80,256]{2,1,0:T(8,128)(2,1)S(1)} async-done(((bf16[32,80,256]{2,1,0:T(8,128)(2,1)}), bf16[32,80,256]{2,1,0:T(8,128)(2,1)S(1)}, u32[]{:S(2)}, u32[]{:S(2)}) %all-to-all-start) | async-done | bytes 1310752 | tf_op jit(solution)/shard_map/all_to_all | solution.py:494
  37.9 1.1 copy-done.3
  39.0 4.0 %all-to-all-start.1 = ((bf16[32,80,256]{2,1,0:T(8,128)(2,1)}), bf16[32,80,256]{2,1,0:T(8,128)(2,1)S(1)}, u32[]{:S(2)}, u32[]{:S(2)}) async-start(bf16[32,80,256]{2,1,0:T(8,128)(2,1)} %copy-done.3), calls=%async_computation.1 | async-start | bytes 2621440 | tf_op jit(solution)/shard_map/all_to_all | solution.py:494
  43.0 1.6 copy-done.2
  45.2 1.0 copy-done.6
  46.3 2.0 gather_fusion.2
  49.9 1.3 broadcast_in_dim.394
  51.1 1.3 broadcast_in_dim.396
  52.4 1.8 stack.8.refs_5_.refs_9_
  54.2 3.2 %bitcast_select_fusion.refs_4_.refs_8_ = bf16[1024,1024]{1,0:T(8,128)(2,1)} fusion(bf16[4,256,1024]{2,1,0:T(8,128)(2,1)} %gather_fusion.2, pred[1024]{0:T(1024)(128)(4,1)S(1)} %broadcast_in_dim.400), kind=kLoop, calls=%fused_computation.3 | loop fusion | flops 1048576 | bytes 4195328 | tf_op jit(solution)/shard_map/jit(_take)/select_n | solution.py:561
  57.4 5.5 %all-to-all-done.1.src = bf16[32,80,256]{2,1,0:T(8,128)(2,1)S(1)} async-done(((bf16[32,80,256]{2,1,0:T(8,128)(2,1)}), bf16[32,80,256]{2,1,0:T(8,128)(2,1)S(1)}, u32[]{:S(2)}, u32[]{:S(2)}) %all-to-all-start.1) | async-done | bytes 1310752 | tf_op jit(solution)/shard_map/all_to_all | solution.py:494
  62.9 1.1 shard_map.94
  64.0 4.7 %all-to-all-start.2 = ((bf16[32,64,256]{2,1,0:T(8,128)(2,1)}), bf16[32,64,256]{2,1,0:T(8,128)(2,1)}, u32[]{:S(2)}, u32[]{:S(2)}) async-start(bf16[32,64,256]{2,1,0:T(8,128)(2,1)} %copy-done.6), calls=%async_computation.2 | async-start | bytes 2097152 | tf_op jit(solution)/shard_map/all_to_all | solution.py:494
  68.6 1.3 collective-permute-start.15
  69.9 1.5 collective-permute-start.17
  71.4 1.3 collective-permute-start.19
  73.5 12.2 %all-to-all-done.2.refs_0_ = bf16[32,64,256]{2,1,0:T(8,128)(2,1)} async-done(((bf16[32,64,256]{2,1,0:T(8,128)(2,1)}), bf16[32,64,256]{2,1,0:T(8,128)(2,1)}, u32[]{:S(2)}, u32[]{:S(2)}) %all-to-all-start.2) | async-done | bytes 1048608 | tf_op jit(solution)/shard_map/all_to_all | solution.py:494
  85.7 2.3 %shard_map.95 = bf16[32,64,256]{2,1,0:T(8,128)(2,1)} custom-call(s32[32]{0:T(128)S(1)} %select_reduce_fusion.5.index_ref, bf16[32,64,256]{2,1,0:T(8,128)(2,1)} %all-to-all-done.2.refs_0_), custom_call_target="tpu_custom_call" | custom-call | tf_op jit(solution)/shard_map/pallas_call | solution.py:68
  87.9 4.6 %all-to-all-start.3 = ((bf16[32,64,256]{2,1,0:T(8,128)(2,1)}), bf16[32,64,256]{2,1,0:T(8,128)(2,1)}, u32[]{:S(2)}, u32[]{:S(2)}) async-start(bf16[32,64,256]{2,1,0:T(8,128)(2,1)} %shard_map.95), calls=%async_computation.3 | async-start | bytes 2097152 | tf_op jit(solution)/shard_map/all_to_all | solution.py:494
  94.0 1.3 collective-permute-start.16
  95.3 1.6 collective-permute-start.20
  97.0 12.5 %all-to-all-done.3.rows_ref = bf16[32,64,256]{2,1,0:T(8,128)(2,1)} async-done(((bf16[32,64,256]{2,1,0:T(8,128)(2,1)}), bf16[32,64,256]{2,1,0:T(8,128)(2,1)}, u32[]{:S(2)}, u32[]{:S(2)}) %all-to-all-start.3) | async-done | bytes 1048608 | tf_op jit(solution)/shard_map/all_to_all | solution.py:494
  109.5 2.1 shard_map.96.refs_0_
  111.7 2.8 %collective-permute-start.10 = (bf16[1088,256]{1,0:T(8,128)(2,1)}, bf16[1088,256]{1,0:T(8,128)(2,1)S(1)}, u32[]{:S(2)}, u32[]{:S(2)}) collective-permute-start(bf16[1088,256]{1,0:T(8,128)(2,1)} %shard_map.96.refs_0_), channel_id=1, source_target_pairs={{0,2},{1,3},{2,0},{3,1},{4,6},{5,7},{6,4},{7,5},{8,10},{9,11},{10,... | collective-permute-start | bytes 1671176 | tf_op jit(solution)/shard_map/ppermute | solution.py:499
  114.5 0.9 collective-permute-start.11
  116.8 1.0 copy-done.7
  117.8 1.0 copy-done.9
  118.8 1.0 copy-done.12
  119.9 15.8 %shard_map.98 = (bf16[32,16,256]{2,1,0:T(8,128)(2,1)}, bf16[32,16,256]{2,1,0:T(8,128)(2,1)}, bf16[32,16,256]{2,1,0:T(8,128)(2,1)}, bf16[32,16,256]{2,1,0:T(8,128)(2,1)}) custom-call(s32[32]{0:T(128)S(1)} %select_reduce_fusion.4.order_ref, s32[1]{0:T(128)} %bitcast.9.rank_ref, bf16[16,64,256]{2,1,0:T(8,128)(2,1)S(1)} %copy-done.7, ...), custom_call_target="tpu_custom_call" | custom-call | tf_op jit(solution)/shard_map/pallas_call | solution.py:216
  136.6 3.0 %collective-permute-start.22 = (bf16[32,16,256]{2,1,0:T(8,128)(2,1)}, bf16[32,16,256]{2,1,0:T(8,128)(2,1)}, u32[]{:S(2)}, u32[]{:S(2)}) collective-permute-start(bf16[32,16,256]{2,1,0:T(8,128)(2,1)} %get-tuple-element.89), channel_id=1, source_target_pairs={{0,2},{1,3},{2,0},{3,1},{4,6},{5,7},{6,4},{7,5},{8,10},{9,11},{10,... | collective-permute-start | bytes 786440 | tf_op jit(solution)/shard_map/ppermute | solution.py:499
  140.1 11.5 %shard_map.97 = (bf16[32,16,256]{2,1,0:T(8,128)(2,1)}, bf16[32,16,256]{2,1,0:T(8,128)(2,1)}, bf16[32,16,256]{2,1,0:T(8,128)(2,1)}, bf16[32,16,256]{2,1,0:T(8,128)(2,1)}) custom-call(s32[32]{0:T(128)S(1)} %get-tuple-element.107.order_ref, s32[32]{0:T(128)S(1)} %broadcast_minimum_fusion.offsets_ref, s32[32]{0:T(128)S(1)} %get-tuple-element.109.slots_ref.seats_ref, ...), custom_call_target="tpu_custom_call" | custom-call | tf_op jit(solution)/shard_map/pallas_call | solution.py:332
  151.6 1.3 collective-permute-start.12
  152.8 2.5 %collective-permute-start.13 = (bf16[32,16,256]{2,1,0:T(8,128)(2,1)}, bf16[32,16,256]{2,1,0:T(8,128)(2,1)}, u32[]{:S(2)}, u32[]{:S(2)}) collective-permute-start(bf16[32,16,256]{2,1,0:T(8,128)(2,1)} %get-tuple-element.79), channel_id=1, source_target_pairs={{0,2},{1,3},{2,0},{3,1},{4,6},{5,7},{6,4},{7,5},{8,10},{9,11},{10,... | collective-permute-start | bytes 786440 | tf_op jit(solution)/shard_map/ppermute | solution.py:499
  155.3 1.1 collective-permute-start.14
  156.6 5.8 %shard_map.99.refs_12_ = bf16[32,4,2,16,256]{4,3,2,1,0:T(8,128)(2,1)} custom-call(s32[33]{0:T(128)S(1)} %pad_add_fusion.1.scalar_ref, bf16[16,64,256]{2,1,0:T(8,128)(2,1)S(1)} %copy-done.8, bf16[16,64,256]{2,1,0:T(8,128)(2,1)} %collective-permute-done.15.refs_1_, bf16[16,64,256]{2,1,0:T(8,128)(2,1)S(1)} %copy-done.13, ...), custom_call_target="tpu_custom_call" | custom-call | tf_op jit(solution)/shard_map/pallas_call | solution.py:394
  163.8 2.5 %collective-permute-done.13.refs_6_ = bf16[32,16,256]{2,1,0:T(8,128)(2,1)} collective-permute-done((bf16[32,16,256]{2,1,0:T(8,128)(2,1)}, bf16[32,16,256]{2,1,0:T(8,128)(2,1)}, u32[]{:S(2)}, u32[]{:S(2)}) %collective-permute-start.13) | collective-permute-done | bytes 262176 | tf_op jit(solution)/shard_map/ppermute | solution.py:499
  166.2 0.9 copy-done.15
  167.2 4.3 %shard_map.100 = bf16[32,4,2,16,256]{4,3,2,1,0:T(8,128)(2,1)} custom-call(s32[33]{0:T(128)S(1)} %pad_add_fusion.scalar_ref, s32[32]{0:T(128)S(1)} %get-tuple-element.109.slots_ref.seats_ref, s32[32]{0:T(128)S(1)} %broadcast_minimum_fusion.offsets_ref, bf16[1088,256]{1,0:T(8,128)(2,1)S(1)} %copy-done.5, ...), custom_call_target="tpu_custom_call", output_to_operand_aliasing={{}: (15, {})} | custom-call | tf_op jit(solution)/shard_map/pallas_call | solution.py:447
  171.5 8.2 %all-to-all-start.4 = ((bf16[128,2,16,256]{3,2,1,0:T(8,128)(2,1)}), bf16[128,2,16,256]{3,2,1,0:T(8,128)(2,1)}, u32[]{:S(2)}, u32[]{:S(2)}) async-start(bf16[128,2,16,256]{3,2,1,0:T(8,128)(2,1)} %bitcast.20), calls=%async_computation.4 | async-start | bytes 4194304 | tf_op jit(solution)/shard_map/all_to_all | solution.py:620
  179.8 30.4 %all-to-all-done.4 = bf16[128,2,16,256]{3,2,1,0:T(8,128)(2,1)} async-done(((bf16[128,2,16,256]{3,2,1,0:T(8,128)(2,1)}), bf16[128,2,16,256]{3,2,1,0:T(8,128)(2,1)}, u32[]{:S(2)}, u32[]{:S(2)}) %all-to-all-start.4) | async-done | bytes 2097184 | tf_op jit(solution)/shard_map/all_to_all | solution.py:620
  210.3 3.2 %shard_map.101 = bf16[32,128,256]{2,1,0:T(8,128)(2,1)} custom-call(s32[32]{0:T(128)S(1)} %broadcast_subtract_fusion.index_ref, bf16[32,4,2,16,256]{4,3,2,1,0:T(8,128)(2,1)} %bitcast.12.src), custom_call_target="tpu_custom_call" | custom-call | tf_op jit(solution)/shard_map/pallas_call | solution.py:37
  (99 shorter events, 14.8 us)
Async XLA Ops:
  0.0 46.3 %copy-start = (bf16[1024,1024]{1,0:T(8,128)(2,1)S(1)}, bf16[1024,1024]{1,0:T(8,128)(2,1)}, u32[]{:S(2)}) copy-start(bf16[1024,1024]{1,0:T(8,128)(2,1)} %param.17) | copy-start | bytes 6291460
  3.0 1.6 copy-start.1
  4.6 0.7 copy-start.17
  5.9 1.1 copy-start.4
  6.9 14.8 %copy-start.19 = (s32[32]{0:T(128)S(1)}, s32[32]{0:T(128)}, u32[]{:S(2)}) copy-start(s32[32]{0:T(128)} %param.16) | copy-start | bytes 388
  6.9 15.6 %copy-start.24 = (f32[2,16]{1,0:T(2,128)S(1)}, f32[2,16]{1,0:T(2,128)}, u32[]{:S(2)}) copy-start(f32[2,16]{1,0:T(2,128)} %param.18) | copy-start | bytes 388
  6.9 29.5 %all-to-all-start = ((bf16[32,80,256]{2,1,0:T(8,128)(2,1)}), bf16[32,80,256]{2,1,0:T(8,128)(2,1)S(1)}, u32[]{:S(2)}, u32[]{:S(2)}) async-start(bf16[32,80,256]{2,1,0:T(8,128)(2,1)} %copy-done.4), calls=%async_computation | async-start | bytes 2621440 | tf_op jit(solution)/shard_map/all_to_all | solution.py:494
  16.7 47.3 %collective-permute-start.6 = (bf16[256,1024]{1,0:T(8,128)(2,1)}, bf16[256,1024]{1,0:T(8,128)(2,1)}, u32[]{:S(2)}, u32[]{:S(2)}) collective-permute-start(bf16[256,1024]{1,0:T(8,128)(2,1)} %refs_8_.2), channel_id=1, source_target_pairs={{0,1},{1,2},{2,3},{3,0},{4,5},{5,6},{6,7},{7,4},{8,9},{9,10},{10,1... | collective-permute-start | bytes 1572872 | tf_op jit(solution)/shard_map/ppermute | solution.py:499
  18.0 46.0 %collective-permute-start.7 = (bf16[256,1024]{1,0:T(8,128)(2,1)}, bf16[256,1024]{1,0:T(8,128)(2,1)}, u32[]{:S(2)}, u32[]{:S(2)}) collective-permute-start(bf16[256,1024]{1,0:T(8,128)(2,1)} %refs_8_.2), channel_id=1, source_target_pairs={{0,2},{1,3},{2,0},{3,1},{4,6},{5,7},{6,4},{7,5},{8,10},{9,11},{10,... | collective-permute-start | bytes 1572872 | tf_op jit(solution)/shard_map/ppermute | solution.py:499
  20.4 43.6 %collective-permute-start.8 = (bf16[256,1024]{1,0:T(8,128)(2,1)}, bf16[256,1024]{1,0:T(8,128)(2,1)}, u32[]{:S(2)}, u32[]{:S(2)}) collective-permute-start(bf16[256,1024]{1,0:T(8,128)(2,1)} %refs_8_.2), channel_id=1, source_target_pairs={{0,3},{1,0},{2,1},{3,2},{4,7},{5,4},{6,5},{7,6},{8,11},{9,8},{10,9... | collective-permute-start | bytes 1572872 | tf_op jit(solution)/shard_map/ppermute | solution.py:499
  37.9 1.1 copy-start.3
  39.0 23.9 %all-to-all-start.1 = ((bf16[32,80,256]{2,1,0:T(8,128)(2,1)}), bf16[32,80,256]{2,1,0:T(8,128)(2,1)S(1)}, u32[]{:S(2)}, u32[]{:S(2)}) async-start(bf16[32,80,256]{2,1,0:T(8,128)(2,1)} %copy-done.3), calls=%async_computation.1 | async-start | bytes 2621440 | tf_op jit(solution)/shard_map/all_to_all | solution.py:494
  43.0 1.6 copy-start.2
  45.2 1.0 copy-start.6
  64.0 21.7 %all-to-all-start.2 = ((bf16[32,64,256]{2,1,0:T(8,128)(2,1)}), bf16[32,64,256]{2,1,0:T(8,128)(2,1)}, u32[]{:S(2)}, u32[]{:S(2)}) async-start(bf16[32,64,256]{2,1,0:T(8,128)(2,1)} %copy-done.6), calls=%async_computation.2 | async-start | bytes 2097152 | tf_op jit(solution)/shard_map/all_to_all | solution.py:494
  68.6 25.3 %collective-permute-start.15 = (bf16[16,64,256]{2,1,0:T(8,128)(2,1)}, bf16[16,64,256]{2,1,0:T(8,128)(2,1)}, u32[]{:S(2)}, u32[]{:S(2)}) collective-permute-start(bf16[16,64,256]{2,1,0:T(8,128)(2,1)} %get-tuple-element.85.refs_0_), channel_id=1, source_target_pairs={{0,1},{1,2},{2,3},{3,0},{4,5},{5,6},{6,7},{7,4},{8,9},{9,10},{10,1... | collective-permute-start | bytes 1572872 | tf_op jit(solution)/shard_map/ppermute | solution.py:499
  69.9 44.6 %collective-permute-start.17 = (bf16[16,64,256]{2,1,0:T(8,128)(2,1)}, bf16[16,64,256]{2,1,0:T(8,128)(2,1)}, u32[]{:S(2)}, u32[]{:S(2)}) collective-permute-start(bf16[16,64,256]{2,1,0:T(8,128)(2,1)} %get-tuple-element.85.refs_0_), channel_id=1, source_target_pairs={{0,3},{1,0},{2,1},{3,2},{4,7},{5,4},{6,5},{7,6},{8,11},{9,8},{10,9... | collective-permute-start | bytes 1572872 | tf_op jit(solution)/shard_map/ppermute | solution.py:499
  71.4 23.9 %collective-permute-start.19 = (bf16[16,64,256]{2,1,0:T(8,128)(2,1)}, bf16[16,64,256]{2,1,0:T(8,128)(2,1)}, u32[]{:S(2)}, u32[]{:S(2)}) collective-permute-start(bf16[16,64,256]{2,1,0:T(8,128)(2,1)} %get-tuple-element.86.refs_4_), channel_id=1, source_target_pairs={{0,3},{1,0},{2,1},{3,2},{4,7},{5,4},{6,5},{7,6},{8,11},{9,8},{10,9... | collective-permute-start | bytes 1572872 | tf_op jit(solution)/shard_map/ppermute | solution.py:499
  72.6 42.7 %collective-permute-start.18 = (bf16[16,64,256]{2,1,0:T(8,128)(2,1)}, bf16[16,64,256]{2,1,0:T(8,128)(2,1)}, u32[]{:S(2)}, u32[]{:S(2)}) collective-permute-start(bf16[16,64,256]{2,1,0:T(8,128)(2,1)} %get-tuple-element.86.refs_4_), channel_id=1, source_target_pairs={{0,1},{1,2},{2,3},{3,0},{4,5},{5,6},{6,7},{7,4},{8,9},{9,10},{10,1... | collective-permute-start | bytes 1572872 | tf_op jit(solution)/shard_map/ppermute | solution.py:499
  87.9 28.8 %copy-start.22 = (f32[32,8,256]{2,1,0:T(8,128)S(1)}, f32[32,8,256]{2,1,0:T(8,128)}, u32[]{:S(2)}) copy-start(f32[32,8,256]{2,1,0:T(8,128)} %stack.8.refs_5_.refs_9_) | copy-start | bytes 786436
  87.9 21.6 %all-to-all-start.3 = ((bf16[32,64,256]{2,1,0:T(8,128)(2,1)}), bf16[32,64,256]{2,1,0:T(8,128)(2,1)}, u32[]{:S(2)}, u32[]{:S(2)}) async-start(bf16[32,64,256]{2,1,0:T(8,128)(2,1)} %shard_map.95), calls=%async_computation.3 | async-start | bytes 2097152 | tf_op jit(solution)/shard_map/all_to_all | solution.py:494
  94.0 22.0 %collective-permute-start.16 = (bf16[16,64,256]{2,1,0:T(8,128)(2,1)}, bf16[16,64,256]{2,1,0:T(8,128)(2,1)S(1)}, u32[]{:S(2)}, u32[]{:S(2)}) collective-permute-start(bf16[16,64,256]{2,1,0:T(8,128)(2,1)} %collective-permute-done.15.refs_1_), channel_id=1, source_target_pairs={{0,1},{1,2},{2,3},{3,0},{4,5},{5,6},{6,7},{7,4},{8,9},{9,10},{10,1... | collective-permute-start | bytes 1572872 | tf_op jit(solution)/shard_map/ppermute | solution.py:499
  95.3 21.5 %collective-permute-start.20 = (bf16[16,64,256]{2,1,0:T(8,128)(2,1)}, bf16[16,64,256]{2,1,0:T(8,128)(2,1)}, u32[]{:S(2)}, u32[]{:S(2)}) collective-permute-start(bf16[16,64,256]{2,1,0:T(8,128)(2,1)} %collective-permute-done.19.refs_7_), channel_id=1, source_target_pairs={{0,3},{1,0},{2,1},{3,2},{4,7},{5,4},{6,5},{7,6},{8,11},{9,8},{10,9... | collective-permute-start | bytes 1572872 | tf_op jit(solution)/shard_map/ppermute | solution.py:499
  111.7 28.0 %collective-permute-start.10 = (bf16[1088,256]{1,0:T(8,128)(2,1)}, bf16[1088,256]{1,0:T(8,128)(2,1)S(1)}, u32[]{:S(2)}, u32[]{:S(2)}) collective-permute-start(bf16[1088,256]{1,0:T(8,128)(2,1)} %shard_map.96.refs_0_), channel_id=1, source_target_pairs={{0,2},{1,3},{2,0},{3,1},{4,6},{5,7},{6,4},{7,5},{8,10},{9,11},{10,... | collective-permute-start | bytes 1671176 | tf_op jit(solution)/shard_map/ppermute | solution.py:499
  114.5 25.2 %collective-permute-start.11 = (bf16[1088,256]{1,0:T(8,128)(2,1)}, bf16[1088,256]{1,0:T(8,128)(2,1)}, u32[]{:S(2)}, u32[]{:S(2)}) collective-permute-start(bf16[1088,256]{1,0:T(8,128)(2,1)} %shard_map.96.refs_0_), channel_id=1, source_target_pairs={{0,3},{1,0},{2,1},{3,2},{4,7},{5,4},{6,5},{7,6},{8,11},{9,8},{10,9... | collective-permute-start | bytes 1671176 | tf_op jit(solution)/shard_map/ppermute | solution.py:499
  115.3 24.7 %collective-permute-start.9 = (bf16[1088,256]{1,0:T(8,128)(2,1)}, bf16[1088,256]{1,0:T(8,128)(2,1)}, u32[]{:S(2)}, u32[]{:S(2)}) collective-permute-start(bf16[1088,256]{1,0:T(8,128)(2,1)} %shard_map.96.refs_0_), channel_id=1, source_target_pairs={{0,1},{1,2},{2,3},{3,0},{4,5},{5,6},{6,7},{7,4},{8,9},{9,10},{10,1... | collective-permute-start | bytes 1671176 | tf_op jit(solution)/shard_map/ppermute | solution.py:499
  116.0 0.8 copy-start.11
  116.8 1.0 copy-start.7
  117.8 1.0 copy-start.9
  118.8 1.0 copy-start.12
  119.9 20.2 %copy-start.5 = (bf16[1088,256]{1,0:T(8,128)(2,1)S(1)}, bf16[1088,256]{1,0:T(8,128)(2,1)}, u32[]{:S(2)}) copy-start(bf16[1088,256]{1,0:T(8,128)(2,1)} %shard_map.96.refs_0_) | copy-start | bytes 1671172
  135.7 19.6 %collective-permute-start.21 = (bf16[32,16,256]{2,1,0:T(8,128)(2,1)}, bf16[32,16,256]{2,1,0:T(8,128)(2,1)S(1)}, u32[]{:S(2)}, u32[]{:S(2)}) collective-permute-start(bf16[32,16,256]{2,1,0:T(8,128)(2,1)} %get-tuple-element.88), channel_id=1, source_target_pairs={{0,1},{1,2},{2,3},{3,0},{4,5},{5,6},{6,7},{7,4},{8,9},{9,10},{10,1... | collective-permute-start | bytes 786440 | tf_op jit(solution)/shard_map/ppermute | solution.py:499
  136.6 20.0 %collective-permute-start.22 = (bf16[32,16,256]{2,1,0:T(8,128)(2,1)}, bf16[32,16,256]{2,1,0:T(8,128)(2,1)}, u32[]{:S(2)}, u32[]{:S(2)}) collective-permute-start(bf16[32,16,256]{2,1,0:T(8,128)(2,1)} %get-tuple-element.89), channel_id=1, source_target_pairs={{0,2},{1,3},{2,0},{3,1},{4,6},{5,7},{6,4},{7,5},{8,10},{9,11},{10,... | collective-permute-start | bytes 786440 | tf_op jit(solution)/shard_map/ppermute | solution.py:499
  139.6 17.0 %collective-permute-start.23 = (bf16[32,16,256]{2,1,0:T(8,128)(2,1)}, bf16[32,16,256]{2,1,0:T(8,128)(2,1)}, u32[]{:S(2)}, u32[]{:S(2)}) collective-permute-start(bf16[32,16,256]{2,1,0:T(8,128)(2,1)} %get-tuple-element.90), channel_id=1, source_target_pairs={{0,3},{1,0},{2,1},{3,2},{4,7},{5,4},{6,5},{7,6},{8,11},{9,8},{10,9... | collective-permute-start | bytes 786440 | tf_op jit(solution)/shard_map/ppermute | solution.py:499
  140.0 16.6 %copy-start.8 = (bf16[16,64,256]{2,1,0:T(8,128)(2,1)S(1)}, bf16[16,64,256]{2,1,0:T(8,128)(2,1)}, u32[]{:S(2)}) copy-start(bf16[16,64,256]{2,1,0:T(8,128)(2,1)} %get-tuple-element.85.refs_0_) | copy-start | bytes 1572868
  140.0 16.6 %copy-start.10 = (bf16[16,64,256]{2,1,0:T(8,128)(2,1)S(1)}, bf16[16,64,256]{2,1,0:T(8,128)(2,1)}, u32[]{:S(2)}) copy-start(bf16[16,64,256]{2,1,0:T(8,128)(2,1)} %get-tuple-element.86.refs_4_) | copy-start | bytes 1572868
  140.0 16.6 %copy-start.13 = (bf16[16,64,256]{2,1,0:T(8,128)(2,1)S(1)}, bf16[16,64,256]{2,1,0:T(8,128)(2,1)}, u32[]{:S(2)}) copy-start(bf16[16,64,256]{2,1,0:T(8,128)(2,1)} %copy-done.11) | copy-start | bytes 1572868
  140.1 16.6 %copy-start.14 = (bf16[32,16,256]{2,1,0:T(8,128)(2,1)S(1)}, bf16[32,16,256]{2,1,0:T(8,128)(2,1)}, u32[]{:S(2)}) copy-start(bf16[32,16,256]{2,1,0:T(8,128)(2,1)} %get-tuple-element.87.refs_8_) | copy-start | bytes 786436
  140.1 16.6 %copy-start.20 = (bf16[256,1024]{1,0:T(8,128)(2,1)S(1)}, bf16[256,1024]{1,0:T(8,128)(2,1)}, u32[]{:S(2)}) copy-start(bf16[256,1024]{1,0:T(8,128)(2,1)} %refs_8_.2) | copy-start | bytes 1572868
  151.6 12.2 %collective-permute-start.12 = (bf16[32,16,256]{2,1,0:T(8,128)(2,1)}, bf16[32,16,256]{2,1,0:T(8,128)(2,1)}, u32[]{:S(2)}, u32[]{:S(2)}) collective-permute-start(bf16[32,16,256]{2,1,0:T(8,128)(2,1)} %get-tuple-element.78), channel_id=1, source_target_pairs={{0,1},{1,2},{2,3},{3,0},{4,5},{5,6},{6,7},{7,4},{8,9},{9,10},{10,1... | collective-permute-start | bytes 786440 | tf_op jit(solution)/shard_map/ppermute | solution.py:499
  152.8 13.4 %collective-permute-start.13 = (bf16[32,16,256]{2,1,0:T(8,128)(2,1)}, bf16[32,16,256]{2,1,0:T(8,128)(2,1)}, u32[]{:S(2)}, u32[]{:S(2)}) collective-permute-start(bf16[32,16,256]{2,1,0:T(8,128)(2,1)} %get-tuple-element.79), channel_id=1, source_target_pairs={{0,2},{1,3},{2,0},{3,1},{4,6},{5,7},{6,4},{7,5},{8,10},{9,11},{10,... | collective-permute-start | bytes 786440 | tf_op jit(solution)/shard_map/ppermute | solution.py:499
  155.3 10.9 %collective-permute-start.14 = (bf16[32,16,256]{2,1,0:T(8,128)(2,1)}, bf16[32,16,256]{2,1,0:T(8,128)(2,1)}, u32[]{:S(2)}, u32[]{:S(2)}) collective-permute-start(bf16[32,16,256]{2,1,0:T(8,128)(2,1)} %get-tuple-element.80), channel_id=1, source_target_pairs={{0,3},{1,0},{2,1},{3,2},{4,7},{5,4},{6,5},{7,6},{8,11},{9,8},{10,9... | collective-permute-start | bytes 786440 | tf_op jit(solution)/shard_map/ppermute | solution.py:499
  166.2 1.0 copy-start.15
  167.2 4.3 %copy-start.23 = (f32[32,8,256]{2,1,0:T(8,128)S(1)}, f32[32,8,256]{2,1,0:T(8,128)}, u32[]{:S(2)}) copy-start(f32[32,8,256]{2,1,0:T(8,128)} %stack.8.refs_5_.refs_9_) | copy-start | bytes 786436
  171.5 38.8 %all-to-all-start.4 = ((bf16[128,2,16,256]{3,2,1,0:T(8,128)(2,1)}), bf16[128,2,16,256]{3,2,1,0:T(8,128)(2,1)}, u32[]{:S(2)}, u32[]{:S(2)}) async-start(bf16[128,2,16,256]{3,2,1,0:T(8,128)(2,1)} %bitcast.20), calls=%async_computation.4 | async-start | bytes 4194304 | tf_op jit(solution)/shard_map/all_to_all | solution.py:620
